TPU v7x, 32 devices: a whole 2x2x4 slice. The times are simulated.
32 devices in a mesh: mp: 2 (over x), tok: 16 (over z, y, core).
Axes of the slice: x: 2, y: 2, z: 4, core: 2. Of those that a mesh axis runs over, the one named last changes fastest.
Arguments:
- inputs: bfloat16 [2, 16, 128, 2048], P('mp', 'tok'), may hold values from -6 to 6
- cotangent: bfloat16 [2, 16, 128, 4096], P('mp', 'tok'), may hold values from -6 to 6
- token_ids: int32 [2, 16, 128], P('mp', 'tok'), may hold values from 0 to 151935
- weights: float32 [2, 16, 256, 2048], P('mp', 'tok'), may hold values from -6 to 6
Outputs:
- merged: float32 [16, 256, 2048], P('tok')
All inputs are finite; a program needn't handle non-finite values.
Results may differ from a plain program's by a relative error of at most 0.0003.
Values may be sent and summed in bfloat16 or wider, within the bound.
No kernel may reach another device: no remote copies, remote signals or barrier semaphores. Data moves between devices by JAX's collectives and lax.ppermute only.
A program may use at most 64 MiB of HBM per device.

v0:
```python
import math

import jax
import jax.numpy as jnp
from jax import lax
from jax.sharding import PartitionSpec as P

ROW_BLOCKS = 8
FIRST_TEXT = 37984


damping = 0.1


def squares(operands):
    row_parts, col_parts = operands
    src_count = row_parts.shape[0]
    item_count = row_parts.shape[1]
    seq_length = row_parts.shape[2]
    row_width = row_parts.shape[3]
    col_width = col_parts.shape[3]
    row_parts = row_parts.reshape(src_count // 8, 8, item_count, seq_length, row_width)
    col_parts = col_parts.reshape(src_count // 8, 8, item_count, seq_length, col_width)
    factor = 1.0 / math.sqrt(seq_length)

    def accumulate(summed, couple):
        gradient = (
            jnp.einsum("gitr,gitc->girc", couple[0], couple[1], preferred_element_type=jnp.float32)
            * factor
        )
        return (summed + jnp.sum(gradient * gradient, axis=0), None)

    start = jnp.zeros((item_count, row_width, col_width), jnp.float32)
    summed, unused = lax.scan(accumulate, start, (row_parts, col_parts))
    return summed


def shards(inputs, cotangent, token_ids, weights):
    device_count = lax.axis_size("tok")
    col_count = device_count // ROW_BLOCKS
    seq_count = inputs.shape[1]
    seq_length = inputs.shape[2]
    feature_width = inputs.shape[3]
    query_width = cotangent.shape[3]
    row_width = feature_width // ROW_BLOCKS
    col_width = query_width // col_count
    kept_mask = (token_ids[0] >= FIRST_TEXT).astype(jnp.bfloat16)
    masked = cotangent[0] * kept_mask[:, :, None]
    row_send = inputs[0].reshape(seq_count, seq_length, ROW_BLOCKS, row_width).transpose(2, 0, 1, 3)
    row_send = jnp.repeat(row_send, col_count, axis=0)
    col_send = masked.reshape(seq_count, seq_length, col_count, col_width).transpose(2, 0, 1, 3)
    col_send = jnp.tile(col_send, (ROW_BLOCKS, 1, 1, 1))
    per_item = squares(
        (
            lax.all_to_all(row_send, "tok", split_axis=0, concat_axis=0, tiled=True),
            lax.all_to_all(col_send, "tok", split_axis=0, concat_axis=0, tiled=True),
        )
    )
    fisher = jnp.sum(per_item, axis=0) / (seq_count * device_count)
    damped = fisher + damping
    product = damped * weights[0, 0]
    shares = (
        lax.psum_scatter(damped, "mp", scatter_dimension=0, tiled=True),
        lax.psum_scatter(product, "mp", scatter_dimension=0, tiled=True),
    )
    quotient = shares[1] / shares[0]
    merged = lax.all_gather(quotient, "mp", axis=0, tiled=True)
    return merged[None]


def solution(mesh):
    in_specs = (
        P("mp", "tok", None, None),
        P("mp", "tok", None, None),
        P("mp", "tok", None),
        P("mp", "tok", None, None),
    )
    out_specs = P("tok", None, None)
    return jax.shard_map(shards, mesh=mesh, in_specs=in_specs, out_specs=out_specs, check_vma=False)
```

profile of v0, /device:TPU:0, one launch (start us, length us, event | category | flops | bytes accessed | tf_op | source)
XLA Modules:
  0.0 365.8 jit_solution(13705251247035545884)
XLA Ops:
  6.5 1.1 copy.11
  7.7 0.4 copy.7
  8.2 0.0 copy-start
  8.2 1.2 broadcast_in_dim.13
  9.4 0.0 copy-start.1
  9.4 7.5 %all-to-all-start = ((bf16[16,1,128,256]{2,3,1,0:T(8,128)(2,1)}), bf16[16,1,128,256]{2,3,1,0:T(8,128)(2,1)S(1)}, u32[]{:S(2)}, u32[]{:S(2)}) async-start(bf16[16,1,128,256]{2,3,1,0:T(8,128)(2,1)} %bitcast.2), calls=%async_computation | async-start | bytes 2097152 | tf_op jit(solution)/shard_map/all_to_all | solution.py:55
  16.9 0.0 copy-done
  16.9 0.8 squeeze.11
  17.7 0.0 copy-done.1
  17.7 1.0 multiply_bitcast_fusion
  18.7 0.4 copy.8
  19.0 20.8 %all-to-all-done = bf16[16,1,128,256]{2,3,1,0:T(8,128)(2,1)S(1)} async-done(((bf16[16,1,128,256]{2,3,1,0:T(8,128)(2,1)}), bf16[16,1,128,256]{2,3,1,0:T(8,128)(2,1)S(1)}, u32[]{:S(2)}, u32[]{:S(2)}) %all-to-all-start) | async-done | bytes 1048608 | tf_op jit(solution)/shard_map/all_to_all | solution.py:55
  39.8 4.3 %tile.12 = bf16[8,2,128,2048]{3,2,1,0:T(8,128)(2,1)} broadcast(bf16[2,128,2048]{2,1,0:T(8,128)(2,1)S(1)} %copy.8), dimensions={1,2,3} | broadcast | bytes 9437184 | tf_op jit(solution)/shard_map/tile | solution.py:52
  44.1 6.9 %all-to-all-start.1 = ((bf16[16,1,128,2048]{3,2,1,0:T(8,128)(2,1)}), bf16[16,1,128,2048]{3,2,1,0:T(8,128)(2,1)}, u32[]{:S(2)}, u32[]{:S(2)}) async-start(bf16[16,1,128,2048]{3,2,1,0:T(8,128)(2,1)} %bitcast.48), calls=%async_computation.1 | async-start | bytes 16777216 | tf_op jit(solution)/shard_map/all_to_all | solution.py:56
  51.0 0.0 reduce-scatter.3.cloned.1.call-start
  51.1 150.6 %all-to-all-done.1 = bf16[16,1,128,2048]{3,2,1,0:T(8,128)(2,1)} async-done(((bf16[16,1,128,2048]{3,2,1,0:T(8,128)(2,1)}), bf16[16,1,128,2048]{3,2,1,0:T(8,128)(2,1)}, u32[]{:S(2)}, u32[]{:S(2)}) %all-to-all-start.1) | async-done | bytes 8388640 | tf_op jit(solution)/shard_map/all_to_all | solution.py:56
  201.7 17.0 %while.11 = (s32[]{:T(128)}, f32[1,256,2048]{2,1,0:T(8,128)S(1)}, bf16[2,8,1,128,256]{3,4,1,2,0:T(8,128)(2,1)S(1)}, bf16[2,8,1,128,2048]{4,3,1,2,0:T(8,128)(2,1)}, s32[]{:T(128)}, /*index=5*/s32[]{:T(128)}) while((s32[]{:T(128)}, f32[1,256,2048]{2,1,0:T(8,128)S(1)}, bf16[2,8,1,128,256]{3,4,1,2,0:T(8,128)(2,1)S(1)}, ...), condition=%wide.region_2.3_spmd.clone, body=%wide.region_0.2_spmd.clone.sunk | while | flops 1086849024 | bytes 13108303 | solution.py:34
  201.7 6.2 %multiply_reduce_fusion.2 = f32[256,2048]{1,0:T(8,128)} fusion(bf16[2,8,1,128,2048]{4,3,1,2,0:T(8,128)(2,1)} %get-tuple-element.95, s32[]{:T(128)} %get-tuple-element.86, bf16[2,8,1,128,256]{3,4,1,2,0:T(8,128)(2,1)S(1)} %get-tuple-element.94), kind=kOutput, calls=%fused_computation.clone.1 | convolution fusion | flops 1085800448 | bytes 6816768 | tf_op jit(solution)/shard_map/while/body/eval_jaxpr/gitr,gitc->girc/dot_general | solution.py:28
  208.0 2.3 bitcast_add_fusion.2
  210.3 6.2 %multiply_reduce_fusion.2 = f32[256,2048]{1,0:T(8,128)} fusion(bf16[2,8,1,128,2048]{4,3,1,2,0:T(8,128)(2,1)} %get-tuple-element.95, s32[]{:T(128)} %get-tuple-element.86, bf16[2,8,1,128,256]{3,4,1,2,0:T(8,128)(2,1)S(1)} %get-tuple-element.94), kind=kOutput, calls=%fused_computation.clone.1 | convolution fusion | flops 1085800448 | bytes 6816768 | tf_op jit(solution)/shard_map/while/body/eval_jaxpr/gitr,gitc->girc/dot_general | solution.py:28
  216.5 2.3 bitcast_add_fusion.2
  218.8 3.4 bitcast_multiply_fusion
  222.2 0.0 reduce-scatter.3.cloned.1.call-update
  222.2 0.0 reduce-scatter.5.cloned.1.call-start
  222.3 1.7 add_bitcast_fusion
  224.0 0.0 reduce-scatter.5.cloned.1.call-update
  224.0 0.0 all-gather.2.cloned.1.call-start
  224.1 61.9 %reduce-scatter.3.cloned.1.call-done = f32[128,2048]{1,0:T(8,128)} async-done(((f32[256,2048]{1,0:T(8,128)}), f32[128,2048]{1,0:T(8,128)}) %reduce-scatter.3.cloned.1.call-update) | async-done | bytes 1048592 | tf_op jit(solution)/shard_map/reduce_scatter | solution.py:64
  286.0 34.2 %reduce-scatter.5.cloned.1.call-done = f32[128,2048]{1,0:T(8,128)} async-done(((f32[256,2048]{1,0:T(8,128)}), f32[128,2048]{1,0:T(8,128)}) %reduce-scatter.5.cloned.1.call-update) | async-done | bytes 1048592 | tf_op jit(solution)/shard_map/reduce_scatter | solution.py:63
  320.2 2.7 div.11
  322.8 0.0 all-gather.2.cloned.1.call-update
  322.9 33.3 %all-gather.2.cloned.1.call-done = f32[256,2048]{1,0:T(8,128)} async-done(((f32[128,2048]{1,0:T(8,128)}), f32[256,2048]{1,0:T(8,128)}) %all-gather.2.cloned.1.call-update) | async-done | bytes 2097168 | tf_op jit(solution)/shard_map/all_gather | solution.py:67
  356.1 3.1 copy.19
  (3 shorter events, 0.0 us)
Async XLA Ops:
  8.2 8.7 %copy-start = (bf16[1,1,128,4096]{3,2,1,0:T(8,128)(2,1)S(1)}, bf16[1,1,128,4096]{3,2,1,0:T(8,128)(2,1)}, u32[]{:S(2)}) copy-start(bf16[1,1,128,4096]{3,2,1,0:T(8,128)(2,1)} %param.7) | copy-start | bytes 3145732
  9.4 8.3 %copy-start.1 = (s32[1,1,128]{2,1,0:T(1,128)S(1)}, s32[1,1,128]{2,1,0:T(1,128)}, u32[]{:S(2)}) copy-start(s32[1,1,128]{2,1,0:T(1,128)} %param.8) | copy-start | bytes 1540
  9.4 30.5 %all-to-all-start = ((bf16[16,1,128,256]{2,3,1,0:T(8,128)(2,1)}), bf16[16,1,128,256]{2,3,1,0:T(8,128)(2,1)S(1)}, u32[]{:S(2)}, u32[]{:S(2)}) async-start(bf16[16,1,128,256]{2,3,1,0:T(8,128)(2,1)} %bitcast.2), calls=%async_computation | async-start | bytes 2097152 | tf_op jit(solution)/shard_map/all_to_all | solution.py:55
  44.1 157.6 %all-to-all-start.1 = ((bf16[16,1,128,2048]{3,2,1,0:T(8,128)(2,1)}), bf16[16,1,128,2048]{3,2,1,0:T(8,128)(2,1)}, u32[]{:S(2)}, u32[]{:S(2)}) async-start(bf16[16,1,128,2048]{3,2,1,0:T(8,128)(2,1)} %bitcast.48), calls=%async_computation.1 | async-start | bytes 16777216 | tf_op jit(solution)/shard_map/all_to_all | solution.py:56
  51.0 235.0 %reduce-scatter.3.cloned.1.call-start = ((), (), s32[]{:S(2)}) async-start(), calls=%async_computation.4 | async-start | bytes 3145728 | tf_op jit(solution)/shard_map/reduce_scatter | solution.py:64
  222.2 98.0 %reduce-scatter.5.cloned.1.call-start = ((), (), s32[]{:S(2)}) async-start(), calls=%async_computation.5 | async-start | bytes 3145728 | tf_op jit(solution)/shard_map/reduce_scatter | solution.py:63
  224.0 132.1 %all-gather.2.cloned.1.call-start = ((), (), s32[]{:S(2)}) async-start(), calls=%async_computation.6 | async-start | bytes 3145728 | tf_op jit(solution)/shard_map/all_gather | solution.py:67
Sparse Core Ops, SparseCore 0:
  222.3 63.6 reduce-scatter.2
  288.3 31.8 reduce-scatter.4
  323.0 33.1 all-gather.1
where the time goes:
time: 366 us
  waiting for transfers between devices  301 us (82%)
  starting transfers between devices  14.6 us (4%)
  other arithmetic  13.4 us (4%)
  between operations  13.2 us (4%)
  matrix products  12.4 us (3%)
  local copies, waits for them, and re-layouts  11.4 us (3%)
    all_to_all x1, waiting for transfers between devices, shards(): lax.all_to_all(col_send, 'tok', split_axis=0, concat_axis=0, tiled=True)  151 us
    reduce_scatter x1, waiting for transfers between devices, shards(): lax.psum_scatter(product, 'mp', scatter_dimension=0, tiled=True)  61.9 us
    reduce_scatter x1, waiting for transfers between devices, shards(): lax.psum_scatter(damped, 'mp', scatter_dimension=0, tiled=True)  34.2 us
    all_gather x1, waiting for transfers between devices, shards(): merged = lax.all_gather(quotient, 'mp', axis=0, tiled=True)  33.3 us
    all_to_all x1, waiting for transfers between devices, shards(): lax.all_to_all(row_send, 'tok', split_axis=0, concat_axis=0, tiled=True)  20.8 us
    dot_general x2, matrix products, accumulate(): jnp.einsum('gitr,gitc->girc', couple[0], couple[1], preferred_element_typ...  12.4 us
    all_to_all x1, starting transfers between devices, shards(): lax.all_to_all(row_send, 'tok', split_axis=0, concat_axis=0, tiled=True)  7.52 us
  transfers between devices with their start and end apart: 5, of which 5 were waited for; matrix products, arithmetic and copies ran while one was open for 1% of the time, Pallas kernels for 0%

commit v1 on v0

v1 whole, which is shorter than its diff:
```python
import functools
import math

import jax
import jax.numpy as jnp
from jax import lax
from jax.experimental import pallas as pl
from jax.experimental.pallas import tpu as pltpu
from jax.sharding import Mesh
from jax.sharding import PartitionSpec as P

ROW_BLOCKS = 8
FIRST_TEXT = 37984
LARGEST = 6.0

damping = 0.1

TOK = ("zh", "zl", "y", "c")
VMEM = pl.BlockSpec(memory_space=pltpu.VMEM)
VMEM_LIMIT = 48 * 1024 * 1024
CHUNKS = (0.5, 0.5)


def swap(value, axes):
    if isinstance(axes, str):
        return lax.ppermute(value, axes, [(0, 1), (1, 0)])
    return lax.ppermute(value, axes, [(i, i ^ 3) for i in range(4)])


def rotate(value, axis, offset):
    size = lax.axis_size(axis)
    return lax.ppermute(value, axis, [(i, (i + offset) % size) for i in range(size)])


def call(body, out_shape, scratch_shapes=(), flops=0, bytes_accessed=0):
    def run(*args):
        return pl.pallas_call(
            body,
            out_shape=out_shape,
            in_specs=[VMEM] * len(args),
            out_specs=jax.tree.map(lambda _: VMEM, out_shape),
            scratch_shapes=list(scratch_shapes),
            compiler_params=pltpu.CompilerParams(vmem_limit_bytes=VMEM_LIMIT),
            cost_estimate=pl.CostEstimate(flops=flops, bytes_accessed=bytes_accessed, transcendentals=0),
        )(*args)

    return run


def row_kernel(inputs_ref, keep_ref, send_ref):
    half = keep_ref.shape[1]
    own = lax.axis_index("zh")
    for ref, part in ((keep_ref, own), (send_ref, 1 - own)):
        for s in range(inputs_ref.shape[0]):
            start = pl.multiple_of(part * half, half)
            ref[s] = inputs_ref[s, :, pl.ds(start, half)].T


def col_kernel(ids_ref, cot_ref, *outs):
    seqs, length, width = ids_ref.shape[0], cot_ref.shape[1], outs[0].shape[3]
    core_count = len(outs) // 2
    own_y, own_c = lax.axis_index("y"), lax.axis_index("c")
    for s in range(seqs):
        kept = jnp.broadcast_to((ids_ref[s : s + 1, :] >= FIRST_TEXT).astype(jnp.float32), (128, length)).T
        kept = kept[:, :1] > 0.5
        for at, ref in enumerate(outs):
            to_y = own_y ^ (at // core_count)
            to_c = lax.rem(own_c + at % core_count, core_count)
            for zl in range(2):
                start = pl.multiple_of(((to_c * 2 + zl) * 2 + to_y) * width, width)
                piece = cot_ref[s, :, pl.ds(start, width)]
                ref[zl, s] = jnp.where(kept, piece, jnp.zeros_like(piece))


def pack_kernel(widths, *refs):
    count = len(refs) - 2 * len(widths)
    ins, outs = refs[:count], refs[count:]
    own = lax.axis_index("zl")
    start = 0
    for at, width in enumerate(widths):
        for which in range(2):
            ref = outs[2 * at + which]
            for i, source in enumerate(ins):
                seqs = source.shape[1]
                ref[i * seqs : (i + 1) * seqs] = source[own ^ which, :, :, start : start + width]
        start += width


def fisher_kernel(row_count, scale, code_scale, *refs):
    rows, cols, outs, total = refs[:row_count], refs[row_count:-5], refs[-5:-1], refs[-1]
    span = outs[0].shape[0]
    own_zl, own_y = lax.axis_index("zl"), lax.axis_index("y")
    per = row_count // len(cols)

    seqs = rows[0].shape[0]
    for group in range(4):
        part = slice(group * span, (group + 1) * span)
        acc = None
        for r in range(row_count):
            for s in range(seqs):
                g = jnp.dot(
                    rows[r][s, part, :], cols[r // per][(r % per) * seqs + s], preferred_element_type=jnp.float32
                )
                acc = g * g if acc is None else acc + g * g
        damped = acc * scale + damping
        code = jnp.round((jnp.log(damped) - math.log(damping)) * code_scale) - 32768.0
        total[part, :] = jnp.clip(code, -32768.0, 32767.0)
    for at, ref in enumerate(outs):
        group = (own_zl ^ (at // 2)) * 2 + (own_y ^ (at % 2))
        start = pl.multiple_of(group * span, span)
        ref[...] = total[pl.ds(start, span), :].astype(jnp.int32).astype(jnp.int16)


def merge_kernel(models, widths, code_scale, *refs):
    weights, codes, out = refs[:models], refs[models:-1], refs[-1]
    chunk_count = len(widths)
    own_zl, own_y, own_m = lax.axis_index("zl"), lax.axis_index("y"), lax.axis_index("mp")

    def pick(values, j):
        chosen = values[0]
        for offset in range(1, models):
            chosen = jnp.where(lax.rem(own_m + models - offset, models) == j, values[offset], chosen)
        return chosen

    for at in range(4):
        sub = (own_zl ^ (at // 2)) * 2 + (own_y ^ (at % 2))
        first = 0
        for k, width in enumerate(widths):
            start = pl.multiple_of(sub * sum(widths) + first, 128)
            first += width
            damped, weight = [], []
            for m in range(models):
                code = codes[(m * 4 + at) * chunk_count + k][...].astype(jnp.int32).astype(jnp.float32)
                damped.append(jnp.exp((code + 32768.0) * (1.0 / code_scale) + math.log(damping)))
                weight.append(weights[m][:, pl.ds(start, width)])
            num, den = None, None
            for j in range(models):
                d = pick(damped, j)
                p = d * pick(weight, j)
                num = p if num is None else num + p
                den = d if den is None else den + d
            out[:, pl.ds(start, width)] = num / den


def shards(inputs, cotangent, token_ids, weights):
    models = lax.axis_size("mp")
    core_count = lax.axis_size("c")
    inputs, cotangent, token_ids, weights = inputs[0], cotangent[0], token_ids[0], weights[0, 0]
    seqs, length, feature_width = inputs.shape
    query_width = cotangent.shape[2]
    bf = jnp.bfloat16
    half = feature_width // 2
    tile_width = query_width // (4 * core_count)
    span = half // 4
    total_seqs = seqs * 8 * core_count
    widths = [int(tile_width * part) for part in CHUNKS]
    if any(width % 128 for width in widths):
        widths = [tile_width]
    peak = LARGEST**4 * length + damping
    code_scale = 65535.0 / (math.log(peak) - math.log(damping))

    other_weights = [rotate(weights, "mp", offset) for offset in range(1, models)]

    row_shape = jax.ShapeDtypeStruct((seqs, half, length), bf)
    keep, send = pl.pallas_call(
        row_kernel,
        out_shape=(row_shape, row_shape),
        in_specs=[VMEM],
        out_specs=(VMEM, VMEM),
        compiler_params=pltpu.CompilerParams(vmem_limit_bytes=VMEM_LIMIT),
    )(inputs)
    col_shape = jax.ShapeDtypeStruct((2, seqs, length, tile_width), bf)
    col_parts = call(col_kernel, (col_shape,) * (2 * core_count))(token_ids, cotangent)

    z2 = swap(send, "zh")
    z1 = swap(keep, "zl")
    z3 = swap(z2, "zl")
    by_z = [keep, z1, z2, z3]
    by_zy = [[r, swap(r, "y")] for r in by_z]
    rows = [[[r] + [rotate(r, "c", o) for o in range(1, core_count)] for r in pair] for pair in by_zy]
    rows = [r for a in rows for b in a for r in b]

    got = []
    for at, part in enumerate(col_parts):
        dy, dc = at // core_count, at % core_count
        if dy and dc:
            size = 2 * core_count
            perm = []
            for i in range(size):
                y, c = i // core_count, i % core_count
                perm.append((i, (y ^ 1) * core_count + (c + dc) % core_count))
            part = lax.ppermute(part, ("y", "c"), perm)
        elif dy:
            part = swap(part, "y")
        elif dc:
            part = rotate(part, "c", dc)
        got.append(part)
    pack_shapes = []
    for width in widths:
        pack_shapes += [jax.ShapeDtypeStruct((seqs * 2 * core_count, length, width), bf)] * 2
    packed = call(functools.partial(pack_kernel, widths), tuple(pack_shapes))(*got)

    codes = []
    for k, width in enumerate(widths):
        own, other = packed[2 * k], packed[2 * k + 1]
        cols = [own, swap(other, "zl"), swap(own, "zh"), swap(other, ("zh", "zl"))]
        code_shape = jax.ShapeDtypeStruct((span, width), jnp.int16)
        outs = call(
            functools.partial(fisher_kernel, len(rows), 1.0 / (length * total_seqs), code_scale),
            (code_shape,) * 4,
            [pltpu.VMEM((half, width), jnp.float32)],
            flops=2 * half * width * length * total_seqs,
            bytes_accessed=2 * length * total_seqs * (half + width),
        )(*rows, *cols)
        codes.append([outs[0], swap(outs[1], "y"), swap(outs[2], "zl"), swap(outs[3], ("zl", "y"))])

    own_codes = [codes[k][at] for at in range(4) for k in range(len(widths))]
    all_codes = list(own_codes)
    for offset in range(1, models):
        all_codes += [rotate(code, "mp", offset) for code in own_codes]
    merged = call(
        functools.partial(merge_kernel, models, widths, code_scale),
        jax.ShapeDtypeStruct(weights.shape, jnp.float32),
    )(weights, *other_weights, *all_codes)
    return merged[None]


def solution(mesh):
    models, devices = mesh.shape["mp"], mesh.shape["tok"]
    grid = Mesh(mesh.devices.reshape(models, 2, 2, ROW_BLOCKS // 4, devices // ROW_BLOCKS), ("mp",) + TOK)
    in_specs = (
        P("mp", TOK, None, None),
        P("mp", TOK, None, None),
        P("mp", TOK, None),
        P("mp", TOK, None, None),
    )
    return jax.shard_map(shards, mesh=grid, in_specs=in_specs, out_specs=P(TOK, None, None), check_vma=False)
```

time: 366 us -> 126 us (0.34)
  waiting for transfers between devices: 301 us -> 69.2 us
  starting transfers between devices: 14.6 us -> 42.5 us
  other arithmetic: 13.4 us -> 0 us
  between operations: 13.2 us -> 0.1 us
  matrix products: 12.4 us -> 0 us
  Pallas kernels: 0 us -> 10.2 us
  local copies, waits for them, and re-layouts: 11.4 us -> 4.26 us
    all_to_all x2 -> x0, waiting for transfers between devices: 171 us -> none  [the longest x1 151 us: shards(): lax.all_to_all(col_send, 'tok', split_axis=0, concat_axis=0, tiled=True)]
    reduce_scatter x2 -> x0, waiting for transfers between devices: 96.1 us -> none  [the longest x1 61.9 us: shards(): lax.psum_scatter(product, 'mp', scatter_dimension=0, tiled=True)]
    ppermute x0 -> x39, waiting for transfers between devices: none -> 69.2 us  [the longest x16 51.3 us: swap(): return lax.ppermute(value, axes, [(0, 1), (1, 0)])]
    ppermute x0 -> x39, starting transfers between devices: none -> 42.5 us  [the longest x16 17.3 us: swap(): return lax.ppermute(value, axes, [(0, 1), (1, 0)])]
    all_gather x1 -> x0, waiting for transfers between devices: 33.3 us -> none  [shards(): merged = lax.all_gather(quotient, 'mp', axis=0, tiled=True)]
    all_to_all x2 -> x0, starting transfers between devices: 14.4 us -> none  [the longest x1 7.52 us: shards(): lax.all_to_all(row_send, 'tok', split_axis=0, concat_axis=0, tiled=True)]
    dot_general x2 -> x0, matrix products: 12.4 us -> none  [accumulate(): jnp.einsum('gitr,gitc->girc', couple[0], couple[1], preferred_element_typ...]
    pallas_call x0 -> x6, Pallas kernels: none -> 10.2 us  [the longest x5 10 us: run(): pl.pallas_call(body, out_shape=out_shape, in_specs=[VMEM] * len(args), ou...]
  transfers between devices with their start and end apart: 5 -> 39, of which waited for: 5 -> 17; matrix products, arithmetic and copies ran while one was open for 1% -> 0% of each run, Pallas kernels for 0% -> 4%
where the time goes in v1:
time: 126 us
  waiting for transfers between devices  69.2 us (55%)
  starting transfers between devices  42.5 us (34%)
  Pallas kernels  10.2 us (8%)
  local copies, waits for them, and re-layouts  4.26 us (3%)
    ppermute x16, waiting for transfers between devices, swap(): return lax.ppermute(value, axes, [(0, 1), (1, 0)])  51.3 us
    ppermute x16, starting transfers between devices, swap(): return lax.ppermute(value, axes, [(0, 1), (1, 0)])  17.3 us
    ppermute x4, starting transfers between devices, swap(): return lax.ppermute(value, axes, [(i, i ^ 3) for i in range(4)])  15.3 us
    ppermute x18, waiting for transfers between devices, rotate(): lax.ppermute(value, axis, [(i, (i + offset) % size) for i in range(size)])  13.1 us
    pallas_call x5, Pallas kernels, run(): pl.pallas_call(body, out_shape=out_shape, in_specs=[VMEM] * len(args), ou...  10 us
    ppermute x18, starting transfers between devices, rotate(): lax.ppermute(value, axis, [(i, (i + offset) % size) for i in range(size)])  9.76 us
    ppermute x1, waiting for transfers between devices, shards(): part = lax.ppermute(part, ('y', 'c'), perm)  4.7 us
    unnamed x10, local copies, waits for them, and re-layouts  4.26 us
  transfers between devices with their start and end apart: 39, of which 17 were waited for; matrix products, arithmetic and copies ran while one was open for 0% of the time, Pallas kernels for 4%

profile of v1, /device:TPU:0, one launch (start us, length us, event | category | flops | bytes accessed | tf_op | source)
XLA Modules:
  0.0 126.2 jit_solution(3279482628809427835)
XLA Ops:
  0.0 1.0 copy-done.2
  1.2 4.1 %collective-permute-start.8 = (bf16[1,1024,128]{2,1,0:T(8,128)(2,1)S(1)}, bf16[1,1024,128]{2,1,0:T(8,128)(2,1)S(1)}, u32[]{:S(2)}, u32[]{:S(2)}) collective-permute-start(bf16[1,1024,128]{2,1,0:T(8,128)(2,1)S(1)} %get-tuple-element.24), channel_id=1, source_target_pairs={{0,8},{8,0},{1,9},{9,1},{2,10},{10,2},{3,11},{11,3},{4,12},{12,4},... | collective-permute-start | bytes 786440 | tf_op jit(solution)/shard_map/ppermute | solution.py:26
  5.3 1.6 %collective-permute-start.4 = (bf16[1,1024,128]{2,1,0:T(8,128)(2,1)S(1)}, bf16[1,1024,128]{2,1,0:T(8,128)(2,1)S(1)}, u32[]{:S(2)}, u32[]{:S(2)}) collective-permute-start(bf16[1,1024,128]{2,1,0:T(8,128)(2,1)S(1)} %get-tuple-element.23.refs_0_), channel_id=1, source_target_pairs={{0,4},{4,0},{1,5},{5,1},{2,6},{6,2},{3,7},{7,3},{8,12},{12,8},{9,1... | collective-permute-start | bytes 786440 | tf_op jit(solution)/shard_map/ppermute | solution.py:26
  6.9 1.5 %collective-permute-start = (f32[256,2048]{1,0:T(8,128)}, f32[256,2048]{1,0:T(8,128)S(1)}, u32[]{:S(2)}, u32[]{:S(2)}) collective-permute-start(f32[256,2048]{1,0:T(8,128)} %bitcast.5), channel_id=1, source_target_pairs={{0,16},{16,0},{1,17},{17,1},{2,18},{18,2},{3,19},{19,3},{4,20},{20... | collective-permute-start | bytes 6291464 | tf_op jit(solution)/shard_map/ppermute | solution.py:32
  8.4 1.5 %collective-permute-start.2 = (bf16[1,1024,128]{2,1,0:T(8,128)(2,1)S(1)}, bf16[1,1024,128]{2,1,0:T(8,128)(2,1)S(1)}, u32[]{:S(2)}, u32[]{:S(2)}) collective-permute-start(bf16[1,1024,128]{2,1,0:T(8,128)(2,1)S(1)} %get-tuple-element.23.refs_0_), channel_id=1, source_target_pairs={{0,2},{2,0},{1,3},{3,1},{4,6},{6,4},{5,7},{7,5},{8,10},{10,8},{9,1... | collective-permute-start | bytes 786440 | tf_op jit(solution)/shard_map/ppermute | solution.py:26
  9.9 1.2 copy-done.1
  11.2 0.7 copy-done.3
  12.0 5.3 %collective-permute-done.8.refs_8_ = bf16[1,1024,128]{2,1,0:T(8,128)(2,1)S(1)} collective-permute-done((bf16[1,1024,128]{2,1,0:T(8,128)(2,1)S(1)}, bf16[1,1024,128]{2,1,0:T(8,128)(2,1)S(1)}, u32[]{:S(2)}, u32[]{:S(2)}) %collective-permute-start.8) | collective-permute-done | bytes 262176 | tf_op jit(solution)/shard_map/ppermute | solution.py:26
  17.6 1.6 %collective-permute-start.17 = (bf16[2,1,128,512]{3,2,1,0:T(8,128)(2,1)S(1)}, bf16[2,1,128,512]{3,2,1,0:T(8,128)(2,1)S(1)}, u32[]{:S(2)}, u32[]{:S(2)}) collective-permute-start(bf16[2,1,128,512]{3,2,1,0:T(8,128)(2,1)S(1)} %get-tuple-element.27), channel_id=1, source_target_pairs={{0,2},{2,0},{1,3},{3,1},{4,6},{6,4},{5,7},{7,5},{8,10},{10,8},{9,1... | collective-permute-start | bytes 786440 | tf_op jit(solution)/shard_map/ppermute | solution.py:26
  19.2 1.4 %collective-permute-start.12 = (bf16[1,1024,128]{2,1,0:T(8,128)(2,1)S(1)}, bf16[1,1024,128]{2,1,0:T(8,128)(2,1)S(1)}, u32[]{:S(2)}, u32[]{:S(2)}) collective-permute-start(bf16[1,1024,128]{2,1,0:T(8,128)(2,1)S(1)} %collective-permute-done.8.refs_8_), channel_id=1, source_target_pairs={{0,4},{4,0},{1,5},{5,1},{2,6},{6,2},{3,7},{7,3},{8,12},{12,8},{9,1... | collective-permute-start | bytes 786440 | tf_op jit(solution)/shard_map/ppermute | solution.py:26
  20.6 0.7 collective-permute-start.10
  21.4 5.3 %collective-permute-done.17.refs_2_ = bf16[2,1,128,512]{3,2,1,0:T(8,128)(2,1)S(1)} collective-permute-done((bf16[2,1,128,512]{3,2,1,0:T(8,128)(2,1)S(1)}, bf16[2,1,128,512]{3,2,1,0:T(8,128)(2,1)S(1)}, u32[]{:S(2)}, u32[]{:S(2)}) %collective-permute-start.17) | collective-permute-done | bytes 262176 | tf_op jit(solution)/shard_map/ppermute | solution.py:26
  26.7 4.7 %collective-permute-done.18.refs_3_ = bf16[2,1,128,512]{3,2,1,0:T(8,128)(2,1)S(1)} collective-permute-done((bf16[2,1,128,512]{3,2,1,0:T(8,128)(2,1)S(1)}, bf16[2,1,128,512]{3,2,1,0:T(8,128)(2,1)S(1)}, u32[]{:S(2)}, u32[]{:S(2)}) %collective-permute-start.18) | collective-permute-done | bytes 262176 | tf_op jit(solution)/shard_map/ppermute | solution.py:192
  31.4 1.3 %collective-permute-start.6 = (bf16[1,1024,128]{2,1,0:T(8,128)(2,1)S(1)}, bf16[1,1024,128]{2,1,0:T(8,128)(2,1)S(1)}, u32[]{:S(2)}, u32[]{:S(2)}) collective-permute-start(bf16[1,1024,128]{2,1,0:T(8,128)(2,1)S(1)} %collective-permute-done.4.refs_4_), channel_id=1, source_target_pairs={{0,2},{2,0},{1,3},{3,1},{4,6},{6,4},{5,7},{7,5},{8,10},{10,8},{9,1... | collective-permute-start | bytes 786440 | tf_op jit(solution)/shard_map/ppermute | solution.py:26
  32.7 1.0 collective-permute-start.5
  33.7 4.2 %collective-permute-done.10.refs_10_ = bf16[1,1024,128]{2,1,0:T(8,128)(2,1)S(1)} collective-permute-done((bf16[1,1024,128]{2,1,0:T(8,128)(2,1)S(1)}, bf16[1,1024,128]{2,1,0:T(8,128)(2,1)S(1)}, u32[]{:S(2)}, u32[]{:S(2)}) %collective-permute-start.10) | collective-permute-done | bytes 262176 | tf_op jit(solution)/shard_map/ppermute | solution.py:26
  38.4 4.6 %collective-permute-done.6.refs_6_ = bf16[1,1024,128]{2,1,0:T(8,128)(2,1)S(1)} collective-permute-done((bf16[1,1024,128]{2,1,0:T(8,128)(2,1)S(1)}, bf16[1,1024,128]{2,1,0:T(8,128)(2,1)S(1)}, u32[]{:S(2)}, u32[]{:S(2)}) %collective-permute-start.6) | collective-permute-done | bytes 262176 | tf_op jit(solution)/shard_map/ppermute | solution.py:26
  42.9 3.4 %collective-permute-start.21 = (bf16[4,128,256]{2,1,0:T(8,128)(2,1)S(1)}, bf16[4,128,256]{2,1,0:T(8,128)(2,1)S(1)}, u32[]{:S(2)}, u32[]{:S(2)}) collective-permute-start(bf16[4,128,256]{2,1,0:T(8,128)(2,1)S(1)} %get-tuple-element.30), channel_id=1, source_target_pairs={{0,12},{4,8},{8,4},{12,0},{1,13},{5,9},{9,5},{13,1},{2,14},{6,10},... | collective-permute-start | bytes 786440 | tf_op jit(solution)/shard_map/ppermute | solution.py:27
  46.4 1.6 %collective-permute-start.14 = (bf16[1,1024,128]{2,1,0:T(8,128)(2,1)S(1)}, bf16[1,1024,128]{2,1,0:T(8,128)(2,1)S(1)}, u32[]{:S(2)}, u32[]{:S(2)}) collective-permute-start(bf16[1,1024,128]{2,1,0:T(8,128)(2,1)S(1)} %collective-permute-done.12.refs_12_), channel_id=1, source_target_pairs={{0,2},{2,0},{1,3},{3,1},{4,6},{6,4},{5,7},{7,5},{8,10},{10,8},{9,1... | collective-permute-start | bytes 786440 | tf_op jit(solution)/shard_map/ppermute | solution.py:26
  48.0 11.4 %collective-permute-done.20.refs_18_ = bf16[4,128,256]{2,1,0:T(8,128)(2,1)S(1)} collective-permute-done((bf16[4,128,256]{2,1,0:T(8,128)(2,1)S(1)}, bf16[4,128,256]{2,1,0:T(8,128)(2,1)S(1)}, u32[]{:S(2)}, u32[]{:S(2)}) %collective-permute-start.20) | collective-permute-done | bytes 262176 | tf_op jit(solution)/shard_map/ppermute | solution.py:26
  59.9 4.4 %collective-permute-done.19.refs_17_ = bf16[4,128,256]{2,1,0:T(8,128)(2,1)S(1)} collective-permute-done((bf16[4,128,256]{2,1,0:T(8,128)(2,1)S(1)}, bf16[4,128,256]{2,1,0:T(8,128)(2,1)S(1)}, u32[]{:S(2)}, u32[]{:S(2)}) %collective-permute-start.19) | collective-permute-done | bytes 262176 | tf_op jit(solution)/shard_map/ppermute | solution.py:26
  64.8 0.7 collective-permute-start.23
  65.5 2.6 %collective-permute-start.24 = (bf16[4,128,256]{2,1,0:T(8,128)(2,1)S(1)}, bf16[4,128,256]{2,1,0:T(8,128)(2,1)S(1)}, u32[]{:S(2)}, u32[]{:S(2)}) collective-permute-start(bf16[4,128,256]{2,1,0:T(8,128)(2,1)S(1)} %get-tuple-element.33), channel_id=1, source_target_pairs={{0,12},{4,8},{8,4},{12,0},{1,13},{5,9},{9,5},{13,1},{2,14},{6,10},... | collective-permute-start | bytes 786440 | tf_op jit(solution)/shard_map/ppermute | solution.py:27
  68.3 2.6 %shard_map.49 = (s16[256,256]{1,0:T(8,128)(2,1)S(1)}, s16[256,256]{1,0:T(8,128)(2,1)S(1)}, s16[256,256]{1,0:T(8,128)(2,1)S(1)}, s16[256,256]{1,0:T(8,128)(2,1)S(1)}) custom-call(bf16[1,1024,128]{2,1,0:T(8,128)(2,1)S(1)} %get-tuple-element.23.refs_0_, bf16[1,1024,128]{2,1,0:T(8,128)(2,1)S(1)} %collective-permute-done.1.refs_1_, ...), custom_call_target="tpu_custom_call" | custom-call | flops 1073741824 | bytes 5242880 | tf_op jit(solution)/shard_map/pallas_call | solution.py:37
  70.9 1.6 %collective-permute-start.25 = (s16[256,256]{1,0:T(8,128)(2,1)S(1)}, s16[256,256]{1,0:T(8,128)(2,1)S(1)}, u32[]{:S(2)}, u32[]{:S(2)}) collective-permute-start(s16[256,256]{1,0:T(8,128)(2,1)S(1)} %get-tuple-element.35), channel_id=1, source_target_pairs={{0,2},{2,0},{1,3},{3,1},{4,6},{6,4},{5,7},{7,5},{8,10},{10,8},{9,1... | collective-permute-start | bytes 393224 | tf_op jit(solution)/shard_map/ppermute | solution.py:26
  72.6 13.5 %collective-permute-done.23.refs_18_ = bf16[4,128,256]{2,1,0:T(8,128)(2,1)S(1)} collective-permute-done((bf16[4,128,256]{2,1,0:T(8,128)(2,1)S(1)}, bf16[4,128,256]{2,1,0:T(8,128)(2,1)S(1)}, u32[]{:S(2)}, u32[]{:S(2)}) %collective-permute-start.23) | collective-permute-done | bytes 262176 | tf_op jit(solution)/shard_map/ppermute | solution.py:26
  86.1 6.4 %collective-permute-start.29 = (s16[256,256]{1,0:T(8,128)(2,1)S(1)}, s16[256,256]{1,0:T(8,128)(2,1)S(1)}, u32[]{:S(2)}, u32[]{:S(2)}) collective-permute-start(s16[256,256]{1,0:T(8,128)(2,1)S(1)} %get-tuple-element.39), channel_id=1, source_target_pairs={{0,6},{2,4},{4,2},{6,0},{1,7},{3,5},{5,3},{7,1},{8,14},{10,12},{12... | collective-permute-start | bytes 393224 | tf_op jit(solution)/shard_map/ppermute | solution.py:27
  92.5 1.5 %collective-permute-start.31 = (s16[256,256]{1,0:T(8,128)(2,1)S(1)}, s16[256,256]{1,0:T(8,128)(2,1)S(1)}, u32[]{:S(2)}, u32[]{:S(2)}) collective-permute-start(s16[256,256]{1,0:T(8,128)(2,1)S(1)} %get-tuple-element.31.refs_2_), channel_id=1, source_target_pairs={{0,16},{16,0},{1,17},{17,1},{2,18},{18,2},{3,19},{19,3},{4,20},{20... | collective-permute-start | bytes 393224 | tf_op jit(solution)/shard_map/ppermute | solution.py:32
  94.0 2.6 %shard_map.50 = (s16[256,256]{1,0:T(8,128)(2,1)S(1)}, s16[256,256]{1,0:T(8,128)(2,1)S(1)}, s16[256,256]{1,0:T(8,128)(2,1)S(1)}, s16[256,256]{1,0:T(8,128)(2,1)S(1)}) custom-call(bf16[1,1024,128]{2,1,0:T(8,128)(2,1)S(1)} %get-tuple-element.23.refs_0_, bf16[1,1024,128]{2,1,0:T(8,128)(2,1)S(1)} %collective-permute-done.1.refs_1_, ...), custom_call_target="tpu_custom_call" | custom-call | flops 1073741824 | bytes 5242880 | tf_op jit(solution)/shard_map/pallas_call | solution.py:37
  96.6 0.6 collective-permute-start.26
  97.3 2.8 %collective-permute-start.30 = (s16[256,256]{1,0:T(8,128)(2,1)S(1)}, s16[256,256]{1,0:T(8,128)(2,1)S(1)}, u32[]{:S(2)}, u32[]{:S(2)}) collective-permute-start(s16[256,256]{1,0:T(8,128)(2,1)S(1)} %get-tuple-element.40), channel_id=1, source_target_pairs={{0,6},{2,4},{4,2},{6,0},{1,7},{3,5},{5,3},{7,1},{8,14},{10,12},{12... | collective-permute-start | bytes 393224 | tf_op jit(solution)/shard_map/ppermute | solution.py:27
  100.1 0.5 collective-permute-start.32
  100.7 2.3 %collective-permute-done.26.refs_5_ = s16[256,256]{1,0:T(8,128)(2,1)S(1)} collective-permute-done((s16[256,256]{1,0:T(8,128)(2,1)S(1)}, s16[256,256]{1,0:T(8,128)(2,1)S(1)}, u32[]{:S(2)}, u32[]{:S(2)}) %collective-permute-start.26) | collective-permute-done | bytes 131104 | tf_op jit(solution)/shard_map/ppermute | solution.py:26
  103.0 0.5 collective-permute-start.33
  103.6 1.5 %collective-permute-start.35 = (s16[256,256]{1,0:T(8,128)(2,1)S(1)}, s16[256,256]{1,0:T(8,128)(2,1)S(1)}, u32[]{:S(2)}, u32[]{:S(2)}) collective-permute-start(s16[256,256]{1,0:T(8,128)(2,1)S(1)} %collective-permute-done.27.refs_6_), channel_id=1, source_target_pairs={{0,16},{16,0},{1,17},{17,1},{2,18},{18,2},{3,19},{19,3},{4,20},{20... | collective-permute-start | bytes 393224 | tf_op jit(solution)/shard_map/ppermute | solution.py:32
  105.1 0.5 collective-permute-start.37
  105.6 1.0 collective-permute-done.32.refs_11_
  106.6 0.5 collective-permute-start.34
  107.1 2.3 %collective-permute-done.33.refs_12_ = s16[256,256]{1,0:T(8,128)(2,1)S(1)} collective-permute-done((s16[256,256]{1,0:T(8,128)(2,1)S(1)}, s16[256,256]{1,0:T(8,128)(2,1)S(1)}, u32[]{:S(2)}, u32[]{:S(2)}) %collective-permute-start.33) | collective-permute-done | bytes 131104 | tf_op jit(solution)/shard_map/ppermute | solution.py:32
  109.5 0.5 collective-permute-start.36
  110.0 2.3 %collective-permute-done.35.refs_14_ = s16[256,256]{1,0:T(8,128)(2,1)S(1)} collective-permute-done((s16[256,256]{1,0:T(8,128)(2,1)S(1)}, s16[256,256]{1,0:T(8,128)(2,1)S(1)}, u32[]{:S(2)}, u32[]{:S(2)}) %collective-permute-start.35) | collective-permute-done | bytes 131104 | tf_op jit(solution)/shard_map/ppermute | solution.py:32
  112.3 0.5 collective-permute-start.38
  112.8 2.3 %collective-permute-done.37.refs_16_ = s16[256,256]{1,0:T(8,128)(2,1)S(1)} collective-permute-done((s16[256,256]{1,0:T(8,128)(2,1)S(1)}, s16[256,256]{1,0:T(8,128)(2,1)S(1)}, u32[]{:S(2)}, u32[]{:S(2)}) %collective-permute-start.37) | collective-permute-done | bytes 131104 | tf_op jit(solution)/shard_map/ppermute | solution.py:32
  115.1 2.4 %collective-permute-done.34.refs_13_ = s16[256,256]{1,0:T(8,128)(2,1)S(1)} collective-permute-done((s16[256,256]{1,0:T(8,128)(2,1)S(1)}, s16[256,256]{1,0:T(8,128)(2,1)S(1)}, u32[]{:S(2)}, u32[]{:S(2)}) %collective-permute-start.34) | collective-permute-done | bytes 131104 | tf_op jit(solution)/shard_map/ppermute | solution.py:32
  117.5 1.4 %collective-permute-done.36.refs_15_ = s16[256,256]{1,0:T(8,128)(2,1)S(1)} collective-permute-done((s16[256,256]{1,0:T(8,128)(2,1)S(1)}, s16[256,256]{1,0:T(8,128)(2,1)S(1)}, u32[]{:S(2)}, u32[]{:S(2)}) %collective-permute-start.36) | collective-permute-done | bytes 131104 | tf_op jit(solution)/shard_map/ppermute | solution.py:32
  118.9 1.4 %collective-permute-done.38.refs_17_ = s16[256,256]{1,0:T(8,128)(2,1)S(1)} collective-permute-done((s16[256,256]{1,0:T(8,128)(2,1)S(1)}, s16[256,256]{1,0:T(8,128)(2,1)S(1)}, u32[]{:S(2)}, u32[]{:S(2)}) %collective-permute-start.38) | collective-permute-done | bytes 131104 | tf_op jit(solution)/shard_map/ppermute | solution.py:32
  120.3 1.3 %copy-done.4 = f32[256,2048]{1,0:T(8,128)} copy-done((f32[256,2048]{1,0:T(8,128)}, f32[256,2048]{1,0:T(8,128)S(1)}, u32[]{:S(2)}) %copy-start.4) | copy-done | bytes 2097176
  121.6 4.6 %shard_map.51 = f32[256,2048]{1,0:T(8,128)} custom-call(f32[256,2048]{1,0:T(8,128)S(1)} %bitcast.6, f32[256,2048]{1,0:T(8,128)} %copy-done.4, s16[256,256]{1,0:T(8,128)(2,1)S(1)} %get-tuple-element.31.refs_2_, s16[256,256]{1,0:T(8,128)(2,1)S(1)} %get-tuple-element.34.refs_3_, s16[256,256]{1,0:T(8,128)(2,1)S(1)} %collective-permute-done.25.refs_4_, ...), custom_call_target="tpu_custom_call" | custom-call | tf_op jit(solution)/shard_map/pallas_call | solution.py:37
  (46 shorter events, 2.5 us)
Async XLA Ops:
  0.0 1.0 copy-start.2
  1.2 16.1 %collective-permute-start.8 = (bf16[1,1024,128]{2,1,0:T(8,128)(2,1)S(1)}, bf16[1,1024,128]{2,1,0:T(8,128)(2,1)S(1)}, u32[]{:S(2)}, u32[]{:S(2)}) collective-permute-start(bf16[1,1024,128]{2,1,0:T(8,128)(2,1)S(1)} %get-tuple-element.24), channel_id=1, source_target_pairs={{0,8},{8,0},{1,9},{9,1},{2,10},{10,2},{3,11},{11,3},{4,12},{12,4},... | collective-permute-start | bytes 786440 | tf_op jit(solution)/shard_map/ppermute | solution.py:26
  5.3 12.2 %collective-permute-start.4 = (bf16[1,1024,128]{2,1,0:T(8,128)(2,1)S(1)}, bf16[1,1024,128]{2,1,0:T(8,128)(2,1)S(1)}, u32[]{:S(2)}, u32[]{:S(2)}) collective-permute-start(bf16[1,1024,128]{2,1,0:T(8,128)(2,1)S(1)} %get-tuple-element.23.refs_0_), channel_id=1, source_target_pairs={{0,4},{4,0},{1,5},{5,1},{2,6},{6,2},{3,7},{7,3},{8,12},{12,8},{9,1... | collective-permute-start | bytes 786440 | tf_op jit(solution)/shard_map/ppermute | solution.py:26
  6.9 113.4 %collective-permute-start = (f32[256,2048]{1,0:T(8,128)}, f32[256,2048]{1,0:T(8,128)S(1)}, u32[]{:S(2)}, u32[]{:S(2)}) collective-permute-start(f32[256,2048]{1,0:T(8,128)} %bitcast.5), channel_id=1, source_target_pairs={{0,16},{16,0},{1,17},{17,1},{2,18},{18,2},{3,19},{19,3},{4,20},{20... | collective-permute-start | bytes 6291464 | tf_op jit(solution)/shard_map/ppermute | solution.py:32
  8.4 10.7 %collective-permute-start.2 = (bf16[1,1024,128]{2,1,0:T(8,128)(2,1)S(1)}, bf16[1,1024,128]{2,1,0:T(8,128)(2,1)S(1)}, u32[]{:S(2)}, u32[]{:S(2)}) collective-permute-start(bf16[1,1024,128]{2,1,0:T(8,128)(2,1)S(1)} %get-tuple-element.23.refs_0_), channel_id=1, source_target_pairs={{0,2},{2,0},{1,3},{3,1},{4,6},{6,4},{5,7},{7,5},{8,10},{10,8},{9,1... | collective-permute-start | bytes 786440 | tf_op jit(solution)/shard_map/ppermute | solution.py:26
  9.9 9.3 %collective-permute-start.1 = (bf16[1,1024,128]{2,1,0:T(8,128)(2,1)S(1)}, bf16[1,1024,128]{2,1,0:T(8,128)(2,1)S(1)}, u32[]{:S(2)}, u32[]{:S(2)}) collective-permute-start(bf16[1,1024,128]{2,1,0:T(8,128)(2,1)S(1)} %get-tuple-element.23.refs_0_), channel_id=1, source_target_pairs={{0,1},{1,0},{2,3},{3,2},{4,5},{5,4},{6,7},{7,6},{8,9},{9,8},{10,11... | collective-permute-start | bytes 786440 | tf_op jit(solution)/shard_map/ppermute | solution.py:32
  9.9 1.2 copy-start.1
  11.2 0.7 copy-start.3
  17.4 3.3 %collective-permute-start.16 = (bf16[2,1,128,512]{3,2,1,0:T(8,128)(2,1)S(1)}, bf16[2,1,128,512]{3,2,1,0:T(8,128)(2,1)S(1)}, u32[]{:S(2)}, u32[]{:S(2)}) collective-permute-start(bf16[2,1,128,512]{3,2,1,0:T(8,128)(2,1)S(1)} %get-tuple-element.26), channel_id=1, source_target_pairs={{0,1},{1,0},{2,3},{3,2},{4,5},{5,4},{6,7},{7,6},{8,9},{9,8},{10,11... | collective-permute-start | bytes 786440 | tf_op jit(solution)/shard_map/ppermute | solution.py:32
  17.6 9.1 %collective-permute-start.17 = (bf16[2,1,128,512]{3,2,1,0:T(8,128)(2,1)S(1)}, bf16[2,1,128,512]{3,2,1,0:T(8,128)(2,1)S(1)}, u32[]{:S(2)}, u32[]{:S(2)}) collective-permute-start(bf16[2,1,128,512]{3,2,1,0:T(8,128)(2,1)S(1)} %get-tuple-element.27), channel_id=1, source_target_pairs={{0,2},{2,0},{1,3},{3,1},{4,6},{6,4},{5,7},{7,5},{8,10},{10,8},{9,1... | collective-permute-start | bytes 786440 | tf_op jit(solution)/shard_map/ppermute | solution.py:26
  19.1 12.3 %collective-permute-start.18 = (bf16[2,1,128,512]{3,2,1,0:T(8,128)(2,1)S(1)}, bf16[2,1,128,512]{3,2,1,0:T(8,128)(2,1)S(1)}, u32[]{:S(2)}, u32[]{:S(2)}) collective-permute-start(bf16[2,1,128,512]{3,2,1,0:T(8,128)(2,1)S(1)} %get-tuple-element.28), channel_id=1, source_target_pairs={{0,3},{1,2},{2,1},{3,0},{4,7},{5,6},{6,5},{7,4},{8,11},{9,10},{10,... | collective-permute-start | bytes 786440 | tf_op jit(solution)/shard_map/ppermute | solution.py:192
  19.2 13.4 %collective-permute-start.12 = (bf16[1,1024,128]{2,1,0:T(8,128)(2,1)S(1)}, bf16[1,1024,128]{2,1,0:T(8,128)(2,1)S(1)}, u32[]{:S(2)}, u32[]{:S(2)}) collective-permute-start(bf16[1,1024,128]{2,1,0:T(8,128)(2,1)S(1)} %collective-permute-done.8.refs_8_), channel_id=1, source_target_pairs={{0,4},{4,0},{1,5},{5,1},{2,6},{6,2},{3,7},{7,3},{8,12},{12,8},{9,1... | collective-permute-start | bytes 786440 | tf_op jit(solution)/shard_map/ppermute | solution.py:26
  20.6 17.3 %collective-permute-start.10 = (bf16[1,1024,128]{2,1,0:T(8,128)(2,1)S(1)}, bf16[1,1024,128]{2,1,0:T(8,128)(2,1)S(1)}, u32[]{:S(2)}, u32[]{:S(2)}) collective-permute-start(bf16[1,1024,128]{2,1,0:T(8,128)(2,1)S(1)} %collective-permute-done.8.refs_8_), channel_id=1, source_target_pairs={{0,2},{2,0},{1,3},{3,1},{4,6},{6,4},{5,7},{7,5},{8,10},{10,8},{9,1... | collective-permute-start | bytes 786440 | tf_op jit(solution)/shard_map/ppermute | solution.py:26
  26.7 11.3 %collective-permute-start.9 = (bf16[1,1024,128]{2,1,0:T(8,128)(2,1)S(1)}, bf16[1,1024,128]{2,1,0:T(8,128)(2,1)S(1)}, u32[]{:S(2)}, u32[]{:S(2)}) collective-permute-start(bf16[1,1024,128]{2,1,0:T(8,128)(2,1)S(1)} %collective-permute-done.8.refs_8_), channel_id=1, source_target_pairs={{0,1},{1,0},{2,3},{3,2},{4,5},{5,4},{6,7},{7,6},{8,9},{9,8},{10,11... | collective-permute-start | bytes 786440 | tf_op jit(solution)/shard_map/ppermute | solution.py:32
  31.4 11.5 %collective-permute-start.6 = (bf16[1,1024,128]{2,1,0:T(8,128)(2,1)S(1)}, bf16[1,1024,128]{2,1,0:T(8,128)(2,1)S(1)}, u32[]{:S(2)}, u32[]{:S(2)}) collective-permute-start(bf16[1,1024,128]{2,1,0:T(8,128)(2,1)S(1)} %collective-permute-done.4.refs_4_), channel_id=1, source_target_pairs={{0,2},{2,0},{1,3},{3,1},{4,6},{6,4},{5,7},{7,5},{8,10},{10,8},{9,1... | collective-permute-start | bytes 786440 | tf_op jit(solution)/shard_map/ppermute | solution.py:26
  32.7 13.7 %collective-permute-start.5 = (bf16[1,1024,128]{2,1,0:T(8,128)(2,1)S(1)}, bf16[1,1024,128]{2,1,0:T(8,128)(2,1)S(1)}, u32[]{:S(2)}, u32[]{:S(2)}) collective-permute-start(bf16[1,1024,128]{2,1,0:T(8,128)(2,1)S(1)} %collective-permute-done.4.refs_4_), channel_id=1, source_target_pairs={{0,1},{1,0},{2,3},{3,2},{4,5},{5,4},{6,7},{7,6},{8,9},{9,8},{10,11... | collective-permute-start | bytes 786440 | tf_op jit(solution)/shard_map/ppermute | solution.py:32
  37.9 8.5 %collective-permute-start.3 = (bf16[1,1024,128]{2,1,0:T(8,128)(2,1)S(1)}, bf16[1,1024,128]{2,1,0:T(8,128)(2,1)S(1)}, u32[]{:S(2)}, u32[]{:S(2)}) collective-permute-start(bf16[1,1024,128]{2,1,0:T(8,128)(2,1)S(1)} %collective-permute-done.2.refs_2_), channel_id=1, source_target_pairs={{0,1},{1,0},{2,3},{3,2},{4,5},{5,4},{6,7},{7,6},{8,9},{9,8},{10,11... | collective-permute-start | bytes 786440 | tf_op jit(solution)/shard_map/ppermute | solution.py:32
  38.0 21.3 %collective-permute-start.20 = (bf16[4,128,256]{2,1,0:T(8,128)(2,1)S(1)}, bf16[4,128,256]{2,1,0:T(8,128)(2,1)S(1)}, u32[]{:S(2)}, u32[]{:S(2)}) collective-permute-start(bf16[4,128,256]{2,1,0:T(8,128)(2,1)S(1)} %get-tuple-element.29.refs_16_), channel_id=1, source_target_pairs={{0,8},{8,0},{1,9},{9,1},{2,10},{10,2},{3,11},{11,3},{4,12},{12,4},... | collective-permute-start | bytes 786440 | tf_op jit(solution)/shard_map/ppermute | solution.py:26
  42.9 16.4 %collective-permute-start.21 = (bf16[4,128,256]{2,1,0:T(8,128)(2,1)S(1)}, bf16[4,128,256]{2,1,0:T(8,128)(2,1)S(1)}, u32[]{:S(2)}, u32[]{:S(2)}) collective-permute-start(bf16[4,128,256]{2,1,0:T(8,128)(2,1)S(1)} %get-tuple-element.30), channel_id=1, source_target_pairs={{0,12},{4,8},{8,4},{12,0},{1,13},{5,9},{9,5},{13,1},{2,14},{6,10},... | collective-permute-start | bytes 786440 | tf_op jit(solution)/shard_map/ppermute | solution.py:27
  46.4 17.9 %collective-permute-start.19 = (bf16[4,128,256]{2,1,0:T(8,128)(2,1)S(1)}, bf16[4,128,256]{2,1,0:T(8,128)(2,1)S(1)}, u32[]{:S(2)}, u32[]{:S(2)}) collective-permute-start(bf16[4,128,256]{2,1,0:T(8,128)(2,1)S(1)} %get-tuple-element.30), channel_id=1, source_target_pairs={{0,4},{4,0},{1,5},{5,1},{2,6},{6,2},{3,7},{7,3},{8,12},{12,8},{9,1... | collective-permute-start | bytes 786440 | tf_op jit(solution)/shard_map/ppermute | solution.py:26
  46.4 17.9 %collective-permute-start.14 = (bf16[1,1024,128]{2,1,0:T(8,128)(2,1)S(1)}, bf16[1,1024,128]{2,1,0:T(8,128)(2,1)S(1)}, u32[]{:S(2)}, u32[]{:S(2)}) collective-permute-start(bf16[1,1024,128]{2,1,0:T(8,128)(2,1)S(1)} %collective-permute-done.12.refs_12_), channel_id=1, source_target_pairs={{0,2},{2,0},{1,3},{3,1},{4,6},{6,4},{5,7},{7,5},{8,10},{10,8},{9,1... | collective-permute-start | bytes 786440 | tf_op jit(solution)/shard_map/ppermute | solution.py:26
  59.4 5.5 %collective-permute-start.13 = (bf16[1,1024,128]{2,1,0:T(8,128)(2,1)S(1)}, bf16[1,1024,128]{2,1,0:T(8,128)(2,1)S(1)}, u32[]{:S(2)}, u32[]{:S(2)}) collective-permute-start(bf16[1,1024,128]{2,1,0:T(8,128)(2,1)S(1)} %collective-permute-done.12.refs_12_), channel_id=1, source_target_pairs={{0,1},{1,0},{2,3},{3,2},{4,5},{5,4},{6,7},{7,6},{8,9},{9,8},{10,11... | collective-permute-start | bytes 786440 | tf_op jit(solution)/shard_map/ppermute | solution.py:32
  59.4 6.1 %collective-permute-start.11 = (bf16[1,1024,128]{2,1,0:T(8,128)(2,1)S(1)}, bf16[1,1024,128]{2,1,0:T(8,128)(2,1)S(1)}, u32[]{:S(2)}, u32[]{:S(2)}) collective-permute-start(bf16[1,1024,128]{2,1,0:T(8,128)(2,1)S(1)} %collective-permute-done.10.refs_10_), channel_id=1, source_target_pairs={{0,1},{1,0},{2,3},{3,2},{4,5},{5,4},{6,7},{7,6},{8,9},{9,8},{10,11... | collective-permute-start | bytes 786440 | tf_op jit(solution)/shard_map/ppermute | solution.py:32
  64.3 3.8 %collective-permute-start.7 = (bf16[1,1024,128]{2,1,0:T(8,128)(2,1)S(1)}, bf16[1,1024,128]{2,1,0:T(8,128)(2,1)S(1)}, u32[]{:S(2)}, u32[]{:S(2)}) collective-permute-start(bf16[1,1024,128]{2,1,0:T(8,128)(2,1)S(1)} %collective-permute-done.6.refs_6_), channel_id=1, source_target_pairs={{0,1},{1,0},{2,3},{3,2},{4,5},{5,4},{6,7},{7,6},{8,9},{9,8},{10,11... | collective-permute-start | bytes 786440 | tf_op jit(solution)/shard_map/ppermute | solution.py:32
  64.3 4.0 %collective-permute-start.15 = (bf16[1,1024,128]{2,1,0:T(8,128)(2,1)S(1)}, bf16[1,1024,128]{2,1,0:T(8,128)(2,1)S(1)}, u32[]{:S(2)}, u32[]{:S(2)}) collective-permute-start(bf16[1,1024,128]{2,1,0:T(8,128)(2,1)S(1)} %collective-permute-done.14.refs_14_), channel_id=1, source_target_pairs={{0,1},{1,0},{2,3},{3,2},{4,5},{5,4},{6,7},{7,6},{8,9},{9,8},{10,11... | collective-permute-start | bytes 786440 | tf_op jit(solution)/shard_map/ppermute | solution.py:32
  64.8 21.3 %collective-permute-start.23 = (bf16[4,128,256]{2,1,0:T(8,128)(2,1)S(1)}, bf16[4,128,256]{2,1,0:T(8,128)(2,1)S(1)}, u32[]{:S(2)}, u32[]{:S(2)}) collective-permute-start(bf16[4,128,256]{2,1,0:T(8,128)(2,1)S(1)} %get-tuple-element.32.refs_16_), channel_id=1, source_target_pairs={{0,8},{8,0},{1,9},{9,1},{2,10},{10,2},{3,11},{11,3},{4,12},{12,4},... | collective-permute-start | bytes 786440 | tf_op jit(solution)/shard_map/ppermute | solution.py:26
  65.5 20.6 %collective-permute-start.24 = (bf16[4,128,256]{2,1,0:T(8,128)(2,1)S(1)}, bf16[4,128,256]{2,1,0:T(8,128)(2,1)S(1)}, u32[]{:S(2)}, u32[]{:S(2)}) collective-permute-start(bf16[4,128,256]{2,1,0:T(8,128)(2,1)S(1)} %get-tuple-element.33), channel_id=1, source_target_pairs={{0,12},{4,8},{8,4},{12,0},{1,13},{5,9},{9,5},{13,1},{2,14},{6,10},... | collective-permute-start | bytes 786440 | tf_op jit(solution)/shard_map/ppermute | solution.py:27
  68.1 24.4 %collective-permute-start.22 = (bf16[4,128,256]{2,1,0:T(8,128)(2,1)S(1)}, bf16[4,128,256]{2,1,0:T(8,128)(2,1)S(1)}, u32[]{:S(2)}, u32[]{:S(2)}) collective-permute-start(bf16[4,128,256]{2,1,0:T(8,128)(2,1)S(1)} %get-tuple-element.33), channel_id=1, source_target_pairs={{0,4},{4,0},{1,5},{5,1},{2,6},{6,2},{3,7},{7,3},{8,12},{12,8},{9,1... | collective-permute-start | bytes 786440 | tf_op jit(solution)/shard_map/ppermute | solution.py:26
  70.9 25.6 %collective-permute-start.25 = (s16[256,256]{1,0:T(8,128)(2,1)S(1)}, s16[256,256]{1,0:T(8,128)(2,1)S(1)}, u32[]{:S(2)}, u32[]{:S(2)}) collective-permute-start(s16[256,256]{1,0:T(8,128)(2,1)S(1)} %get-tuple-element.35), channel_id=1, source_target_pairs={{0,2},{2,0},{1,3},{3,1},{4,6},{6,4},{5,7},{7,5},{8,10},{10,8},{9,1... | collective-permute-start | bytes 393224 | tf_op jit(solution)/shard_map/ppermute | solution.py:26
  86.1 11.1 %collective-permute-start.27 = (s16[256,256]{1,0:T(8,128)(2,1)S(1)}, s16[256,256]{1,0:T(8,128)(2,1)S(1)}, u32[]{:S(2)}, u32[]{:S(2)}) collective-permute-start(s16[256,256]{1,0:T(8,128)(2,1)S(1)} %get-tuple-element.37), channel_id=1, source_target_pairs={{0,4},{4,0},{1,5},{5,1},{2,6},{6,2},{3,7},{7,3},{8,12},{12,8},{9,1... | collective-permute-start | bytes 393224 | tf_op jit(solution)/shard_map/ppermute | solution.py:26
  86.1 11.2 %collective-permute-start.29 = (s16[256,256]{1,0:T(8,128)(2,1)S(1)}, s16[256,256]{1,0:T(8,128)(2,1)S(1)}, u32[]{:S(2)}, u32[]{:S(2)}) collective-permute-start(s16[256,256]{1,0:T(8,128)(2,1)S(1)} %get-tuple-element.39), channel_id=1, source_target_pairs={{0,6},{2,4},{4,2},{6,0},{1,7},{3,5},{5,3},{7,1},{8,14},{10,12},{12... | collective-permute-start | bytes 393224 | tf_op jit(solution)/shard_map/ppermute | solution.py:27
  92.5 29.2 %copy-start = (f32[1,1,256,2048]{3,2,1,0:T(8,128)S(1)}, f32[1,1,256,2048]{3,2,1,0:T(8,128)}, u32[]{:S(2)}) copy-start(f32[1,1,256,2048]{3,2,1,0:T(8,128)} %param.7) | copy-start | bytes 6291460
  92.5 7.7 %collective-permute-start.31 = (s16[256,256]{1,0:T(8,128)(2,1)S(1)}, s16[256,256]{1,0:T(8,128)(2,1)S(1)}, u32[]{:S(2)}, u32[]{:S(2)}) collective-permute-start(s16[256,256]{1,0:T(8,128)(2,1)S(1)} %get-tuple-element.31.refs_2_), channel_id=1, source_target_pairs={{0,16},{16,0},{1,17},{17,1},{2,18},{18,2},{3,19},{19,3},{4,20},{20... | collective-permute-start | bytes 393224 | tf_op jit(solution)/shard_map/ppermute | solution.py:32
  96.6 6.4 %collective-permute-start.26 = (s16[256,256]{1,0:T(8,128)(2,1)S(1)}, s16[256,256]{1,0:T(8,128)(2,1)S(1)}, u32[]{:S(2)}, u32[]{:S(2)}) collective-permute-start(s16[256,256]{1,0:T(8,128)(2,1)S(1)} %get-tuple-element.36), channel_id=1, source_target_pairs={{0,2},{2,0},{1,3},{3,1},{4,6},{6,4},{5,7},{7,5},{8,10},{10,8},{9,1... | collective-permute-start | bytes 393224 | tf_op jit(solution)/shard_map/ppermute | solution.py:26
  97.2 6.4 %collective-permute-start.28 = (s16[256,256]{1,0:T(8,128)(2,1)S(1)}, s16[256,256]{1,0:T(8,128)(2,1)S(1)}, u32[]{:S(2)}, u32[]{:S(2)}) collective-permute-start(s16[256,256]{1,0:T(8,128)(2,1)S(1)} %get-tuple-element.38), channel_id=1, source_target_pairs={{0,4},{4,0},{1,5},{5,1},{2,6},{6,2},{3,7},{7,3},{8,12},{12,8},{9,1... | collective-permute-start | bytes 393224 | tf_op jit(solution)/shard_map/ppermute | solution.py:26
  97.3 7.8 %collective-permute-start.30 = (s16[256,256]{1,0:T(8,128)(2,1)S(1)}, s16[256,256]{1,0:T(8,128)(2,1)S(1)}, u32[]{:S(2)}, u32[]{:S(2)}) collective-permute-start(s16[256,256]{1,0:T(8,128)(2,1)S(1)} %get-tuple-element.40), channel_id=1, source_target_pairs={{0,6},{2,4},{4,2},{6,0},{1,7},{3,5},{5,3},{7,1},{8,14},{10,12},{12... | collective-permute-start | bytes 393224 | tf_op jit(solution)/shard_map/ppermute | solution.py:27
  100.1 6.4 %collective-permute-start.32 = (s16[256,256]{1,0:T(8,128)(2,1)S(1)}, s16[256,256]{1,0:T(8,128)(2,1)S(1)}, u32[]{:S(2)}, u32[]{:S(2)}) collective-permute-start(s16[256,256]{1,0:T(8,128)(2,1)S(1)} %get-tuple-element.34.refs_3_), channel_id=1, source_target_pairs={{0,16},{16,0},{1,17},{17,1},{2,18},{18,2},{3,19},{19,3},{4,20},{20... | collective-permute-start | bytes 393224 | tf_op jit(solution)/shard_map/ppermute | solution.py:32
  103.0 6.4 %collective-permute-start.33 = (s16[256,256]{1,0:T(8,128)(2,1)S(1)}, s16[256,256]{1,0:T(8,128)(2,1)S(1)}, u32[]{:S(2)}, u32[]{:S(2)}) collective-permute-start(s16[256,256]{1,0:T(8,128)(2,1)S(1)} %collective-permute-done.25.refs_4_), channel_id=1, source_target_pairs={{0,16},{16,0},{1,17},{17,1},{2,18},{18,2},{3,19},{19,3},{4,20},{20... | collective-permute-start | bytes 393224 | tf_op jit(solution)/shard_map/ppermute | solution.py:32
  103.6 8.7 %collective-permute-start.35 = (s16[256,256]{1,0:T(8,128)(2,1)S(1)}, s16[256,256]{1,0:T(8,128)(2,1)S(1)}, u32[]{:S(2)}, u32[]{:S(2)}) collective-permute-start(s16[256,256]{1,0:T(8,128)(2,1)S(1)} %collective-permute-done.27.refs_6_), channel_id=1, source_target_pairs={{0,16},{16,0},{1,17},{17,1},{2,18},{18,2},{3,19},{19,3},{4,20},{20... | collective-permute-start | bytes 393224 | tf_op jit(solution)/shard_map/ppermute | solution.py:32
  105.1 10.0 %collective-permute-start.37 = (s16[256,256]{1,0:T(8,128)(2,1)S(1)}, s16[256,256]{1,0:T(8,128)(2,1)S(1)}, u32[]{:S(2)}, u32[]{:S(2)}) collective-permute-start(s16[256,256]{1,0:T(8,128)(2,1)S(1)} %collective-permute-done.29.refs_8_), channel_id=1, source_target_pairs={{0,16},{16,0},{1,17},{17,1},{2,18},{18,2},{3,19},{19,3},{4,20},{20... | collective-permute-start | bytes 393224 | tf_op jit(solution)/shard_map/ppermute | solution.py:32
  106.6 10.9 %collective-permute-start.34 = (s16[256,256]{1,0:T(8,128)(2,1)S(1)}, s16[256,256]{1,0:T(8,128)(2,1)S(1)}, u32[]{:S(2)}, u32[]{:S(2)}) collective-permute-start(s16[256,256]{1,0:T(8,128)(2,1)S(1)} %collective-permute-done.26.refs_5_), channel_id=1, source_target_pairs={{0,16},{16,0},{1,17},{17,1},{2,18},{18,2},{3,19},{19,3},{4,20},{20... | collective-permute-start | bytes 393224 | tf_op jit(solution)/shard_map/ppermute | solution.py:32
  109.5 9.4 %collective-permute-start.36 = (s16[256,256]{1,0:T(8,128)(2,1)S(1)}, s16[256,256]{1,0:T(8,128)(2,1)S(1)}, u32[]{:S(2)}, u32[]{:S(2)}) collective-permute-start(s16[256,256]{1,0:T(8,128)(2,1)S(1)} %collective-permute-done.28.refs_7_), channel_id=1, source_target_pairs={{0,16},{16,0},{1,17},{17,1},{2,18},{18,2},{3,19},{19,3},{4,20},{20... | collective-permute-start | bytes 393224 | tf_op jit(solution)/shard_map/ppermute | solution.py:32
  112.3 8.0 %collective-permute-start.38 = (s16[256,256]{1,0:T(8,128)(2,1)S(1)}, s16[256,256]{1,0:T(8,128)(2,1)S(1)}, u32[]{:S(2)}, u32[]{:S(2)}) collective-permute-start(s16[256,256]{1,0:T(8,128)(2,1)S(1)} %collective-permute-done.30.refs_9_), channel_id=1, source_target_pairs={{0,16},{16,0},{1,17},{17,1},{2,18},{18,2},{3,19},{19,3},{4,20},{20... | collective-permute-start | bytes 393224 | tf_op jit(solution)/shard_map/ppermute | solution.py:32
  120.3 1.3 %copy-start.4 = (f32[256,2048]{1,0:T(8,128)}, f32[256,2048]{1,0:T(8,128)S(1)}, u32[]{:S(2)}) copy-start(f32[256,2048]{1,0:T(8,128)S(1)} %collective-permute-done.refs_1_) | copy-start | bytes 6291460

commit v2 on v1

v2 whole, which is shorter than its diff:
```python
import functools
import math

import jax
import jax.numpy as jnp
from jax import lax
from jax.experimental import pallas as pl
from jax.experimental.pallas import tpu as pltpu
from jax.sharding import Mesh
from jax.sharding import PartitionSpec as P

ROW_BLOCKS = 8
FIRST_TEXT = 37984
LARGEST = 6.0

damping = 0.1

TOK = ("zh", "zl", "y", "c")
VMEM = pl.BlockSpec(memory_space=pltpu.VMEM)
VMEM_LIMIT = 48 * 1024 * 1024

CHUNKS = (0.5, 0.5)


def swap(value, axes):
    if isinstance(axes, str):
        return lax.ppermute(value, axes, [(0, 1), (1, 0)])
    return lax.ppermute(value, axes, [(i, i ^ 3) for i in range(4)])


def rotate(value, axis, offset):
    size = lax.axis_size(axis)
    return lax.ppermute(value, axis, [(i, (i + offset) % size) for i in range(size)])


def call(body, out_shape, scratch_shapes=(), flops=0, bytes_accessed=0):
    def run(*args, after=()):
        def kernel(*refs):
            body(*refs[: len(args)], *refs[len(args) + len(after) :])

        return pl.pallas_call(
            kernel,
            out_shape=out_shape,
            in_specs=[VMEM] * len(args) + [pl.BlockSpec(memory_space=pl.ANY)] * len(after),
            out_specs=jax.tree.map(lambda _: VMEM, out_shape),
            scratch_shapes=list(scratch_shapes),
            compiler_params=pltpu.CompilerParams(vmem_limit_bytes=VMEM_LIMIT),
            cost_estimate=pl.CostEstimate(flops=flops, bytes_accessed=bytes_accessed, transcendentals=0),
        )(*args, *after)

    return run


def front_kernel(inputs_ref, ids_ref, cot_ref, keep_ref, send_ref, *outs):
    half = keep_ref.shape[1]
    own = lax.axis_index("zh")
    for ref, part in ((keep_ref, own), (send_ref, 1 - own)):
        for s in range(inputs_ref.shape[0]):
            start = pl.multiple_of(part * half, half)
            ref[s] = inputs_ref[s, :, pl.ds(start, half)].T
    seqs, length, width = ids_ref.shape[0], cot_ref.shape[1], outs[0].shape[3]
    core_count = len(outs) // 2
    own_y, own_c = lax.axis_index("y"), lax.axis_index("c")
    for s in range(seqs):
        kept = jnp.broadcast_to((ids_ref[s : s + 1, :] >= FIRST_TEXT).astype(jnp.float32), (128, length)).T
        kept = kept[:, :1] > 0.5
        for at, ref in enumerate(outs):
            to_y = own_y ^ (at // core_count)
            to_c = lax.rem(own_c + at % core_count, core_count)
            for zl in range(2):
                start = pl.multiple_of(((to_c * 2 + zl) * 2 + to_y) * width, width)
                piece = cot_ref[s, :, pl.ds(start, width)]
                ref[zl, s] = jnp.where(kept, piece, jnp.zeros_like(piece))


def fill(out, *refs):
    at = 0
    for ref in refs:
        out[at : at + ref.shape[0]] = ref[...]
        at += ref.shape[0]


def pack(start, own_ref, other_ref, sources):
    own, width = lax.axis_index("zl"), own_ref.shape[2]
    for which, ref in enumerate((own_ref, other_ref)):
        for i, source in enumerate(sources):
            seqs = source.shape[1]
            ref[i * seqs : (i + 1) * seqs] = source[own ^ which, :, :, start : start + width]


def gather_kernel(keep, z1, z2, *refs):
    near, joint, own_ref, other_ref = refs[-4:]
    fill(near, keep, z1, z2)
    pack(0, own_ref, other_ref, refs[:-4])
    at = 0
    for s in range(z2.shape[0]):
        joint[at : at + z2.shape[1], :] = z2[s]
        at += z2.shape[1]
    count, length, width = other_ref.shape
    for i in range(count):
        for start in range(0, width, 128):
            joint[at : at + length, :] = other_ref[i, :, start : start + 128]
            at += length


def second_kernel(starts, near, joint, *refs):
    count = 3 + 2 * len(starts)
    sources, (own_rows, far, cols, *outs) = refs[:-count], refs[-count:]
    at = 0
    for s in range(far.shape[0]):
        far[s] = joint[at : at + far.shape[1], :]
        at += far.shape[1]
    fill(own_rows, near, far)
    count, length, width = cols.shape
    for i in range(count):
        for start in range(0, width, 128):
            cols[i, :, start : start + 128] = joint[at : at + length, :]
            at += length
    for k, start in enumerate(starts):
        pack(start, outs[2 * k], outs[2 * k + 1], sources)


def third_kernel(first, second, out):
    fill(out, first, second)


def code_kernel(*refs):
    for at, ref in enumerate(refs[:-1]):
        refs[-1][at] = ref[...]


def fisher_kernel(places, row_count, scale, code_scale, *refs):
    rows, cols, outs, total = refs[:row_count], refs[row_count:-5], refs[-5:-1], refs[-1]
    span = outs[0].shape[0]
    own_zl, own_y = lax.axis_index("zl"), lax.axis_index("y")

    for group in range(4):
        part = slice(group * span, (group + 1) * span)
        acc = None
        for row_at, row_sub, col_at, col_sub in places:
            g = jnp.dot(rows[row_at][row_sub, part, :], cols[col_at][col_sub], preferred_element_type=jnp.float32)
            acc = g * g if acc is None else acc + g * g
        damped = acc * scale + damping
        code = jnp.round((jnp.log(damped) - math.log(damping)) * code_scale) - 32768.0
        total[part, :] = jnp.clip(code, -32768.0, 32767.0)
    for at, ref in enumerate(outs):
        group = (own_zl ^ (at // 2)) * 2 + (own_y ^ (at % 2))
        start = pl.multiple_of(group * span, span)
        ref[...] = total[pl.ds(start, span), :].astype(jnp.int32).astype(jnp.int16)


def merge_chunk(models, tile_width, first, width, code_scale, weights, codes, store):
    own_zl, own_y, own_m = lax.axis_index("zl"), lax.axis_index("y"), lax.axis_index("mp")

    def pick(values, j):
        chosen = values[0]
        for offset in range(1, models):
            chosen = jnp.where(lax.rem(own_m + models - offset, models) == j, values[offset], chosen)
        return chosen

    for at in range(4):
        sub = (own_zl ^ (at // 2)) * 2 + (own_y ^ (at % 2))
        start = pl.multiple_of(sub * tile_width + first, 128)
        codes_here = [code[at].astype(jnp.int32) for code in codes]
        weights_here = [weight[:, pl.ds(start, width)] for weight in weights]
        base = pick(codes_here, 0)
        num, den = pick(weights_here, 0), None
        for j in range(1, models):
            ratio = jnp.exp((pick(codes_here, j) - base).astype(jnp.float32) * (1.0 / code_scale))
            num = num + ratio * pick(weights_here, j)
            den = 1.0 + ratio if den is None else den + ratio
        store(at, start, num if den is None else num / den)


def early_merge_kernel(models, tile_width, first, width, code_scale, *refs):
    def store(at, start, value):
        refs[-1][at] = value

    weights, codes = refs[:models], refs[models:-1]
    merge_chunk(models, tile_width, first, width, code_scale, weights, codes, store)


def last_merge_kernel(models, tile_width, firsts, width, code_scale, *refs):
    weights, codes, early, out = refs[:models], refs[models : 2 * models], refs[2 * models : -1], refs[-1]
    own_zl, own_y = lax.axis_index("zl"), lax.axis_index("y")
    for first, ref in zip(firsts, early):
        for at in range(4):
            sub = (own_zl ^ (at // 2)) * 2 + (own_y ^ (at % 2))
            start = pl.multiple_of(sub * tile_width + first, 128)
            out[:, pl.ds(start, ref.shape[2])] = ref[at]

    def store(at, start, value):
        out[:, pl.ds(start, width)] = value

    merge_chunk(models, tile_width, firsts[-1], width, code_scale, weights, codes, store)


def shards(inputs, cotangent, token_ids, weights):
    models = lax.axis_size("mp")
    core_count = lax.axis_size("c")
    inputs, cotangent, token_ids, weights = inputs[0], cotangent[0], token_ids[0], weights[0, 0]
    seqs, length, feature_width = inputs.shape
    query_width = cotangent.shape[2]
    bf = jnp.bfloat16
    half = feature_width // 2
    tile_width = query_width // (4 * core_count)
    span = half // 4
    total_seqs = seqs * 8 * core_count
    widths = [int(tile_width * part) for part in CHUNKS]
    if any(width % 128 for width in widths):
        widths = [tile_width]
    peak = LARGEST**4 * length + damping
    code_scale = 65535.0 / (math.log(peak) - math.log(damping))

    other_weights = [rotate(weights, "mp", offset) for offset in range(1, models)]

    col_shape = jax.ShapeDtypeStruct((2, seqs, length, tile_width), bf)
    row_shape = jax.ShapeDtypeStruct((seqs, half, length), bf)
    keep, send, *col_parts = call(front_kernel, (row_shape,) * 2 + (col_shape,) * (2 * core_count))(
        inputs, token_ids, cotangent
    )

    got = []
    for at, part in enumerate(col_parts):
        dy, dc = at // core_count, at % core_count
        if dy and dc:
            size = 2 * core_count
            perm = []
            for i in range(size):
                y, c = i // core_count, i % core_count
                perm.append((i, (y ^ 1) * core_count + (c + dc) % core_count))
            part = lax.ppermute(part, ("y", "c"), perm)
        elif dy:
            part = swap(part, "y")
        elif dc:
            part = rotate(part, "c", dc)
        got.append(part)

    starts = [sum(widths[:k]) for k in range(len(widths))]

    def several(count, width):
        return jax.ShapeDtypeStruct((seqs * count, length, width), bf)

    def many_rows(count):
        return jax.ShapeDtypeStruct((seqs * count, half, length), bf)

    z2 = swap(send, "zh")
    z1 = swap(keep, "zl")
    packs = [None] * len(widths)
    pieces = seqs * (half + 2 * core_count * length * (widths[0] // 128))
    near, joint, own, other = call(
        gather_kernel,
        (many_rows(3), jax.ShapeDtypeStruct((pieces, length), bf)) + (several(2 * core_count, widths[0]),) * 2,
    )(keep, z1, z2, *got)
    packs[0] = [own, other]
    pack_shapes = [several(2 * core_count, width) for width in widths[1:] for _ in range(2)]
    own_rows, far, near_cols, *others = call(
        functools.partial(second_kernel, starts[1:]),
        (many_rows(4), many_rows(1), several(2 * core_count, widths[0])) + tuple(pack_shapes),
    )(near, swap(joint, "zl"), *got)
    for k in range(1, len(widths)):
        packs[k] = others[2 * k - 2 : 2 * k]
    first_cols = [packs[0][0], near_cols, swap(packs[0][0], "zh"), swap(packs[0][1], ("zh", "zl"))]
    y_rows = call(third_kernel, many_rows(4))(swap(near, "y"), swap(far, "y"), after=first_cols[2:])
    rows = []
    for dc in range(core_count):
        rows += [own_rows, y_rows] if dc == 0 else [rotate(own_rows, "c", dc), rotate(y_rows, "c", dc)]
    places = []
    for dz in range(4):
        for dy in range(2):
            for dc in range(core_count):
                for s in range(seqs):
                    places.append((dc * 2 + dy, dz * seqs + s, dz, (dy * core_count + dc) * seqs + s))

    merged = []
    for k, width in enumerate(widths):
        own, other = packs[k]
        cols = [own, swap(other, "zl"), swap(own, "zh"), swap(other, ("zh", "zl"))] if k else first_cols
        code_shape = jax.ShapeDtypeStruct((span, width), jnp.int16)
        outs = call(
            functools.partial(fisher_kernel, places, len(rows), 1.0 / (length * total_seqs), code_scale),
            (code_shape,) * 4,
            [pltpu.VMEM((half, width), jnp.float32)],
            flops=2 * half * width * length * total_seqs,
            bytes_accessed=2 * length * total_seqs * (half + width),
        )(*rows, *cols)
        codes = call(code_kernel, jax.ShapeDtypeStruct((4, span, width), jnp.int16))(
            outs[0],
            swap(outs[1], "y"),
            swap(outs[2], "zl"),
            swap(outs[3], ("zl", "y")),
            after=() if k else other_weights,
        )
        all_codes = [codes] + [rotate(codes, "mp", offset) for offset in range(1, models)]
        if k < len(widths) - 1:
            merged.append(
                call(
                    functools.partial(early_merge_kernel, models, tile_width, starts[k], width, code_scale),
                    jax.ShapeDtypeStruct((4, span, width), jnp.float32),
                )(weights, *other_weights, *all_codes)
            )
        else:
            result = call(
                functools.partial(last_merge_kernel, models, tile_width, starts, width, code_scale),
                jax.ShapeDtypeStruct(weights.shape, jnp.float32),
            )(weights, *other_weights, *all_codes, *merged)
    return result[None]


def solution(mesh):
    models, devices = mesh.shape["mp"], mesh.shape["tok"]
    grid = Mesh(mesh.devices.reshape(models, 2, 2, ROW_BLOCKS // 4, devices // ROW_BLOCKS), ("mp",) + TOK)
    in_specs = (
        P("mp", TOK, None, None),
        P("mp", TOK, None, None),
        P("mp", TOK, None),
        P("mp", TOK, None, None),
    )
    return jax.shard_map(shards, mesh=grid, in_specs=in_specs, out_specs=P(TOK, None, None), check_vma=False)
```

time: 126 us -> 116 us (0.921)
  starting transfers between devices: 42.5 us -> 36.1 us
  waiting for transfers between devices: 69.2 us -> 64.4 us
  Pallas kernels: 10.2 us -> 11.7 us
  local copies, waits for them, and re-layouts: 4.26 us -> 2.93 us
    ppermute x18 -> x6, starting transfers between devices: 9.76 us -> 4.57 us  [rotate(): lax.ppermute(value, axis, [(i, (i + offset) % size) for i in range(size)])]
    ppermute x16 -> x13, waiting for transfers between devices: 51.3 us -> 46.8 us  [swap(): return lax.ppermute(value, axes, [(0, 1), (1, 0)])]
    ppermute x1, waiting for transfers between devices: 4.7 us -> 0.37 us  [shards(): part = lax.ppermute(part, ('y', 'c'), perm)]
    ppermute x4, waiting for transfers between devices: 0.01 us -> 2.5 us  [swap(): return lax.ppermute(value, axes, [(i, i ^ 3) for i in range(4)])]
    ppermute x18 -> x6, waiting for transfers between devices: 13.1 us -> 14.8 us  [rotate(): lax.ppermute(value, axis, [(i, (i + offset) % size) for i in range(size)])]
    pallas_call x6 -> x10, Pallas kernels: 10.2 us -> 11.7 us  [run(): pl.pallas_call(kernel, out_shape=out_shape, in_specs=[VMEM] * len(args) +...]
    unnamed x10, local copies, waits for them, and re-layouts: 4.26 us -> 2.93 us
    ppermute x4, starting transfers between devices: 15.3 us -> 14 us  [swap(): return lax.ppermute(value, axes, [(i, i ^ 3) for i in range(4)])]
  transfers between devices with their start and end apart: 39 -> 24, of which waited for: 17 -> 12; matrix products, arithmetic and copies ran while one was open for 0% -> 0% of each run, Pallas kernels for 4% -> 7%
where the time goes in v2:
time: 116 us; the launch traced here: 115 us
  waiting for transfers between devices  64.4 us (56%)
  starting transfers between devices  36.1 us (31%)
  Pallas kernels  11.7 us (10%)
  local copies, waits for them, and re-layouts  2.93 us (3%)
    ppermute x13, waiting for transfers between devices, swap(): return lax.ppermute(value, axes, [(0, 1), (1, 0)])  46.8 us
    ppermute x13, starting transfers between devices, swap(): return lax.ppermute(value, axes, [(0, 1), (1, 0)])  17.3 us
    ppermute x6, waiting for transfers between devices, rotate(): lax.ppermute(value, axis, [(i, (i + offset) % size) for i in range(size)])  14.8 us
    ppermute x4, starting transfers between devices, swap(): return lax.ppermute(value, axes, [(i, i ^ 3) for i in range(4)])  14 us
    pallas_call x10, Pallas kernels, run(): pl.pallas_call(kernel, out_shape=out_shape, in_specs=[VMEM] * len(args) +...  11.7 us
    ppermute x6, starting transfers between devices, rotate(): lax.ppermute(value, axis, [(i, (i + offset) % size) for i in range(size)])  4.57 us
    unnamed x10, local copies, waits for them, and re-layouts  2.93 us
    ppermute x4, waiting for transfers between devices, swap(): return lax.ppermute(value, axes, [(i, i ^ 3) for i in range(4)])  2.5 us
  transfers between devices with their start and end apart: 24, of which 12 were waited for; matrix products, arithmetic and copies ran while one was open for 0% of the time, Pallas kernels for 7%

profile of v2, /device:TPU:0, one launch (start us, length us, event | category | flops | bytes accessed | tf_op | source)
XLA Modules:
  0.0 115.3 jit_solution(1481676121280591074)
XLA Ops:
  0.0 1.2 %copy-done.2 = bf16[1,1,128,4096]{3,2,1,0:T(8,128)(2,1)S(1)} copy-done((bf16[1,1,128,4096]{3,2,1,0:T(8,128)(2,1)S(1)}, bf16[1,1,128,4096]{3,2,1,0:T(8,128)(2,1)}, u32[]{:S(2)}) %copy-start.2) | copy-done | bytes 1048600
  1.2 1.0 copy-done.3
  2.3 0.7 copy-done.4
  2.9 0.3 shard_map.46
  3.3 4.1 %collective-permute-start.2 = (bf16[1,1024,128]{2,1,0:T(8,128)(2,1)S(1)}, bf16[1,1024,128]{2,1,0:T(8,128)(2,1)S(1)}, u32[]{:S(2)}, u32[]{:S(2)}) collective-permute-start(bf16[1,1024,128]{2,1,0:T(8,128)(2,1)S(1)} %get-tuple-element.29), channel_id=1, source_target_pairs={{0,8},{8,0},{1,9},{9,1},{2,10},{10,2},{3,11},{11,3},{4,12},{12,4},... | collective-permute-start | bytes 786440 | tf_op jit(solution)/shard_map/ppermute | solution.py:27
  7.4 1.5 %collective-permute-start.4 = (bf16[2,1,128,512]{3,2,1,0:T(8,128)(2,1)S(1)}, bf16[2,1,128,512]{3,2,1,0:T(8,128)(2,1)S(1)}, u32[]{:S(2)}, u32[]{:S(2)}) collective-permute-start(bf16[2,1,128,512]{3,2,1,0:T(8,128)(2,1)S(1)} %get-tuple-element.32), channel_id=1, source_target_pairs={{0,2},{2,0},{1,3},{3,1},{4,6},{6,4},{5,7},{7,5},{8,10},{10,8},{9,1... | collective-permute-start | bytes 786440 | tf_op jit(solution)/shard_map/ppermute | solution.py:27
  8.9 0.3 collective-permute-start.5
  9.2 1.6 %collective-permute-start.1 = (bf16[1,1024,128]{2,1,0:T(8,128)(2,1)S(1)}, bf16[1,1024,128]{2,1,0:T(8,128)(2,1)S(1)}, u32[]{:S(2)}, u32[]{:S(2)}) collective-permute-start(bf16[1,1024,128]{2,1,0:T(8,128)(2,1)S(1)} %get-tuple-element.28.refs_0_), channel_id=1, source_target_pairs={{0,4},{4,0},{1,5},{5,1},{2,6},{6,2},{3,7},{7,3},{8,12},{12,8},{9,1... | collective-permute-start | bytes 786440 | tf_op jit(solution)/shard_map/ppermute | solution.py:27
  10.8 8.6 %collective-permute-done.2.refs_2_ = bf16[1,1024,128]{2,1,0:T(8,128)(2,1)S(1)} collective-permute-done((bf16[1,1024,128]{2,1,0:T(8,128)(2,1)S(1)}, bf16[1,1024,128]{2,1,0:T(8,128)(2,1)S(1)}, u32[]{:S(2)}, u32[]{:S(2)}) %collective-permute-start.2) | collective-permute-done | bytes 262176 | tf_op jit(solution)/shard_map/ppermute | solution.py:27
  19.4 1.5 %collective-permute-start = (f32[256,2048]{1,0:T(8,128)}, f32[256,2048]{1,0:T(8,128)S(1)}, u32[]{:S(2)}, u32[]{:S(2)}) collective-permute-start(f32[256,2048]{1,0:T(8,128)} %bitcast.5), channel_id=1, source_target_pairs={{0,16},{16,0},{1,17},{17,1},{2,18},{18,2},{3,19},{19,3},{4,20},{20... | collective-permute-start | bytes 6291464 | tf_op jit(solution)/shard_map/ppermute | solution.py:33
  20.9 0.0 collective-permute-done.3.refs_4_.refs_3_
  20.9 0.0 collective-permute-done.4.refs_5_.refs_4_
  20.9 0.4 collective-permute-done.5.refs_6_.refs_5_
  21.3 0.9 collective-permute-done.1.refs_1_
  22.2 0.1 shard_map.47
  22.3 0.8 collective-permute-start.6
  23.1 1.5 %collective-permute-start.7 = (bf16[3,1024,128]{2,1,0:T(8,128)(2,1)S(1)}, bf16[3,1024,128]{2,1,0:T(8,128)(2,1)S(1)}, u32[]{:S(2)}, u32[]{:S(2)}) collective-permute-start(bf16[3,1024,128]{2,1,0:T(8,128)(2,1)S(1)} %get-tuple-element.34.refs_0_), channel_id=1, source_target_pairs={{0,2},{2,0},{1,3},{3,1},{4,6},{6,4},{5,7},{7,5},{8,10},{10,8},{9,1... | collective-permute-start | bytes 2359304 | tf_op jit(solution)/shard_map/ppermute | solution.py:27
  24.6 1.8 %collective-permute-start.10 = (bf16[4,128,256]{2,1,0:T(8,128)(2,1)S(1)}, bf16[4,128,256]{2,1,0:T(8,128)(2,1)S(1)}, u32[]{:S(2)}, u32[]{:S(2)}) collective-permute-start(bf16[4,128,256]{2,1,0:T(8,128)(2,1)S(1)} %get-tuple-element.39), channel_id=1, source_target_pairs={{0,12},{4,8},{8,4},{12,0},{1,13},{5,9},{9,5},{13,1},{2,14},{6,10},... | collective-permute-start | bytes 786440 | tf_op jit(solution)/shard_map/ppermute | solution.py:28
  26.4 1.0 collective-permute-start.9
  27.5 17.8 %collective-permute-done.6.refs_1_ = bf16[2048,128]{1,0:T(8,128)(2,1)S(1)} collective-permute-done((bf16[2048,128]{1,0:T(8,128)(2,1)S(1)}, bf16[2048,128]{1,0:T(8,128)(2,1)S(1)}, u32[]{:S(2)}, u32[]{:S(2)}) %collective-permute-start.6) | collective-permute-done | bytes 524320 | tf_op jit(solution)/shard_map/ppermute | solution.py:27
  45.2 0.2 shard_map.48
  45.4 2.7 %collective-permute-start.8 = (bf16[1,1024,128]{2,1,0:T(8,128)(2,1)S(1)}, bf16[1,1024,128]{2,1,0:T(8,128)(2,1)S(1)}, u32[]{:S(2)}, u32[]{:S(2)}) collective-permute-start(bf16[1,1024,128]{2,1,0:T(8,128)(2,1)S(1)} %get-tuple-element.37), channel_id=1, source_target_pairs={{0,2},{2,0},{1,3},{3,1},{4,6},{6,4},{5,7},{7,5},{8,10},{10,8},{9,1... | collective-permute-start | bytes 786440 | tf_op jit(solution)/shard_map/ppermute | solution.py:27
  48.1 1.5 %collective-permute-done.9.refs_2_.refs_6_ = bf16[4,128,256]{2,1,0:T(8,128)(2,1)S(1)} collective-permute-done((bf16[4,128,256]{2,1,0:T(8,128)(2,1)S(1)}, bf16[4,128,256]{2,1,0:T(8,128)(2,1)S(1)}, u32[]{:S(2)}, u32[]{:S(2)}) %collective-permute-start.9) | collective-permute-done | bytes 262176 | tf_op jit(solution)/shard_map/ppermute | solution.py:27
  49.6 3.7 %collective-permute-done.8.refs_1_ = bf16[1,1024,128]{2,1,0:T(8,128)(2,1)S(1)} collective-permute-done((bf16[1,1024,128]{2,1,0:T(8,128)(2,1)S(1)}, bf16[1,1024,128]{2,1,0:T(8,128)(2,1)S(1)}, u32[]{:S(2)}, u32[]{:S(2)}) %collective-permute-start.8) | collective-permute-done | bytes 262176 | tf_op jit(solution)/shard_map/ppermute | solution.py:27
  53.2 0.1 shard_map.49.refs_1_
  53.3 0.1 collective-permute-start.12
  53.4 0.6 collective-permute-start.14
  54.0 2.0 %collective-permute-start.15 = (bf16[4,128,256]{2,1,0:T(8,128)(2,1)S(1)}, bf16[4,128,256]{2,1,0:T(8,128)(2,1)S(1)}, u32[]{:S(2)}, u32[]{:S(2)}) collective-permute-start(bf16[4,128,256]{2,1,0:T(8,128)(2,1)S(1)} %get-tuple-element.41), channel_id=1, source_target_pairs={{0,12},{4,8},{8,4},{12,0},{1,13},{5,9},{9,5},{13,1},{2,14},{6,10},... | collective-permute-start | bytes 786440 | tf_op jit(solution)/shard_map/ppermute | solution.py:28
  56.0 1.0 collective-permute-start.13
  56.9 0.0 collective-permute-done.12.refs_3_
  56.9 2.6 %shard_map.52 = (s16[256,256]{1,0:T(8,128)(2,1)S(1)}, s16[256,256]{1,0:T(8,128)(2,1)S(1)}, s16[256,256]{1,0:T(8,128)(2,1)S(1)}, s16[256,256]{1,0:T(8,128)(2,1)S(1)}) custom-call(bf16[4,1024,128]{2,1,0:T(8,128)(2,1)S(1)} %get-tuple-element.36.refs_0_, bf16[4,1024,128]{2,1,0:T(8,128)(2,1)S(1)} %shard_map.49.refs_1_, ...), custom_call_target="tpu_custom_call" | custom-call | flops 1073741824 | bytes 5242880 | tf_op jit(solution)/shard_map/pallas_call | solution.py:41
  59.5 1.8 %collective-permute-start.20 = (s16[256,256]{1,0:T(8,128)(2,1)S(1)}, s16[256,256]{1,0:T(8,128)(2,1)S(1)}, u32[]{:S(2)}, u32[]{:S(2)}) collective-permute-start(s16[256,256]{1,0:T(8,128)(2,1)S(1)} %get-tuple-element.48), channel_id=1, source_target_pairs={{0,2},{2,0},{1,3},{3,1},{4,6},{6,4},{5,7},{7,5},{8,10},{10,8},{9,1... | collective-permute-start | bytes 393224 | tf_op jit(solution)/shard_map/ppermute | solution.py:27
  61.4 12.8 %collective-permute-done.14.refs_6_ = bf16[4,128,256]{2,1,0:T(8,128)(2,1)S(1)} collective-permute-done((bf16[4,128,256]{2,1,0:T(8,128)(2,1)S(1)}, bf16[4,128,256]{2,1,0:T(8,128)(2,1)S(1)}, u32[]{:S(2)}, u32[]{:S(2)}) %collective-permute-start.14) | collective-permute-done | bytes 262176 | tf_op jit(solution)/shard_map/ppermute | solution.py:27
  74.1 0.0 collective-permute-start.21
  74.1 7.3 %collective-permute-start.22 = (s16[256,256]{1,0:T(8,128)(2,1)S(1)}, s16[256,256]{1,0:T(8,128)(2,1)S(1)}, u32[]{:S(2)}, u32[]{:S(2)}) collective-permute-start(s16[256,256]{1,0:T(8,128)(2,1)S(1)} %get-tuple-element.50), channel_id=1, source_target_pairs={{0,6},{2,4},{4,2},{6,0},{1,7},{3,5},{5,3},{7,1},{8,14},{10,12},{12... | collective-permute-start | bytes 393224 | tf_op jit(solution)/shard_map/ppermute | solution.py:28
  81.4 2.6 %shard_map.50 = (s16[256,256]{1,0:T(8,128)(2,1)S(1)}, s16[256,256]{1,0:T(8,128)(2,1)S(1)}, s16[256,256]{1,0:T(8,128)(2,1)S(1)}, s16[256,256]{1,0:T(8,128)(2,1)S(1)}) custom-call(bf16[4,1024,128]{2,1,0:T(8,128)(2,1)S(1)} %get-tuple-element.36.refs_0_, bf16[4,1024,128]{2,1,0:T(8,128)(2,1)S(1)} %shard_map.49.refs_1_, ...), custom_call_target="tpu_custom_call" | custom-call | flops 1073741824 | bytes 5242880 | tf_op jit(solution)/shard_map/pallas_call | solution.py:41
  84.0 0.4 collective-permute-start.16
  84.4 0.3 collective-permute-start.17
  84.7 2.9 %collective-permute-start.18 = (s16[256,256]{1,0:T(8,128)(2,1)S(1)}, s16[256,256]{1,0:T(8,128)(2,1)S(1)}, u32[]{:S(2)}, u32[]{:S(2)}) collective-permute-start(s16[256,256]{1,0:T(8,128)(2,1)S(1)} %get-tuple-element.45), channel_id=1, source_target_pairs={{0,6},{2,4},{4,2},{6,0},{1,7},{3,5},{5,3},{7,1},{8,14},{10,12},{12... | collective-permute-start | bytes 393224 | tf_op jit(solution)/shard_map/ppermute | solution.py:28
  87.7 1.5 %collective-permute-start.23 = (s16[4,256,256]{2,1,0:T(8,128)(2,1)S(1)}, s16[4,256,256]{2,1,0:T(8,128)(2,1)S(1)}, u32[]{:S(2)}, u32[]{:S(2)}) collective-permute-start(s16[4,256,256]{2,1,0:T(8,128)(2,1)S(1)} %shard_map.53.refs_2_), channel_id=1, source_target_pairs={{0,16},{16,0},{1,17},{17,1},{2,18},{18,2},{3,19},{19,3},{4,20},{20... | collective-permute-start | bytes 1572872 | tf_op jit(solution)/shard_map/ppermute | solution.py:33
  89.1 0.5 collective-permute-done.16.refs_1_
  89.6 1.2 %collective-permute-done.17.refs_2_ = s16[256,256]{1,0:T(8,128)(2,1)S(1)} collective-permute-done((s16[256,256]{1,0:T(8,128)(2,1)S(1)}, s16[256,256]{1,0:T(8,128)(2,1)S(1)}, u32[]{:S(2)}, u32[]{:S(2)}) %collective-permute-start.17) | collective-permute-done | bytes 131104 | tf_op jit(solution)/shard_map/ppermute | solution.py:27
  90.8 2.5 %collective-permute-done.18.refs_3_ = s16[256,256]{1,0:T(8,128)(2,1)S(1)} collective-permute-done((s16[256,256]{1,0:T(8,128)(2,1)S(1)}, s16[256,256]{1,0:T(8,128)(2,1)S(1)}, u32[]{:S(2)}, u32[]{:S(2)}) %collective-permute-start.18) | collective-permute-done | bytes 131104 | tf_op jit(solution)/shard_map/ppermute | solution.py:28
  93.3 1.5 %collective-permute-start.19 = (s16[4,256,256]{2,1,0:T(8,128)(2,1)S(1)}, s16[4,256,256]{2,1,0:T(8,128)(2,1)S(1)}, u32[]{:S(2)}, u32[]{:S(2)}) collective-permute-start(s16[4,256,256]{2,1,0:T(8,128)(2,1)S(1)} %shard_map.51.refs_2_), channel_id=1, source_target_pairs={{0,16},{16,0},{1,17},{17,1},{2,18},{18,2},{3,19},{19,3},{4,20},{20... | collective-permute-start | bytes 1572872 | tf_op jit(solution)/shard_map/ppermute | solution.py:33
  94.8 7.8 %collective-permute-done.23.refs_3_ = s16[4,256,256]{2,1,0:T(8,128)(2,1)S(1)} collective-permute-done((s16[4,256,256]{2,1,0:T(8,128)(2,1)S(1)}, s16[4,256,256]{2,1,0:T(8,128)(2,1)S(1)}, u32[]{:S(2)}, u32[]{:S(2)}) %collective-permute-start.23) | collective-permute-done | bytes 524320 | tf_op jit(solution)/shard_map/ppermute | solution.py:33
  102.6 2.2 %shard_map.54.refs_4_ = f32[4,256,256]{2,1,0:T(8,128)S(1)} custom-call(f32[256,2048]{1,0:T(8,128)S(1)} %bitcast.6, f32[256,2048]{1,0:T(8,128)} %copy-done, s16[4,256,256]{2,1,0:T(8,128)(2,1)S(1)} %shard_map.53.refs_2_, s16[4,256,256]{2,1,0:T(8,128)(2,1)S(1)} %collective-permute-done.23.refs_3_), custom_call_target="tpu_custom_call" | custom-call | tf_op jit(solution)/shard_map/pallas_call | solution.py:41
  104.7 7.0 %collective-permute-done.19.refs_3_ = s16[4,256,256]{2,1,0:T(8,128)(2,1)S(1)} collective-permute-done((s16[4,256,256]{2,1,0:T(8,128)(2,1)S(1)}, s16[4,256,256]{2,1,0:T(8,128)(2,1)S(1)}, u32[]{:S(2)}, u32[]{:S(2)}) %collective-permute-start.19) | collective-permute-done | bytes 524320 | tf_op jit(solution)/shard_map/ppermute | solution.py:33
  111.7 3.5 %shard_map.55 = f32[256,2048]{1,0:T(8,128)} custom-call(f32[256,2048]{1,0:T(8,128)S(1)} %bitcast.7, f32[256,2048]{1,0:T(8,128)} %copy-done, s16[4,256,256]{2,1,0:T(8,128)(2,1)S(1)} %shard_map.51.refs_2_, s16[4,256,256]{2,1,0:T(8,128)(2,1)S(1)} %collective-permute-done.19.refs_3_, f32[4,256,256]{2,1,0:T(8,128)S(1)} %shard_map.54.refs_4_), custom_call_target="tpu_custom_call" | custom-call | tf_op jit(solution)/shard_map/pallas_call | solution.py:41
  (20 shorter events, 0.1 us)
Async XLA Ops:
  0.0 1.2 %copy-start.2 = (bf16[1,1,128,4096]{3,2,1,0:T(8,128)(2,1)S(1)}, bf16[1,1,128,4096]{3,2,1,0:T(8,128)(2,1)}, u32[]{:S(2)}) copy-start(bf16[1,1,128,4096]{3,2,1,0:T(8,128)(2,1)} %param.5) | copy-start | bytes 3145732
  1.2 1.0 copy-start.3
  2.3 0.7 copy-start.4
  3.3 16.1 %collective-permute-start.2 = (bf16[1,1024,128]{2,1,0:T(8,128)(2,1)S(1)}, bf16[1,1024,128]{2,1,0:T(8,128)(2,1)S(1)}, u32[]{:S(2)}, u32[]{:S(2)}) collective-permute-start(bf16[1,1024,128]{2,1,0:T(8,128)(2,1)S(1)} %get-tuple-element.29), channel_id=1, source_target_pairs={{0,8},{8,0},{1,9},{9,1},{2,10},{10,2},{3,11},{11,3},{4,12},{12,4},... | collective-permute-start | bytes 786440 | tf_op jit(solution)/shard_map/ppermute | solution.py:27
  7.4 13.6 %collective-permute-start.3 = (bf16[2,1,128,512]{3,2,1,0:T(8,128)(2,1)S(1)}, bf16[2,1,128,512]{3,2,1,0:T(8,128)(2,1)S(1)}, u32[]{:S(2)}, u32[]{:S(2)}) collective-permute-start(bf16[2,1,128,512]{3,2,1,0:T(8,128)(2,1)S(1)} %get-tuple-element.31), channel_id=1, source_target_pairs={{0,1},{1,0},{2,3},{3,2},{4,5},{5,4},{6,7},{7,6},{8,9},{9,8},{10,11... | collective-permute-start | bytes 786440 | tf_op jit(solution)/shard_map/ppermute | solution.py:33
  7.4 13.6 %collective-permute-start.4 = (bf16[2,1,128,512]{3,2,1,0:T(8,128)(2,1)S(1)}, bf16[2,1,128,512]{3,2,1,0:T(8,128)(2,1)S(1)}, u32[]{:S(2)}, u32[]{:S(2)}) collective-permute-start(bf16[2,1,128,512]{3,2,1,0:T(8,128)(2,1)S(1)} %get-tuple-element.32), channel_id=1, source_target_pairs={{0,2},{2,0},{1,3},{3,1},{4,6},{6,4},{5,7},{7,5},{8,10},{10,8},{9,1... | collective-permute-start | bytes 786440 | tf_op jit(solution)/shard_map/ppermute | solution.py:27
  8.9 12.4 %collective-permute-start.5 = (bf16[2,1,128,512]{3,2,1,0:T(8,128)(2,1)S(1)}, bf16[2,1,128,512]{3,2,1,0:T(8,128)(2,1)S(1)}, u32[]{:S(2)}, u32[]{:S(2)}) collective-permute-start(bf16[2,1,128,512]{3,2,1,0:T(8,128)(2,1)S(1)} %get-tuple-element.33), channel_id=1, source_target_pairs={{0,3},{1,2},{2,1},{3,0},{4,7},{5,6},{6,5},{7,4},{8,11},{9,10},{10,... | collective-permute-start | bytes 786440 | tf_op jit(solution)/shard_map/ppermute | solution.py:232
  9.2 12.9 %collective-permute-start.1 = (bf16[1,1024,128]{2,1,0:T(8,128)(2,1)S(1)}, bf16[1,1024,128]{2,1,0:T(8,128)(2,1)S(1)}, u32[]{:S(2)}, u32[]{:S(2)}) collective-permute-start(bf16[1,1024,128]{2,1,0:T(8,128)(2,1)S(1)} %get-tuple-element.28.refs_0_), channel_id=1, source_target_pairs={{0,4},{4,0},{1,5},{5,1},{2,6},{6,2},{3,7},{7,3},{8,12},{12,8},{9,1... | collective-permute-start | bytes 786440 | tf_op jit(solution)/shard_map/ppermute | solution.py:27
  19.4 65.0 %collective-permute-start = (f32[256,2048]{1,0:T(8,128)}, f32[256,2048]{1,0:T(8,128)S(1)}, u32[]{:S(2)}, u32[]{:S(2)}) collective-permute-start(f32[256,2048]{1,0:T(8,128)} %bitcast.5), channel_id=1, source_target_pairs={{0,16},{16,0},{1,17},{17,1},{2,18},{18,2},{3,19},{19,3},{4,20},{20... | collective-permute-start | bytes 6291464 | tf_op jit(solution)/shard_map/ppermute | solution.py:33
  22.3 22.9 %collective-permute-start.6 = (bf16[2048,128]{1,0:T(8,128)(2,1)S(1)}, bf16[2048,128]{1,0:T(8,128)(2,1)S(1)}, u32[]{:S(2)}, u32[]{:S(2)}) collective-permute-start(bf16[2048,128]{1,0:T(8,128)(2,1)S(1)} %get-tuple-element.35), channel_id=1, source_target_pairs={{0,4},{4,0},{1,5},{5,1},{2,6},{6,2},{3,7},{7,3},{8,12},{12,8},{9,1... | collective-permute-start | bytes 1572872 | tf_op jit(solution)/shard_map/ppermute | solution.py:27
  23.1 30.1 %collective-permute-start.7 = (bf16[3,1024,128]{2,1,0:T(8,128)(2,1)S(1)}, bf16[3,1024,128]{2,1,0:T(8,128)(2,1)S(1)}, u32[]{:S(2)}, u32[]{:S(2)}) collective-permute-start(bf16[3,1024,128]{2,1,0:T(8,128)(2,1)S(1)} %get-tuple-element.34.refs_0_), channel_id=1, source_target_pairs={{0,2},{2,0},{1,3},{3,1},{4,6},{6,4},{5,7},{7,5},{8,10},{10,8},{9,1... | collective-permute-start | bytes 2359304 | tf_op jit(solution)/shard_map/ppermute | solution.py:27
  24.6 23.4 %collective-permute-start.10 = (bf16[4,128,256]{2,1,0:T(8,128)(2,1)S(1)}, bf16[4,128,256]{2,1,0:T(8,128)(2,1)S(1)}, u32[]{:S(2)}, u32[]{:S(2)}) collective-permute-start(bf16[4,128,256]{2,1,0:T(8,128)(2,1)S(1)} %get-tuple-element.39), channel_id=1, source_target_pairs={{0,12},{4,8},{8,4},{12,0},{1,13},{5,9},{9,5},{13,1},{2,14},{6,10},... | collective-permute-start | bytes 786440 | tf_op jit(solution)/shard_map/ppermute | solution.py:28
  26.4 23.2 %collective-permute-start.9 = (bf16[4,128,256]{2,1,0:T(8,128)(2,1)S(1)}, bf16[4,128,256]{2,1,0:T(8,128)(2,1)S(1)}, u32[]{:S(2)}, u32[]{:S(2)}) collective-permute-start(bf16[4,128,256]{2,1,0:T(8,128)(2,1)S(1)} %get-tuple-element.38.refs_4_), channel_id=1, source_target_pairs={{0,8},{8,0},{1,9},{9,1},{2,10},{10,2},{3,11},{11,3},{4,12},{12,4},... | collective-permute-start | bytes 786440 | tf_op jit(solution)/shard_map/ppermute | solution.py:27
  45.4 7.9 %collective-permute-start.8 = (bf16[1,1024,128]{2,1,0:T(8,128)(2,1)S(1)}, bf16[1,1024,128]{2,1,0:T(8,128)(2,1)S(1)}, u32[]{:S(2)}, u32[]{:S(2)}) collective-permute-start(bf16[1,1024,128]{2,1,0:T(8,128)(2,1)S(1)} %get-tuple-element.37), channel_id=1, source_target_pairs={{0,2},{2,0},{1,3},{3,1},{4,6},{6,4},{5,7},{7,5},{8,10},{10,8},{9,1... | collective-permute-start | bytes 786440 | tf_op jit(solution)/shard_map/ppermute | solution.py:27
  48.1 7.9 %collective-permute-start.11 = (bf16[4,1024,128]{2,1,0:T(8,128)(2,1)S(1)}, bf16[4,1024,128]{2,1,0:T(8,128)(2,1)S(1)}, u32[]{:S(2)}, u32[]{:S(2)}) collective-permute-start(bf16[4,1024,128]{2,1,0:T(8,128)(2,1)S(1)} %get-tuple-element.36.refs_0_), channel_id=1, source_target_pairs={{0,1},{1,0},{2,3},{3,2},{4,5},{5,4},{6,7},{7,6},{8,9},{9,8},{10,11... | collective-permute-start | bytes 3145736 | tf_op jit(solution)/shard_map/ppermute | solution.py:33
  53.3 3.6 %collective-permute-start.12 = (bf16[4,1024,128]{2,1,0:T(8,128)(2,1)S(1)}, bf16[4,1024,128]{2,1,0:T(8,128)(2,1)S(1)}, u32[]{:S(2)}, u32[]{:S(2)}) collective-permute-start(bf16[4,1024,128]{2,1,0:T(8,128)(2,1)S(1)} %shard_map.49.refs_1_), channel_id=1, source_target_pairs={{0,1},{1,0},{2,3},{3,2},{4,5},{5,4},{6,7},{7,6},{8,9},{9,8},{10,11... | collective-permute-start | bytes 3145736 | tf_op jit(solution)/shard_map/ppermute | solution.py:33
  53.4 20.7 %collective-permute-start.14 = (bf16[4,128,256]{2,1,0:T(8,128)(2,1)S(1)}, bf16[4,128,256]{2,1,0:T(8,128)(2,1)S(1)}, u32[]{:S(2)}, u32[]{:S(2)}) collective-permute-start(bf16[4,128,256]{2,1,0:T(8,128)(2,1)S(1)} %get-tuple-element.40.refs_4_), channel_id=1, source_target_pairs={{0,8},{8,0},{1,9},{9,1},{2,10},{10,2},{3,11},{11,3},{4,12},{12,4},... | collective-permute-start | bytes 786440 | tf_op jit(solution)/shard_map/ppermute | solution.py:27
  54.0 20.2 %collective-permute-start.15 = (bf16[4,128,256]{2,1,0:T(8,128)(2,1)S(1)}, bf16[4,128,256]{2,1,0:T(8,128)(2,1)S(1)}, u32[]{:S(2)}, u32[]{:S(2)}) collective-permute-start(bf16[4,128,256]{2,1,0:T(8,128)(2,1)S(1)} %get-tuple-element.41), channel_id=1, source_target_pairs={{0,12},{4,8},{8,4},{12,0},{1,13},{5,9},{9,5},{13,1},{2,14},{6,10},... | collective-permute-start | bytes 786440 | tf_op jit(solution)/shard_map/ppermute | solution.py:28
  56.0 25.5 %collective-permute-start.13 = (bf16[4,128,256]{2,1,0:T(8,128)(2,1)S(1)}, bf16[4,128,256]{2,1,0:T(8,128)(2,1)S(1)}, u32[]{:S(2)}, u32[]{:S(2)}) collective-permute-start(bf16[4,128,256]{2,1,0:T(8,128)(2,1)S(1)} %get-tuple-element.41), channel_id=1, source_target_pairs={{0,4},{4,0},{1,5},{5,1},{2,6},{6,2},{3,7},{7,3},{8,12},{12,8},{9,1... | collective-permute-start | bytes 786440 | tf_op jit(solution)/shard_map/ppermute | solution.py:27
  59.5 25.1 %collective-permute-start.20 = (s16[256,256]{1,0:T(8,128)(2,1)S(1)}, s16[256,256]{1,0:T(8,128)(2,1)S(1)}, u32[]{:S(2)}, u32[]{:S(2)}) collective-permute-start(s16[256,256]{1,0:T(8,128)(2,1)S(1)} %get-tuple-element.48), channel_id=1, source_target_pairs={{0,2},{2,0},{1,3},{3,1},{4,6},{6,4},{5,7},{7,5},{8,10},{10,8},{9,1... | collective-permute-start | bytes 393224 | tf_op jit(solution)/shard_map/ppermute | solution.py:27
  74.1 13.5 %collective-permute-start.21 = (s16[256,256]{1,0:T(8,128)(2,1)S(1)}, s16[256,256]{1,0:T(8,128)(2,1)S(1)}, u32[]{:S(2)}, u32[]{:S(2)}) collective-permute-start(s16[256,256]{1,0:T(8,128)(2,1)S(1)} %get-tuple-element.49), channel_id=1, source_target_pairs={{0,4},{4,0},{1,5},{5,1},{2,6},{6,2},{3,7},{7,3},{8,12},{12,8},{9,1... | collective-permute-start | bytes 393224 | tf_op jit(solution)/shard_map/ppermute | solution.py:27
  74.1 13.5 %collective-permute-start.22 = (s16[256,256]{1,0:T(8,128)(2,1)S(1)}, s16[256,256]{1,0:T(8,128)(2,1)S(1)}, u32[]{:S(2)}, u32[]{:S(2)}) collective-permute-start(s16[256,256]{1,0:T(8,128)(2,1)S(1)} %get-tuple-element.50), channel_id=1, source_target_pairs={{0,6},{2,4},{4,2},{6,0},{1,7},{3,5},{5,3},{7,1},{8,14},{10,12},{12... | collective-permute-start | bytes 393224 | tf_op jit(solution)/shard_map/ppermute | solution.py:28
  84.0 5.6 %collective-permute-start.16 = (s16[256,256]{1,0:T(8,128)(2,1)S(1)}, s16[256,256]{1,0:T(8,128)(2,1)S(1)}, u32[]{:S(2)}, u32[]{:S(2)}) collective-permute-start(s16[256,256]{1,0:T(8,128)(2,1)S(1)} %get-tuple-element.43), channel_id=1, source_target_pairs={{0,2},{2,0},{1,3},{3,1},{4,6},{6,4},{5,7},{7,5},{8,10},{10,8},{9,1... | collective-permute-start | bytes 393224 | tf_op jit(solution)/shard_map/ppermute | solution.py:27
  84.4 8.9 %copy-start = (f32[256,2048]{1,0:T(8,128)}, f32[256,2048]{1,0:T(8,128)S(1)}, u32[]{:S(2)}) copy-start(f32[256,2048]{1,0:T(8,128)S(1)} %collective-permute-done.refs_4_.refs_1_) | copy-start | bytes 6291460
  84.4 6.4 %collective-permute-start.17 = (s16[256,256]{1,0:T(8,128)(2,1)S(1)}, s16[256,256]{1,0:T(8,128)(2,1)S(1)}, u32[]{:S(2)}, u32[]{:S(2)}) collective-permute-start(s16[256,256]{1,0:T(8,128)(2,1)S(1)} %get-tuple-element.44), channel_id=1, source_target_pairs={{0,4},{4,0},{1,5},{5,1},{2,6},{6,2},{3,7},{7,3},{8,12},{12,8},{9,1... | collective-permute-start | bytes 393224 | tf_op jit(solution)/shard_map/ppermute | solution.py:27
  84.7 8.6 %collective-permute-start.18 = (s16[256,256]{1,0:T(8,128)(2,1)S(1)}, s16[256,256]{1,0:T(8,128)(2,1)S(1)}, u32[]{:S(2)}, u32[]{:S(2)}) collective-permute-start(s16[256,256]{1,0:T(8,128)(2,1)S(1)} %get-tuple-element.45), channel_id=1, source_target_pairs={{0,6},{2,4},{4,2},{6,0},{1,7},{3,5},{5,3},{7,1},{8,14},{10,12},{12... | collective-permute-start | bytes 393224 | tf_op jit(solution)/shard_map/ppermute | solution.py:28
  87.6 15.0 %copy-start.1 = (f32[1,1,256,2048]{3,2,1,0:T(8,128)S(1)}, f32[1,1,256,2048]{3,2,1,0:T(8,128)}, u32[]{:S(2)}) copy-start(f32[1,1,256,2048]{3,2,1,0:T(8,128)} %param.7) | copy-start | bytes 6291460
  87.7 14.9 %collective-permute-start.23 = (s16[4,256,256]{2,1,0:T(8,128)(2,1)S(1)}, s16[4,256,256]{2,1,0:T(8,128)(2,1)S(1)}, u32[]{:S(2)}, u32[]{:S(2)}) collective-permute-start(s16[4,256,256]{2,1,0:T(8,128)(2,1)S(1)} %shard_map.53.refs_2_), channel_id=1, source_target_pairs={{0,16},{16,0},{1,17},{17,1},{2,18},{18,2},{3,19},{19,3},{4,20},{20... | collective-permute-start | bytes 1572872 | tf_op jit(solution)/shard_map/ppermute | solution.py:33
  93.3 18.4 %collective-permute-start.19 = (s16[4,256,256]{2,1,0:T(8,128)(2,1)S(1)}, s16[4,256,256]{2,1,0:T(8,128)(2,1)S(1)}, u32[]{:S(2)}, u32[]{:S(2)}) collective-permute-start(s16[4,256,256]{2,1,0:T(8,128)(2,1)S(1)} %shard_map.51.refs_2_), channel_id=1, source_target_pairs={{0,16},{16,0},{1,17},{17,1},{2,18},{18,2},{3,19},{19,3},{4,20},{20... | collective-permute-start | bytes 1572872 | tf_op jit(solution)/shard_map/ppermute | solution.py:33

commit v3 on v2

--- a/solution.py
+++ b/solution.py
@@ -81,7 +81,7 @@
 
 
 def pack(start, own_ref, other_ref, sources):
-    own, width = lax.axis_index("zl"), own_ref.shape[2]
+    own, width = lax.axis_index("zl"), other_ref.shape[2]
     for which, ref in enumerate((own_ref, other_ref)):
         for i, source in enumerate(sources):
             seqs = source.shape[1]
@@ -89,39 +89,23 @@
 
 
 def gather_kernel(keep, z1, z2, *refs):
-    near, joint, own_ref, other_ref = refs[-4:]
+    near, pass_on, own_ref, other_ref = refs[-4:]
     fill(near, keep, z1, z2)
+    fill(pass_on, z2)
     pack(0, own_ref, other_ref, refs[:-4])
-    at = 0
-    for s in range(z2.shape[0]):
-        joint[at : at + z2.shape[1], :] = z2[s]
-        at += z2.shape[1]
-    count, length, width = other_ref.shape
-    for i in range(count):
-        for start in range(0, width, 128):
-            joint[at : at + length, :] = other_ref[i, :, start : start + 128]
-            at += length
-
-
-def second_kernel(starts, near, joint, *refs):
-    count = 3 + 2 * len(starts)
-    sources, (own_rows, far, cols, *outs) = refs[:-count], refs[-count:]
-    at = 0
-    for s in range(far.shape[0]):
-        far[s] = joint[at : at + far.shape[1], :]
-        at += far.shape[1]
-    fill(own_rows, near, far)
-    count, length, width = cols.shape
-    for i in range(count):
-        for start in range(0, width, 128):
-            cols[i, :, start : start + 128] = joint[at : at + length, :]
-            at += length
+
+
+def second_kernel(starts, near, z3, *refs):
+    count = 2 + 2 * len(starts)
+    sources, (own_rows, far, *outs) = refs[:-count], refs[-count:]
+    fill(far, z3)
+    fill(own_rows, near, z3)
     for k, start in enumerate(starts):
         pack(start, outs[2 * k], outs[2 * k + 1], sources)
 
 
-def third_kernel(first, second, out):
-    fill(out, first, second)
+def third_kernel(own, first, second, out):
+    fill(out, own, first, second)
 
 
 def code_kernel(*refs):
@@ -130,8 +114,8 @@
 
 
 def fisher_kernel(places, row_count, scale, code_scale, *refs):
-    rows, cols, outs, total = refs[:row_count], refs[row_count:-5], refs[-5:-1], refs[-1]
-    span = outs[0].shape[0]
+    rows, cols, outs, total = refs[:row_count], refs[row_count : row_count + 4], refs[row_count + 4 : -1], refs[-1]
+    span = total.shape[0] // 4
     own_zl, own_y = lax.axis_index("zl"), lax.axis_index("y")
 
     for group in range(4):
@@ -143,10 +127,20 @@
         damped = acc * scale + damping
         code = jnp.round((jnp.log(damped) - math.log(damping)) * code_scale) - 32768.0
         total[part, :] = jnp.clip(code, -32768.0, 32767.0)
-    for at, ref in enumerate(outs):
+    for at in range(4):
         group = (own_zl ^ (at // 2)) * 2 + (own_y ^ (at % 2))
         start = pl.multiple_of(group * span, span)
-        ref[...] = total[pl.ds(start, span), :].astype(jnp.int32).astype(jnp.int16)
+        code = total[pl.ds(start, span), :].astype(jnp.int32).astype(jnp.int16)
+        if len(outs) == 1:
+            outs[0][at] = code
+        else:
+            outs[at][...] = code
+
+
+def models_kernel(models, *refs):
+    for at, out in enumerate(refs[models:]):
+        for m in range(models):
+            out[m] = refs[m][at]
 
 
 def merge_chunk(models, tile_width, first, width, code_scale, weights, codes, store):
@@ -161,8 +155,11 @@
     for at in range(4):
         sub = (own_zl ^ (at // 2)) * 2 + (own_y ^ (at % 2))
         start = pl.multiple_of(sub * tile_width + first, 128)
-        codes_here = [code[at].astype(jnp.int32) for code in codes]
-        weights_here = [weight[:, pl.ds(start, width)] for weight in weights]
+        codes_here = [codes(m, at).astype(jnp.int32) for m in range(models)]
+        weights_here = [weights[0][:, pl.ds(start, width)]]
+        for m in range(1, models):
+            halves = [half[:, pl.ds(start, width)] for half in weights[2 * m - 1 : 2 * m + 1]]
+            weights_here.append(jnp.concatenate(halves, axis=0))
         base = pick(codes_here, 0)
         num, den = pick(weights_here, 0), None
         for j in range(1, models):
@@ -176,23 +173,33 @@
     def store(at, start, value):
         refs[-1][at] = value
 
-    weights, codes = refs[:models], refs[models:-1]
-    merge_chunk(models, tile_width, first, width, code_scale, weights, codes, store)
-
-
-def last_merge_kernel(models, tile_width, firsts, width, code_scale, *refs):
-    weights, codes, early, out = refs[:models], refs[models : 2 * models], refs[2 * models : -1], refs[-1]
+    weights, codes = refs[: 2 * models - 1], refs[2 * models - 1 : -1]
+    merge_chunk(models, tile_width, first, width, code_scale, weights, lambda m, at: codes[m][at], store)
+
+
+def last_merge_kernel(models, tile_width, firsts, widths, code_scale, *refs):
+    early, out, parts, done = refs[0], refs[-3], refs[-2], refs[-1]
+    weights, codes = refs[1 : 2 * models], refs[2 * models : -3]
     own_zl, own_y = lax.axis_index("zl"), lax.axis_index("y")
-    for first, ref in zip(firsts, early):
-        for at in range(4):
-            sub = (own_zl ^ (at // 2)) * 2 + (own_y ^ (at % 2))
-            start = pl.multiple_of(sub * tile_width + first, 128)
-            out[:, pl.ds(start, ref.shape[2])] = ref[at]
-
-    def store(at, start, value):
-        out[:, pl.ds(start, width)] = value
-
-    merge_chunk(models, tile_width, firsts[-1], width, code_scale, weights, codes, store)
+    copies = []
+
+    def send(source, start, width):
+        copies.append(pltpu.make_async_copy(source, out.at[:, pl.ds(start, width)], done.at[len(copies)]))
+        copies[-1].start()
+
+    for at in range(4):
+        sub = (own_zl ^ (at // 2)) * 2 + (own_y ^ (at % 2))
+        send(early.at[at], pl.multiple_of(sub * tile_width + firsts[-1], 128), widths[-1])
+    for k, width in enumerate(widths[:-1]):
+
+        def store(at, start, value):
+            parts[at, :, firsts[k] : firsts[k] + width] = value
+            send(parts.at[at, :, pl.ds(firsts[k], width)], start, width)
+
+        here = codes[4 * k : 4 * k + 4]
+        merge_chunk(models, tile_width, firsts[k], width, code_scale, weights, lambda m, at: here[at][m], store)
+    for copy in copies:
+        copy.wait()
 
 
 def shards(inputs, cotangent, token_ids, weights):
@@ -212,7 +219,10 @@
     peak = LARGEST**4 * length + damping
     code_scale = 65535.0 / (math.log(peak) - math.log(damping))
 
-    other_weights = [rotate(weights, "mp", offset) for offset in range(1, models)]
+    early_rows = weights.shape[0] // 2
+    other_weights = []
+    for offset in range(1, models):
+        other_weights += [rotate(weights[:early_rows], "mp", offset), rotate(weights[early_rows:], "mp", offset)]
 
     col_shape = jax.ShapeDtypeStruct((2, seqs, length, tile_width), bf)
     row_shape = jax.ShapeDtypeStruct((seqs, half, length), bf)
@@ -247,63 +257,78 @@
     z2 = swap(send, "zh")
     z1 = swap(keep, "zl")
     packs = [None] * len(widths)
-    pieces = seqs * (half + 2 * core_count * length * (widths[0] // 128))
-    near, joint, own, other = call(
-        gather_kernel,
-        (many_rows(3), jax.ShapeDtypeStruct((pieces, length), bf)) + (several(2 * core_count, widths[0]),) * 2,
+    near, pass_on, own, other = call(
+        gather_kernel, (many_rows(3), many_rows(1)) + (several(2 * core_count, widths[0]),) * 2
     )(keep, z1, z2, *got)
     packs[0] = [own, other]
     pack_shapes = [several(2 * core_count, width) for width in widths[1:] for _ in range(2)]
-    own_rows, far, near_cols, *others = call(
-        functools.partial(second_kernel, starts[1:]),
-        (many_rows(4), many_rows(1), several(2 * core_count, widths[0])) + tuple(pack_shapes),
-    )(near, swap(joint, "zl"), *got)
+    own_rows, far, *others = call(
+        functools.partial(second_kernel, starts[1:]), (many_rows(4), many_rows(1)) + tuple(pack_shapes)
+    )(near, swap(pass_on, "zl"), *got)
     for k in range(1, len(widths)):
         packs[k] = others[2 * k - 2 : 2 * k]
-    first_cols = [packs[0][0], near_cols, swap(packs[0][0], "zh"), swap(packs[0][1], ("zh", "zl"))]
-    y_rows = call(third_kernel, many_rows(4))(swap(near, "y"), swap(far, "y"), after=first_cols[2:])
-    rows = []
-    for dc in range(core_count):
-        rows += [own_rows, y_rows] if dc == 0 else [rotate(own_rows, "c", dc), rotate(y_rows, "c", dc)]
+    from_zh = swap(packs[0][0], "zh")
+    from_zl = swap(packs[0][1], "zl")
+    from_both = swap(packs[0][1], ("zh", "zl"))
+    first_cols = [packs[0][0], from_zl, from_zh, from_both]
+    all_rows = call(third_kernel, many_rows(8))(
+        own_rows, swap(near, "y"), swap(far, "y"), after=[from_zh, from_zl, from_both] + other_weights[::2]
+    )
+    rows = [rotate(all_rows, "c", dc) if dc else all_rows for dc in range(core_count)]
     places = []
     for dz in range(4):
         for dy in range(2):
             for dc in range(core_count):
                 for s in range(seqs):
-                    places.append((dc * 2 + dy, dz * seqs + s, dz, (dy * core_count + dc) * seqs + s))
-
-    merged = []
+                    places.append((dc, (dy * 4 + dz) * seqs + s, dz, (dy * core_count + dc) * seqs + s))
+
+    chunks = []
     for k, width in enumerate(widths):
         own, other = packs[k]
         cols = [own, swap(other, "zl"), swap(own, "zh"), swap(other, ("zh", "zl"))] if k else first_cols
+        last = k == len(widths) - 1
         code_shape = jax.ShapeDtypeStruct((span, width), jnp.int16)
+        four_shape = jax.ShapeDtypeStruct((4, span, width), jnp.int16)
         outs = call(
             functools.partial(fisher_kernel, places, len(rows), 1.0 / (length * total_seqs), code_scale),
-            (code_shape,) * 4,
+            (code_shape,) * 4 if last else (four_shape,),
             [pltpu.VMEM((half, width), jnp.float32)],
             flops=2 * half * width * length * total_seqs,
             bytes_accessed=2 * length * total_seqs * (half + width),
         )(*rows, *cols)
-        codes = call(code_kernel, jax.ShapeDtypeStruct((4, span, width), jnp.int16))(
-            outs[0],
-            swap(outs[1], "y"),
-            swap(outs[2], "zl"),
-            swap(outs[3], ("zl", "y")),
-            after=() if k else other_weights,
-        )
-        all_codes = [codes] + [rotate(codes, "mp", offset) for offset in range(1, models)]
-        if k < len(widths) - 1:
-            merged.append(
-                call(
-                    functools.partial(early_merge_kernel, models, tile_width, starts[k], width, code_scale),
-                    jax.ShapeDtypeStruct((4, span, width), jnp.float32),
-                )(weights, *other_weights, *all_codes)
+        if not last:
+            from_models = [rotate(outs[0], "mp", offset) for offset in range(1, models)]
+            parts = call(
+                functools.partial(models_kernel, models),
+                (jax.ShapeDtypeStruct((models, span, width), jnp.int16),) * 4,
+            )(outs[0], *from_models, after=other_weights[1::2])
+            parts = [parts[0], swap(parts[1], "y"), swap(parts[2], "zl"), swap(parts[3], ("zl", "y"))]
+            chunks += parts
+        else:
+            codes = call(code_kernel, four_shape)(
+                outs[0],
+                swap(outs[1], "y"),
+                swap(outs[2], "zl"),
+                swap(outs[3], ("zl", "y")),
+                after=() if k else other_weights[1::2],
             )
-        else:
-            result = call(
-                functools.partial(last_merge_kernel, models, tile_width, starts, width, code_scale),
-                jax.ShapeDtypeStruct(weights.shape, jnp.float32),
-            )(weights, *other_weights, *all_codes, *merged)
+            all_codes = [codes] + [rotate(codes, "mp", offset) for offset in range(1, models)]
+    early = call(
+        functools.partial(early_merge_kernel, models, tile_width, starts[-1], widths[-1], code_scale),
+        jax.ShapeDtypeStruct((4, span, widths[-1]), jnp.float32),
+    )(weights, *other_weights, *all_codes)
+    operands = [early, weights, *other_weights, *chunks]
+    result = pl.pallas_call(
+        functools.partial(last_merge_kernel, models, tile_width, starts, widths, code_scale),
+        out_shape=jax.ShapeDtypeStruct(weights.shape, jnp.float32),
+        in_specs=[VMEM] * len(operands),
+        out_specs=pl.BlockSpec(memory_space=pltpu.HBM),
+        scratch_shapes=[
+            pltpu.VMEM((4, span, tile_width), jnp.float32),
+            pltpu.SemaphoreType.DMA((4 * len(widths),)),
+        ],
+        compiler_params=pltpu.CompilerParams(vmem_limit_bytes=VMEM_LIMIT),
+    )(*operands)
     return result[None]
 
 

time: 116 us -> 109 us (0.940)
  starting transfers between devices: 36.1 us -> 31.9 us
  waiting for transfers between devices: 64.4 us -> 60.8 us
  local copies, waits for them, and re-layouts: 2.93 us -> 4.67 us
    ppermute x4, starting transfers between devices: 14 us -> 5.33 us  [swap(): return lax.ppermute(value, axes, [(i, i ^ 3) for i in range(4)])]
    ppermute x6, waiting for transfers between devices: 14.8 us -> 8.86 us  [rotate(): lax.ppermute(value, axis, [(i, (i + offset) % size) for i in range(size)])]
    ppermute x13 -> x14, starting transfers between devices: 17.3 us -> 21.8 us  [swap(): return lax.ppermute(value, axes, [(0, 1), (1, 0)])]
    pallas_call x10 -> x9, Pallas kernels: 11.7 us -> 8.18 us  [run(): pl.pallas_call(kernel, out_shape=out_shape, in_specs=[VMEM] * len(args) +...]
    pallas_call x0 -> x1, Pallas kernels: none -> 2.97 us  [shards(): pl.pallas_call(functools.partial(last_merge_kernel, models, tile_width, s...]
    slice x0 -> x1, local copies, waits for them, and re-layouts: none -> 1.75 us  [shards(): weights[early_rows:]]
    ppermute x13 -> x14, waiting for transfers between devices: 46.8 us -> 48.3 us  [swap(): return lax.ppermute(value, axes, [(0, 1), (1, 0)])]
    unnamed x10 -> x6, local copies, waits for them, and re-layouts: 2.93 us -> 2.92 us
  transfers between devices with their start and end apart: 24 -> 25, of which waited for: 12 -> 12; matrix products, arithmetic and copies ran while one was open for 0% -> 2% of each run, Pallas kernels for 7% -> 7%
where the time goes in v3:
time: 109 us
  waiting for transfers between devices  60.8 us (56%)
  starting transfers between devices  31.9 us (29%)
  Pallas kernels  11.2 us (10%)
  local copies, waits for them, and re-layouts  4.67 us (4%)
    ppermute x14, waiting for transfers between devices, swap(): return lax.ppermute(value, axes, [(0, 1), (1, 0)])  48.3 us
    ppermute x14, starting transfers between devices, swap(): return lax.ppermute(value, axes, [(0, 1), (1, 0)])  21.8 us
    ppermute x6, waiting for transfers between devices, rotate(): lax.ppermute(value, axis, [(i, (i + offset) % size) for i in range(size)])  8.86 us
    pallas_call x9, Pallas kernels, run(): pl.pallas_call(kernel, out_shape=out_shape, in_specs=[VMEM] * len(args) +...  8.18 us
    ppermute x4, starting transfers between devices, swap(): return lax.ppermute(value, axes, [(i, i ^ 3) for i in range(4)])  5.33 us
    ppermute x6, starting transfers between devices, rotate(): lax.ppermute(value, axis, [(i, (i + offset) % size) for i in range(size)])  4.44 us
    ppermute x4, waiting for transfers between devices, swap(): return lax.ppermute(value, axes, [(i, i ^ 3) for i in range(4)])  3.26 us
    pallas_call x1, Pallas kernels, shards(): pl.pallas_call(functools.partial(last_merge_kernel, models, tile_width, s...  2.97 us
  transfers between devices with their start and end apart: 25, of which 12 were waited for; matrix products, arithmetic and copies ran while one was open for 2% of the time, Pallas kernels for 7%

profile of v3, /device:TPU:0, one launch (start us, length us, event | category | flops | bytes accessed | tf_op | source)
XLA Modules:
  0.0 108.6 jit_solution(8178796238770873329)
XLA Ops:
  0.0 1.2 %copy-done = bf16[1,1,128,4096]{3,2,1,0:T(8,128)(2,1)S(1)} copy-done((bf16[1,1,128,4096]{3,2,1,0:T(8,128)(2,1)S(1)}, bf16[1,1,128,4096]{3,2,1,0:T(8,128)(2,1)}, u32[]{:S(2)}) %copy-start) | copy-done | bytes 1048600
  1.2 1.0 copy-done.1
  2.3 0.7 copy-done.2
  2.9 0.3 shard_map.46
  3.3 4.1 %collective-permute-start.3 = (bf16[1,1024,128]{2,1,0:T(8,128)(2,1)S(1)}, bf16[1,1024,128]{2,1,0:T(8,128)(2,1)S(1)}, u32[]{:S(2)}, u32[]{:S(2)}) collective-permute-start(bf16[1,1024,128]{2,1,0:T(8,128)(2,1)S(1)} %get-tuple-element.28), channel_id=1, source_target_pairs={{0,8},{8,0},{1,9},{9,1},{2,10},{10,2},{3,11},{11,3},{4,12},{12,4},... | collective-permute-start | bytes 786440 | tf_op jit(solution)/shard_map/ppermute | solution.py:27
  7.4 1.5 %collective-permute-start.5 = (bf16[2,1,128,512]{3,2,1,0:T(8,128)(2,1)S(1)}, bf16[2,1,128,512]{3,2,1,0:T(8,128)(2,1)S(1)}, u32[]{:S(2)}, u32[]{:S(2)}) collective-permute-start(bf16[2,1,128,512]{3,2,1,0:T(8,128)(2,1)S(1)} %get-tuple-element.31), channel_id=1, source_target_pairs={{0,2},{2,0},{1,3},{3,1},{4,6},{6,4},{5,7},{7,5},{8,10},{10,8},{9,1... | collective-permute-start | bytes 786440 | tf_op jit(solution)/shard_map/ppermute | solution.py:27
  8.9 0.3 collective-permute-start.6
  9.2 1.6 %collective-permute-start.2 = (bf16[1,1024,128]{2,1,0:T(8,128)(2,1)S(1)}, bf16[1,1024,128]{2,1,0:T(8,128)(2,1)S(1)}, u32[]{:S(2)}, u32[]{:S(2)}) collective-permute-start(bf16[1,1024,128]{2,1,0:T(8,128)(2,1)S(1)} %get-tuple-element.27.refs_0_), channel_id=1, source_target_pairs={{0,4},{4,0},{1,5},{5,1},{2,6},{6,2},{3,7},{7,3},{8,12},{12,8},{9,1... | collective-permute-start | bytes 786440 | tf_op jit(solution)/shard_map/ppermute | solution.py:27
  10.8 1.8 %slice_bitcast_fusion = (f32[128,2048]{1,0:T(8,128)S(1)}, f32[128,2048]{1,0:T(8,128)S(1)}) fusion(f32[1,1,256,2048]{3,2,1,0:T(8,128)} %param.7), kind=kLoop, calls=%fused_computation | loop fusion | bytes 4194304 | tf_op jit(solution)/shard_map/slice | solution.py:225
  12.6 6.8 %collective-permute-done.3.refs_2_ = bf16[1,1024,128]{2,1,0:T(8,128)(2,1)S(1)} collective-permute-done((bf16[1,1024,128]{2,1,0:T(8,128)(2,1)S(1)}, bf16[1,1024,128]{2,1,0:T(8,128)(2,1)S(1)}, u32[]{:S(2)}, u32[]{:S(2)}) %collective-permute-start.3) | collective-permute-done | bytes 262176 | tf_op jit(solution)/shard_map/ppermute | solution.py:27
  19.4 1.5 %collective-permute-start = (f32[128,2048]{1,0:T(8,128)S(1)}, f32[128,2048]{1,0:T(8,128)S(1)}, u32[]{:S(2)}, u32[]{:S(2)}) collective-permute-start(f32[128,2048]{1,0:T(8,128)S(1)} %get-tuple-element.50), channel_id=1, source_target_pairs={{0,16},{16,0},{1,17},{17,1},{2,18},{18,2},{3,19},{19,3},{4,20},{20... | collective-permute-start | bytes 3145736 | tf_op jit(solution)/shard_map/ppermute | solution.py:33
  20.9 0.0 collective-permute-done.4.refs_4_.refs_3_
  20.9 0.4 collective-permute-done.6.refs_6_.refs_5_
  21.3 0.9 collective-permute-done.2.refs_1_
  22.2 0.1 shard_map.47
  22.3 1.6 %collective-permute-start.8 = (bf16[3,1024,128]{2,1,0:T(8,128)(2,1)S(1)}, bf16[3,1024,128]{2,1,0:T(8,128)(2,1)S(1)}, u32[]{:S(2)}, u32[]{:S(2)}) collective-permute-start(bf16[3,1024,128]{2,1,0:T(8,128)(2,1)S(1)} %get-tuple-element.33.refs_0_), channel_id=1, source_target_pairs={{0,2},{2,0},{1,3},{3,1},{4,6},{6,4},{5,7},{7,5},{8,10},{10,8},{9,1... | collective-permute-start | bytes 2359304 | tf_op jit(solution)/shard_map/ppermute | solution.py:27
  24.0 0.7 collective-permute-start.7
  24.6 2.3 %collective-permute-start.10 = (bf16[4,128,256]{2,1,0:T(8,128)(2,1)S(1)}, bf16[4,128,256]{2,1,0:T(8,128)(2,1)S(1)}, u32[]{:S(2)}, u32[]{:S(2)}) collective-permute-start(bf16[4,128,256]{2,1,0:T(8,128)(2,1)S(1)} %get-tuple-element.37.refs_2_), channel_id=1, source_target_pairs={{0,8},{8,0},{1,9},{9,1},{2,10},{10,2},{3,11},{11,3},{4,12},{12,4},... | collective-permute-start | bytes 786440 | tf_op jit(solution)/shard_map/ppermute | solution.py:27
  26.9 1.5 %collective-permute-start.12 = (bf16[4,128,256]{2,1,0:T(8,128)(2,1)S(1)}, bf16[4,128,256]{2,1,0:T(8,128)(2,1)S(1)}, u32[]{:S(2)}, u32[]{:S(2)}) collective-permute-start(bf16[4,128,256]{2,1,0:T(8,128)(2,1)S(1)} %get-tuple-element.38), channel_id=1, source_target_pairs={{0,12},{4,8},{8,4},{12,0},{1,13},{5,9},{9,5},{13,1},{2,14},{6,10},... | collective-permute-start | bytes 786440 | tf_op jit(solution)/shard_map/ppermute | solution.py:28
  28.3 7.5 %collective-permute-done.7.refs_1_ = bf16[1,1024,128]{2,1,0:T(8,128)(2,1)S(1)} collective-permute-done((bf16[1,1024,128]{2,1,0:T(8,128)(2,1)S(1)}, bf16[1,1024,128]{2,1,0:T(8,128)(2,1)S(1)}, u32[]{:S(2)}, u32[]{:S(2)}) %collective-permute-start.7) | collective-permute-done | bytes 262176 | tf_op jit(solution)/shard_map/ppermute | solution.py:27
  35.8 0.1 shard_map.48
  35.9 10.1 %collective-permute-done.10.refs_3_.refs_4_ = bf16[4,128,256]{2,1,0:T(8,128)(2,1)S(1)} collective-permute-done((bf16[4,128,256]{2,1,0:T(8,128)(2,1)S(1)}, bf16[4,128,256]{2,1,0:T(8,128)(2,1)S(1)}, u32[]{:S(2)}, u32[]{:S(2)}) %collective-permute-start.10) | collective-permute-done | bytes 262176 | tf_op jit(solution)/shard_map/ppermute | solution.py:27
  46.0 0.5 collective-permute-start.9
  46.5 2.5 %collective-permute-done.11.refs_4_.refs_3_ = bf16[4,128,256]{2,1,0:T(8,128)(2,1)S(1)} collective-permute-done((bf16[4,128,256]{2,1,0:T(8,128)(2,1)S(1)}, bf16[4,128,256]{2,1,0:T(8,128)(2,1)S(1)}, u32[]{:S(2)}, u32[]{:S(2)}) %collective-permute-start.11) | collective-permute-done | bytes 262176 | tf_op jit(solution)/shard_map/ppermute | solution.py:27
  49.1 3.3 %collective-permute-done.9.refs_2_ = bf16[1,1024,128]{2,1,0:T(8,128)(2,1)S(1)} collective-permute-done((bf16[1,1024,128]{2,1,0:T(8,128)(2,1)S(1)}, bf16[1,1024,128]{2,1,0:T(8,128)(2,1)S(1)}, u32[]{:S(2)}, u32[]{:S(2)}) %collective-permute-start.9) | collective-permute-done | bytes 262176 | tf_op jit(solution)/shard_map/ppermute | solution.py:27
  52.4 0.1 shard_map.49.refs_0_
  52.5 0.1 collective-permute-start.13
  52.6 1.6 %collective-permute-start.1 = (f32[128,2048]{1,0:T(8,128)S(1)}, f32[128,2048]{1,0:T(8,128)S(1)}, u32[]{:S(2)}, u32[]{:S(2)}) collective-permute-start(f32[128,2048]{1,0:T(8,128)S(1)} %get-tuple-element.49), channel_id=1, source_target_pairs={{0,16},{16,0},{1,17},{17,1},{2,18},{18,2},{3,19},{19,3},{4,20},{20... | collective-permute-start | bytes 3145736 | tf_op jit(solution)/shard_map/ppermute | solution.py:33
  54.2 1.7 %collective-permute-start.16 = (bf16[4,128,256]{2,1,0:T(8,128)(2,1)S(1)}, bf16[4,128,256]{2,1,0:T(8,128)(2,1)S(1)}, u32[]{:S(2)}, u32[]{:S(2)}) collective-permute-start(bf16[4,128,256]{2,1,0:T(8,128)(2,1)S(1)} %get-tuple-element.40), channel_id=1, source_target_pairs={{0,12},{4,8},{8,4},{12,0},{1,13},{5,9},{9,5},{13,1},{2,14},{6,10},... | collective-permute-start | bytes 786440 | tf_op jit(solution)/shard_map/ppermute | solution.py:28
  55.9 1.8 %collective-permute-start.14 = (bf16[4,128,256]{2,1,0:T(8,128)(2,1)S(1)}, bf16[4,128,256]{2,1,0:T(8,128)(2,1)S(1)}, u32[]{:S(2)}, u32[]{:S(2)}) collective-permute-start(bf16[4,128,256]{2,1,0:T(8,128)(2,1)S(1)} %get-tuple-element.40), channel_id=1, source_target_pairs={{0,4},{4,0},{1,5},{5,1},{2,6},{6,2},{3,7},{7,3},{8,12},{12,8},{9,1... | collective-permute-start | bytes 786440 | tf_op jit(solution)/shard_map/ppermute | solution.py:27
  57.7 2.6 %shard_map.53.refs_0_ = s16[4,256,256]{2,1,0:T(8,128)(2,1)S(1)} custom-call(bf16[8,1024,128]{2,1,0:T(8,128)(2,1)S(1)} %shard_map.49.refs_0_, bf16[8,1024,128]{2,1,0:T(8,128)(2,1)S(1)} %collective-permute-done.13.refs_1_, bf16[4,128,256]{2,1,0:T(8,128)(2,1)S(1)} %get-tuple-element.37.refs_2_, ...), custom_call_target="tpu_custom_call" | custom-call | flops 1073741824 | bytes 5242880 | tf_op jit(solution)/shard_map/pallas_call | solution.py:41
  60.3 0.7 collective-permute-start.21
  60.9 12.9 %collective-permute-done.15.refs_4_ = bf16[4,128,256]{2,1,0:T(8,128)(2,1)S(1)} collective-permute-done((bf16[4,128,256]{2,1,0:T(8,128)(2,1)S(1)}, bf16[4,128,256]{2,1,0:T(8,128)(2,1)S(1)}, u32[]{:S(2)}, u32[]{:S(2)}) %collective-permute-start.15) | collective-permute-done | bytes 262176 | tf_op jit(solution)/shard_map/ppermute | solution.py:27
  73.9 1.3 %collective-permute-done.14.refs_3_ = bf16[4,128,256]{2,1,0:T(8,128)(2,1)S(1)} collective-permute-done((bf16[4,128,256]{2,1,0:T(8,128)(2,1)S(1)}, bf16[4,128,256]{2,1,0:T(8,128)(2,1)S(1)}, u32[]{:S(2)}, u32[]{:S(2)}) %collective-permute-start.14) | collective-permute-done | bytes 262176 | tf_op jit(solution)/shard_map/ppermute | solution.py:27
  75.2 2.6 %shard_map.50 = (s16[256,256]{1,0:T(8,128)(2,1)S(1)}, s16[256,256]{1,0:T(8,128)(2,1)S(1)}, s16[256,256]{1,0:T(8,128)(2,1)S(1)}, s16[256,256]{1,0:T(8,128)(2,1)S(1)}) custom-call(bf16[8,1024,128]{2,1,0:T(8,128)(2,1)S(1)} %shard_map.49.refs_0_, bf16[8,1024,128]{2,1,0:T(8,128)(2,1)S(1)} %collective-permute-done.13.refs_1_, ...), custom_call_target="tpu_custom_call" | custom-call | flops 1073741824 | bytes 5242880 | tf_op jit(solution)/shard_map/pallas_call | solution.py:41
  77.8 0.6 collective-permute-start.17
  78.4 4.8 %collective-permute-start.18 = (s16[256,256]{1,0:T(8,128)(2,1)S(1)}, s16[256,256]{1,0:T(8,128)(2,1)S(1)}, u32[]{:S(2)}, u32[]{:S(2)}) collective-permute-start(s16[256,256]{1,0:T(8,128)(2,1)S(1)} %get-tuple-element.43), channel_id=1, source_target_pairs={{0,4},{4,0},{1,5},{5,1},{2,6},{6,2},{3,7},{7,3},{8,12},{12,8},{9,1... | collective-permute-start | bytes 393224 | tf_op jit(solution)/shard_map/ppermute | solution.py:27
  83.2 0.9 collective-permute-start.19
  84.1 3.0 %collective-permute-done.18.refs_2_ = s16[256,256]{1,0:T(8,128)(2,1)S(1)} collective-permute-done((s16[256,256]{1,0:T(8,128)(2,1)S(1)}, s16[256,256]{1,0:T(8,128)(2,1)S(1)}, u32[]{:S(2)}, u32[]{:S(2)}) %collective-permute-start.18) | collective-permute-done | bytes 131104 | tf_op jit(solution)/shard_map/ppermute | solution.py:27
  87.1 3.3 %collective-permute-done.19.refs_3_ = s16[256,256]{1,0:T(8,128)(2,1)S(1)} collective-permute-done((s16[256,256]{1,0:T(8,128)(2,1)S(1)}, s16[256,256]{1,0:T(8,128)(2,1)S(1)}, u32[]{:S(2)}, u32[]{:S(2)}) %collective-permute-start.19) | collective-permute-done | bytes 131104 | tf_op jit(solution)/shard_map/ppermute | solution.py:28
  90.4 0.6 collective-permute-start.20
  91.0 0.1 shard_map.54
  91.1 0.6 collective-permute-start.22
  91.7 1.7 %collective-permute-start.23 = (s16[2,256,256]{2,1,0:T(8,128)(2,1)S(1)}, s16[2,256,256]{2,1,0:T(8,128)(2,1)S(1)}, u32[]{:S(2)}, u32[]{:S(2)}) collective-permute-start(s16[2,256,256]{2,1,0:T(8,128)(2,1)S(1)} %get-tuple-element.47), channel_id=1, source_target_pairs={{0,4},{4,0},{1,5},{5,1},{2,6},{6,2},{3,7},{7,3},{8,12},{12,8},{9,1... | collective-permute-start | bytes 786440 | tf_op jit(solution)/shard_map/ppermute | solution.py:27
  93.4 1.2 %collective-permute-start.24 = (s16[2,256,256]{2,1,0:T(8,128)(2,1)S(1)}, s16[2,256,256]{2,1,0:T(8,128)(2,1)S(1)}, u32[]{:S(2)}, u32[]{:S(2)}) collective-permute-start(s16[2,256,256]{2,1,0:T(8,128)(2,1)S(1)} %get-tuple-element.48), channel_id=1, source_target_pairs={{0,6},{2,4},{4,2},{6,0},{1,7},{3,5},{5,3},{7,1},{8,14},{10,12},{12... | collective-permute-start | bytes 786440 | tf_op jit(solution)/shard_map/ppermute | solution.py:28
  94.6 8.9 %collective-permute-done.20.refs_4_ = s16[4,256,256]{2,1,0:T(8,128)(2,1)S(1)} collective-permute-done((s16[4,256,256]{2,1,0:T(8,128)(2,1)S(1)}, s16[4,256,256]{2,1,0:T(8,128)(2,1)S(1)}, u32[]{:S(2)}, u32[]{:S(2)}) %collective-permute-start.20) | collective-permute-done | bytes 524320 | tf_op jit(solution)/shard_map/ppermute | solution.py:33
  103.5 2.2 %shard_map.52.refs_0_ = f32[4,256,256]{2,1,0:T(8,128)S(1)} custom-call(f32[256,2048]{1,0:T(8,128)} %bitcast.12, f32[128,2048]{1,0:T(8,128)S(1)} %collective-permute-done.refs_6_.refs_1_.refs_2_, f32[128,2048]{1,0:T(8,128)S(1)} %collective-permute-done.1.refs_2_.refs_3_, s16[4,256,256]{2,1,0:T(8,128)(2,1)S(1)} %shard_map.51.refs_3_, ...), custom_call_target="tpu_custom_call" | custom-call | tf_op jit(solution)/shard_map/pallas_call | solution.py:41
  105.7 3.0 %shard_map.55 = f32[256,2048]{1,0:T(8,128)} custom-call(f32[4,256,256]{2,1,0:T(8,128)S(1)} %shard_map.52.refs_0_, f32[256,2048]{1,0:T(8,128)} %bitcast.13, f32[128,2048]{1,0:T(8,128)S(1)} %collective-permute-done.refs_6_.refs_1_.refs_2_, f32[128,2048]{1,0:T(8,128)S(1)} %collective-permute-done.1.refs_2_.refs_3_, ...), custom_call_target="tpu_custom_call" | custom-call | tf_op jit(solution)/shard_map/pallas_call | solution.py:321
  (19 shorter events, 0.1 us)
Async XLA Ops:
  0.0 1.2 %copy-start = (bf16[1,1,128,4096]{3,2,1,0:T(8,128)(2,1)S(1)}, bf16[1,1,128,4096]{3,2,1,0:T(8,128)(2,1)}, u32[]{:S(2)}) copy-start(bf16[1,1,128,4096]{3,2,1,0:T(8,128)(2,1)} %param.5) | copy-start | bytes 3145732
  1.2 1.0 copy-start.1
  2.3 0.7 copy-start.2
  3.3 16.1 %collective-permute-start.3 = (bf16[1,1024,128]{2,1,0:T(8,128)(2,1)S(1)}, bf16[1,1024,128]{2,1,0:T(8,128)(2,1)S(1)}, u32[]{:S(2)}, u32[]{:S(2)}) collective-permute-start(bf16[1,1024,128]{2,1,0:T(8,128)(2,1)S(1)} %get-tuple-element.28), channel_id=1, source_target_pairs={{0,8},{8,0},{1,9},{9,1},{2,10},{10,2},{3,11},{11,3},{4,12},{12,4},... | collective-permute-start | bytes 786440 | tf_op jit(solution)/shard_map/ppermute | solution.py:27
  7.4 13.6 %collective-permute-start.4 = (bf16[2,1,128,512]{3,2,1,0:T(8,128)(2,1)S(1)}, bf16[2,1,128,512]{3,2,1,0:T(8,128)(2,1)S(1)}, u32[]{:S(2)}, u32[]{:S(2)}) collective-permute-start(bf16[2,1,128,512]{3,2,1,0:T(8,128)(2,1)S(1)} %get-tuple-element.30), channel_id=1, source_target_pairs={{0,1},{1,0},{2,3},{3,2},{4,5},{5,4},{6,7},{7,6},{8,9},{9,8},{10,11... | collective-permute-start | bytes 786440 | tf_op jit(solution)/shard_map/ppermute | solution.py:33
  7.4 13.6 %collective-permute-start.5 = (bf16[2,1,128,512]{3,2,1,0:T(8,128)(2,1)S(1)}, bf16[2,1,128,512]{3,2,1,0:T(8,128)(2,1)S(1)}, u32[]{:S(2)}, u32[]{:S(2)}) collective-permute-start(bf16[2,1,128,512]{3,2,1,0:T(8,128)(2,1)S(1)} %get-tuple-element.31), channel_id=1, source_target_pairs={{0,2},{2,0},{1,3},{3,1},{4,6},{6,4},{5,7},{7,5},{8,10},{10,8},{9,1... | collective-permute-start | bytes 786440 | tf_op jit(solution)/shard_map/ppermute | solution.py:27
  8.9 12.4 %collective-permute-start.6 = (bf16[2,1,128,512]{3,2,1,0:T(8,128)(2,1)S(1)}, bf16[2,1,128,512]{3,2,1,0:T(8,128)(2,1)S(1)}, u32[]{:S(2)}, u32[]{:S(2)}) collective-permute-start(bf16[2,1,128,512]{3,2,1,0:T(8,128)(2,1)S(1)} %get-tuple-element.32), channel_id=1, source_target_pairs={{0,3},{1,2},{2,1},{3,0},{4,7},{5,6},{6,5},{7,4},{8,11},{9,10},{10,... | collective-permute-start | bytes 786440 | tf_op jit(solution)/shard_map/ppermute | solution.py:242
  9.2 12.9 %collective-permute-start.2 = (bf16[1,1024,128]{2,1,0:T(8,128)(2,1)S(1)}, bf16[1,1024,128]{2,1,0:T(8,128)(2,1)S(1)}, u32[]{:S(2)}, u32[]{:S(2)}) collective-permute-start(bf16[1,1024,128]{2,1,0:T(8,128)(2,1)S(1)} %get-tuple-element.27.refs_0_), channel_id=1, source_target_pairs={{0,4},{4,0},{1,5},{5,1},{2,6},{6,2},{3,7},{7,3},{8,12},{12,8},{9,1... | collective-permute-start | bytes 786440 | tf_op jit(solution)/shard_map/ppermute | solution.py:27
  19.4 33.0 %collective-permute-start = (f32[128,2048]{1,0:T(8,128)S(1)}, f32[128,2048]{1,0:T(8,128)S(1)}, u32[]{:S(2)}, u32[]{:S(2)}) collective-permute-start(f32[128,2048]{1,0:T(8,128)S(1)} %get-tuple-element.50), channel_id=1, source_target_pairs={{0,16},{16,0},{1,17},{17,1},{2,18},{18,2},{3,19},{19,3},{4,20},{20... | collective-permute-start | bytes 3145736 | tf_op jit(solution)/shard_map/ppermute | solution.py:33
  22.3 30.1 %collective-permute-start.8 = (bf16[3,1024,128]{2,1,0:T(8,128)(2,1)S(1)}, bf16[3,1024,128]{2,1,0:T(8,128)(2,1)S(1)}, u32[]{:S(2)}, u32[]{:S(2)}) collective-permute-start(bf16[3,1024,128]{2,1,0:T(8,128)(2,1)S(1)} %get-tuple-element.33.refs_0_), channel_id=1, source_target_pairs={{0,2},{2,0},{1,3},{3,1},{4,6},{6,4},{5,7},{7,5},{8,10},{10,8},{9,1... | collective-permute-start | bytes 2359304 | tf_op jit(solution)/shard_map/ppermute | solution.py:27
  24.0 11.8 %collective-permute-start.7 = (bf16[1,1024,128]{2,1,0:T(8,128)(2,1)S(1)}, bf16[1,1024,128]{2,1,0:T(8,128)(2,1)S(1)}, u32[]{:S(2)}, u32[]{:S(2)}) collective-permute-start(bf16[1,1024,128]{2,1,0:T(8,128)(2,1)S(1)} %get-tuple-element.34), channel_id=1, source_target_pairs={{0,4},{4,0},{1,5},{5,1},{2,6},{6,2},{3,7},{7,3},{8,12},{12,8},{9,1... | collective-permute-start | bytes 786440 | tf_op jit(solution)/shard_map/ppermute | solution.py:27
  24.6 21.4 %collective-permute-start.10 = (bf16[4,128,256]{2,1,0:T(8,128)(2,1)S(1)}, bf16[4,128,256]{2,1,0:T(8,128)(2,1)S(1)}, u32[]{:S(2)}, u32[]{:S(2)}) collective-permute-start(bf16[4,128,256]{2,1,0:T(8,128)(2,1)S(1)} %get-tuple-element.37.refs_2_), channel_id=1, source_target_pairs={{0,8},{8,0},{1,9},{9,1},{2,10},{10,2},{3,11},{11,3},{4,12},{12,4},... | collective-permute-start | bytes 786440 | tf_op jit(solution)/shard_map/ppermute | solution.py:27
  26.9 19.7 %collective-permute-start.12 = (bf16[4,128,256]{2,1,0:T(8,128)(2,1)S(1)}, bf16[4,128,256]{2,1,0:T(8,128)(2,1)S(1)}, u32[]{:S(2)}, u32[]{:S(2)}) collective-permute-start(bf16[4,128,256]{2,1,0:T(8,128)(2,1)S(1)} %get-tuple-element.38), channel_id=1, source_target_pairs={{0,12},{4,8},{8,4},{12,0},{1,13},{5,9},{9,5},{13,1},{2,14},{6,10},... | collective-permute-start | bytes 786440 | tf_op jit(solution)/shard_map/ppermute | solution.py:28
  35.8 13.3 %collective-permute-start.11 = (bf16[4,128,256]{2,1,0:T(8,128)(2,1)S(1)}, bf16[4,128,256]{2,1,0:T(8,128)(2,1)S(1)}, u32[]{:S(2)}, u32[]{:S(2)}) collective-permute-start(bf16[4,128,256]{2,1,0:T(8,128)(2,1)S(1)} %get-tuple-element.38), channel_id=1, source_target_pairs={{0,4},{4,0},{1,5},{5,1},{2,6},{6,2},{3,7},{7,3},{8,12},{12,8},{9,1... | collective-permute-start | bytes 786440 | tf_op jit(solution)/shard_map/ppermute | solution.py:27
  46.0 6.4 %collective-permute-start.9 = (bf16[1,1024,128]{2,1,0:T(8,128)(2,1)S(1)}, bf16[1,1024,128]{2,1,0:T(8,128)(2,1)S(1)}, u32[]{:S(2)}, u32[]{:S(2)}) collective-permute-start(bf16[1,1024,128]{2,1,0:T(8,128)(2,1)S(1)} %get-tuple-element.36), channel_id=1, source_target_pairs={{0,2},{2,0},{1,3},{3,1},{4,6},{6,4},{5,7},{7,5},{8,10},{10,8},{9,1... | collective-permute-start | bytes 786440 | tf_op jit(solution)/shard_map/ppermute | solution.py:27
  52.5 5.1 %collective-permute-start.13 = (bf16[8,1024,128]{2,1,0:T(8,128)(2,1)S(1)}, bf16[8,1024,128]{2,1,0:T(8,128)(2,1)S(1)}, u32[]{:S(2)}, u32[]{:S(2)}) collective-permute-start(bf16[8,1024,128]{2,1,0:T(8,128)(2,1)S(1)} %shard_map.49.refs_0_), channel_id=1, source_target_pairs={{0,1},{1,0},{2,3},{3,2},{4,5},{5,4},{6,7},{7,6},{8,9},{9,8},{10,11... | collective-permute-start | bytes 6291464 | tf_op jit(solution)/shard_map/ppermute | solution.py:33
  52.6 38.4 %collective-permute-start.1 = (f32[128,2048]{1,0:T(8,128)S(1)}, f32[128,2048]{1,0:T(8,128)S(1)}, u32[]{:S(2)}, u32[]{:S(2)}) collective-permute-start(f32[128,2048]{1,0:T(8,128)S(1)} %get-tuple-element.49), channel_id=1, source_target_pairs={{0,16},{16,0},{1,17},{17,1},{2,18},{18,2},{3,19},{19,3},{4,20},{20... | collective-permute-start | bytes 3145736 | tf_op jit(solution)/shard_map/ppermute | solution.py:33
  54.2 19.7 %collective-permute-start.15 = (bf16[4,128,256]{2,1,0:T(8,128)(2,1)S(1)}, bf16[4,128,256]{2,1,0:T(8,128)(2,1)S(1)}, u32[]{:S(2)}, u32[]{:S(2)}) collective-permute-start(bf16[4,128,256]{2,1,0:T(8,128)(2,1)S(1)} %get-tuple-element.39.refs_2_), channel_id=1, source_target_pairs={{0,8},{8,0},{1,9},{9,1},{2,10},{10,2},{3,11},{11,3},{4,12},{12,4},... | collective-permute-start | bytes 786440 | tf_op jit(solution)/shard_map/ppermute | solution.py:27
  54.2 19.7 %collective-permute-start.16 = (bf16[4,128,256]{2,1,0:T(8,128)(2,1)S(1)}, bf16[4,128,256]{2,1,0:T(8,128)(2,1)S(1)}, u32[]{:S(2)}, u32[]{:S(2)}) collective-permute-start(bf16[4,128,256]{2,1,0:T(8,128)(2,1)S(1)} %get-tuple-element.40), channel_id=1, source_target_pairs={{0,12},{4,8},{8,4},{12,0},{1,13},{5,9},{9,5},{13,1},{2,14},{6,10},... | collective-permute-start | bytes 786440 | tf_op jit(solution)/shard_map/ppermute | solution.py:28
  55.9 19.3 %collective-permute-start.14 = (bf16[4,128,256]{2,1,0:T(8,128)(2,1)S(1)}, bf16[4,128,256]{2,1,0:T(8,128)(2,1)S(1)}, u32[]{:S(2)}, u32[]{:S(2)}) collective-permute-start(bf16[4,128,256]{2,1,0:T(8,128)(2,1)S(1)} %get-tuple-element.40), channel_id=1, source_target_pairs={{0,4},{4,0},{1,5},{5,1},{2,6},{6,2},{3,7},{7,3},{8,12},{12,8},{9,1... | collective-permute-start | bytes 786440 | tf_op jit(solution)/shard_map/ppermute | solution.py:27
  60.3 30.7 %collective-permute-start.21 = (s16[4,256,256]{2,1,0:T(8,128)(2,1)S(1)}, s16[4,256,256]{2,1,0:T(8,128)(2,1)S(1)}, u32[]{:S(2)}, u32[]{:S(2)}) collective-permute-start(s16[4,256,256]{2,1,0:T(8,128)(2,1)S(1)} %shard_map.53.refs_0_), channel_id=1, source_target_pairs={{0,16},{16,0},{1,17},{17,1},{2,18},{18,2},{3,19},{19,3},{4,20},{20... | collective-permute-start | bytes 1572872 | tf_op jit(solution)/shard_map/ppermute | solution.py:33
  77.8 6.3 %collective-permute-start.17 = (s16[256,256]{1,0:T(8,128)(2,1)S(1)}, s16[256,256]{1,0:T(8,128)(2,1)S(1)}, u32[]{:S(2)}, u32[]{:S(2)}) collective-permute-start(s16[256,256]{1,0:T(8,128)(2,1)S(1)} %get-tuple-element.42), channel_id=1, source_target_pairs={{0,2},{2,0},{1,3},{3,1},{4,6},{6,4},{5,7},{7,5},{8,10},{10,8},{9,1... | collective-permute-start | bytes 393224 | tf_op jit(solution)/shard_map/ppermute | solution.py:27
  78.4 8.7 %collective-permute-start.18 = (s16[256,256]{1,0:T(8,128)(2,1)S(1)}, s16[256,256]{1,0:T(8,128)(2,1)S(1)}, u32[]{:S(2)}, u32[]{:S(2)}) collective-permute-start(s16[256,256]{1,0:T(8,128)(2,1)S(1)} %get-tuple-element.43), channel_id=1, source_target_pairs={{0,4},{4,0},{1,5},{5,1},{2,6},{6,2},{3,7},{7,3},{8,12},{12,8},{9,1... | collective-permute-start | bytes 393224 | tf_op jit(solution)/shard_map/ppermute | solution.py:27
  83.2 7.2 %collective-permute-start.19 = (s16[256,256]{1,0:T(8,128)(2,1)S(1)}, s16[256,256]{1,0:T(8,128)(2,1)S(1)}, u32[]{:S(2)}, u32[]{:S(2)}) collective-permute-start(s16[256,256]{1,0:T(8,128)(2,1)S(1)} %get-tuple-element.44), channel_id=1, source_target_pairs={{0,6},{2,4},{4,2},{6,0},{1,7},{3,5},{5,3},{7,1},{8,14},{10,12},{12... | collective-permute-start | bytes 393224 | tf_op jit(solution)/shard_map/ppermute | solution.py:28
  90.4 13.1 %collective-permute-start.20 = (s16[4,256,256]{2,1,0:T(8,128)(2,1)S(1)}, s16[4,256,256]{2,1,0:T(8,128)(2,1)S(1)}, u32[]{:S(2)}, u32[]{:S(2)}) collective-permute-start(s16[4,256,256]{2,1,0:T(8,128)(2,1)S(1)} %shard_map.51.refs_3_), channel_id=1, source_target_pairs={{0,16},{16,0},{1,17},{17,1},{2,18},{18,2},{3,19},{19,3},{4,20},{20... | collective-permute-start | bytes 1572872 | tf_op jit(solution)/shard_map/ppermute | solution.py:33
  91.1 14.6 %collective-permute-start.22 = (s16[2,256,256]{2,1,0:T(8,128)(2,1)S(1)}, s16[2,256,256]{2,1,0:T(8,128)(2,1)S(1)}, u32[]{:S(2)}, u32[]{:S(2)}) collective-permute-start(s16[2,256,256]{2,1,0:T(8,128)(2,1)S(1)} %get-tuple-element.46), channel_id=1, source_target_pairs={{0,2},{2,0},{1,3},{3,1},{4,6},{6,4},{5,7},{7,5},{8,10},{10,8},{9,1... | collective-permute-start | bytes 786440 | tf_op jit(solution)/shard_map/ppermute | solution.py:27
  91.7 14.0 %collective-permute-start.23 = (s16[2,256,256]{2,1,0:T(8,128)(2,1)S(1)}, s16[2,256,256]{2,1,0:T(8,128)(2,1)S(1)}, u32[]{:S(2)}, u32[]{:S(2)}) collective-permute-start(s16[2,256,256]{2,1,0:T(8,128)(2,1)S(1)} %get-tuple-element.47), channel_id=1, source_target_pairs={{0,4},{4,0},{1,5},{5,1},{2,6},{6,2},{3,7},{7,3},{8,12},{12,8},{9,1... | collective-permute-start | bytes 786440 | tf_op jit(solution)/shard_map/ppermute | solution.py:27
  93.4 12.3 %collective-permute-start.24 = (s16[2,256,256]{2,1,0:T(8,128)(2,1)S(1)}, s16[2,256,256]{2,1,0:T(8,128)(2,1)S(1)}, u32[]{:S(2)}, u32[]{:S(2)}) collective-permute-start(s16[2,256,256]{2,1,0:T(8,128)(2,1)S(1)} %get-tuple-element.48), channel_id=1, source_target_pairs={{0,6},{2,4},{4,2},{6,0},{1,7},{3,5},{5,3},{7,1},{8,14},{10,12},{12... | collective-permute-start | bytes 786440 | tf_op jit(solution)/shard_map/ppermute | solution.py:28

commit v4 on v3

--- a/solution.py
+++ b/solution.py
@@ -17,7 +17,7 @@
 
 TOK = ("zh", "zl", "y", "c")
 VMEM = pl.BlockSpec(memory_space=pltpu.VMEM)
-VMEM_LIMIT = 48 * 1024 * 1024
+VMEM_LIMIT = 28 * 1024 * 1024
 
 CHUNKS = (0.5, 0.5)
 
@@ -143,7 +143,7 @@
             out[m] = refs[m][at]
 
 
-def merge_chunk(models, tile_width, first, width, code_scale, weights, codes, store):
+def merge_chunk(senders, models, tile_width, first, width, code_scale, weights, codes, store):
     own_zl, own_y, own_m = lax.axis_index("zl"), lax.axis_index("y"), lax.axis_index("mp")
 
     def pick(values, j):
@@ -152,7 +152,7 @@
             chosen = jnp.where(lax.rem(own_m + models - offset, models) == j, values[offset], chosen)
         return chosen
 
-    for at in range(4):
+    for at in senders:
         sub = (own_zl ^ (at // 2)) * 2 + (own_y ^ (at % 2))
         start = pl.multiple_of(sub * tile_width + first, 128)
         codes_here = [codes(m, at).astype(jnp.int32) for m in range(models)]
@@ -174,12 +174,21 @@
         refs[-1][at] = value
 
     weights, codes = refs[: 2 * models - 1], refs[2 * models - 1 : -1]
-    merge_chunk(models, tile_width, first, width, code_scale, weights, lambda m, at: codes[m][at], store)
+    merge_chunk(range(4), models, tile_width, first, width, code_scale, weights, lambda m, at: codes[m][at], store)
+
+
+def near_merge_kernel(models, tile_width, first, width, code_scale, *refs):
+    def store(at, start, value):
+        refs[-1][at] = value
+
+    weights, codes = refs[: 2 * models - 1], refs[2 * models - 1 : -1]
+    merge_chunk(range(2), models, tile_width, first, width, code_scale, weights, lambda m, at: codes[at][m], store)
 
 
 def last_merge_kernel(models, tile_width, firsts, widths, code_scale, *refs):
-    early, out, parts, done = refs[0], refs[-3], refs[-2], refs[-1]
-    weights, codes = refs[1 : 2 * models], refs[2 * models : -3]
+    count = len(widths) - 1
+    last, nears, refs = refs[0], refs[1 : 1 + count], refs[1 + count :]
+    weights, codes, (out, parts, done) = refs[: 2 * models - 1], refs[2 * models - 1 : -3], refs[-3:]
     own_zl, own_y = lax.axis_index("zl"), lax.axis_index("y")
     copies = []
 
@@ -187,17 +196,21 @@
         copies.append(pltpu.make_async_copy(source, out.at[:, pl.ds(start, width)], done.at[len(copies)]))
         copies[-1].start()
 
-    for at in range(4):
-        sub = (own_zl ^ (at // 2)) * 2 + (own_y ^ (at % 2))
-        send(early.at[at], pl.multiple_of(sub * tile_width + firsts[-1], 128), widths[-1])
-    for k, width in enumerate(widths[:-1]):
+    for ref, first, width, senders in zip((last, *nears), (firsts[-1], *firsts), (widths[-1], *widths), (4, 2, 2, 2)):
+        for at in range(senders):
+            sub = (own_zl ^ (at // 2)) * 2 + (own_y ^ (at % 2))
+            send(ref.at[at], pl.multiple_of(sub * tile_width + first, 128), width)
+    for k in range(count):
+        first, width = firsts[k], widths[k]
 
         def store(at, start, value):
-            parts[at, :, firsts[k] : firsts[k] + width] = value
-            send(parts.at[at, :, pl.ds(firsts[k], width)], start, width)
-
-        here = codes[4 * k : 4 * k + 4]
-        merge_chunk(models, tile_width, firsts[k], width, code_scale, weights, lambda m, at: here[at][m], store)
+            parts[at - 2, :, first : first + width] = value
+            send(parts.at[at - 2, :, pl.ds(first, width)], start, width)
+
+        here = codes[2 * k : 2 * k + 2]
+        merge_chunk(
+            range(2, 4), models, tile_width, first, width, code_scale, weights, lambda m, at: here[at - 2][m], store
+        )
     for copy in copies:
         copy.wait()
 
@@ -282,7 +295,7 @@
                 for s in range(seqs):
                     places.append((dc, (dy * 4 + dz) * seqs + s, dz, (dy * core_count + dc) * seqs + s))
 
-    chunks = []
+    nears, chunks = [], []
     for k, width in enumerate(widths):
         own, other = packs[k]
         cols = [own, swap(other, "zl"), swap(own, "zh"), swap(other, ("zh", "zl"))] if k else first_cols
@@ -303,28 +316,37 @@
                 (jax.ShapeDtypeStruct((models, span, width), jnp.int16),) * 4,
             )(outs[0], *from_models, after=other_weights[1::2])
             parts = [parts[0], swap(parts[1], "y"), swap(parts[2], "zl"), swap(parts[3], ("zl", "y"))]
-            chunks += parts
+            nears.append(
+                call(
+                    functools.partial(near_merge_kernel, models, tile_width, starts[k], width, code_scale),
+                    jax.ShapeDtypeStruct((2, span, width), jnp.float32),
+                )(weights, *other_weights, *parts[:2])
+            )
+            chunks += parts[2:]
         else:
+            far = swap(outs[3], ("zl", "y"))
+            over_z = swap(outs[2], "zl")
+            over_y = swap(outs[1], "y")
             codes = call(code_kernel, four_shape)(
                 outs[0],
-                swap(outs[1], "y"),
-                swap(outs[2], "zl"),
-                swap(outs[3], ("zl", "y")),
+                over_y,
+                over_z,
+                far,
                 after=() if k else other_weights[1::2],
             )
             all_codes = [codes] + [rotate(codes, "mp", offset) for offset in range(1, models)]
     early = call(
         functools.partial(early_merge_kernel, models, tile_width, starts[-1], widths[-1], code_scale),
         jax.ShapeDtypeStruct((4, span, widths[-1]), jnp.float32),
-    )(weights, *other_weights, *all_codes)
-    operands = [early, weights, *other_weights, *chunks]
+    )(weights, *other_weights, *all_codes, after=nears)
+    operands = [early, *nears, weights, *other_weights, *chunks]
     result = pl.pallas_call(
         functools.partial(last_merge_kernel, models, tile_width, starts, widths, code_scale),
         out_shape=jax.ShapeDtypeStruct(weights.shape, jnp.float32),
         in_specs=[VMEM] * len(operands),
         out_specs=pl.BlockSpec(memory_space=pltpu.HBM),
         scratch_shapes=[
-            pltpu.VMEM((4, span, tile_width), jnp.float32),
+            pltpu.VMEM((2, span, tile_width), jnp.float32),
             pltpu.SemaphoreType.DMA((4 * len(widths),)),
         ],
         compiler_params=pltpu.CompilerParams(vmem_limit_bytes=VMEM_LIMIT),

time: 109 us -> 107 us (0.982)
  Pallas kernels: 11.2 us -> 8.27 us
    ppermute x6, waiting for transfers between devices: 8.86 us -> 3.71 us  [rotate(): lax.ppermute(value, axis, [(i, (i + offset) % size) for i in range(size)])]
    ppermute x14, waiting for transfers between devices: 48.3 us -> 53.2 us  [swap(): return lax.ppermute(value, axes, [(0, 1), (1, 0)])]
    pallas_call x1, Pallas kernels: 2.97 us -> 1.38 us  [shards(): pl.pallas_call(functools.partial(last_merge_kernel, models, tile_width, s...]
    pallas_call x9 -> x10, Pallas kernels: 8.18 us -> 6.89 us  [run(): pl.pallas_call(kernel, out_shape=out_shape, in_specs=[VMEM] * len(args) +...]
    unnamed x6 -> x8, local copies, waits for them, and re-layouts: 2.92 us -> 2.93 us
  transfers between devices with their start and end apart: 25 -> 25, of which waited for: 12 -> 14; matrix products, arithmetic and copies ran while one was open for 2% -> 2% of each run, Pallas kernels for 7% -> 6%
where the time goes in v4:
time: 107 us; the launch traced here: 106 us
  waiting for transfers between devices  61.5 us (57%)
  starting transfers between devices  31.9 us (30%)
  Pallas kernels  8.27 us (8%)
  local copies, waits for them, and re-layouts  4.68 us (4%)
    ppermute x14, waiting for transfers between devices, swap(): return lax.ppermute(value, axes, [(0, 1), (1, 0)])  53.2 us
    ppermute x14, starting transfers between devices, swap(): return lax.ppermute(value, axes, [(0, 1), (1, 0)])  21.8 us
    pallas_call x10, Pallas kernels, run(): pl.pallas_call(kernel, out_shape=out_shape, in_specs=[VMEM] * len(args) +...  6.89 us
    ppermute x4, starting transfers between devices, swap(): return lax.ppermute(value, axes, [(i, i ^ 3) for i in range(4)])  5.33 us
    ppermute x6, starting transfers between devices, rotate(): lax.ppermute(value, axis, [(i, (i + offset) % size) for i in range(size)])  4.44 us
    ppermute x4, waiting for transfers between devices, swap(): return lax.ppermute(value, axes, [(i, i ^ 3) for i in range(4)])  4.26 us
    ppermute x6, waiting for transfers between devices, rotate(): lax.ppermute(value, axis, [(i, (i + offset) % size) for i in range(size)])  3.71 us
    unnamed x8, local copies, waits for them, and re-layouts  2.93 us
  transfers between devices with their start and end apart: 25, of which 14 were waited for; matrix products, arithmetic and copies ran while one was open for 2% of the time, Pallas kernels for 6%

profile of v4, /device:TPU:0, one launch (start us, length us, event | category | flops | bytes accessed | tf_op | source)
XLA Modules:
  0.0 106.5 jit_solution(10627461342732636392)
XLA Ops:
  0.0 1.2 %copy-done.1 = bf16[1,1,128,4096]{3,2,1,0:T(8,128)(2,1)S(1)} copy-done((bf16[1,1,128,4096]{3,2,1,0:T(8,128)(2,1)S(1)}, bf16[1,1,128,4096]{3,2,1,0:T(8,128)(2,1)}, u32[]{:S(2)}) %copy-start.1) | copy-done | bytes 1048600
  1.2 1.0 copy-done.2
  2.3 0.7 copy-done.3
  2.9 0.3 shard_map.46
  3.3 4.1 %collective-permute-start.3 = (bf16[1,1024,128]{2,1,0:T(8,128)(2,1)S(1)}, bf16[1,1024,128]{2,1,0:T(8,128)(2,1)S(1)}, u32[]{:S(2)}, u32[]{:S(2)}) collective-permute-start(bf16[1,1024,128]{2,1,0:T(8,128)(2,1)S(1)} %get-tuple-element.28), channel_id=1, source_target_pairs={{0,8},{8,0},{1,9},{9,1},{2,10},{10,2},{3,11},{11,3},{4,12},{12,4},... | collective-permute-start | bytes 786440 | tf_op jit(solution)/shard_map/ppermute | solution.py:27
  7.4 1.5 %collective-permute-start.5 = (bf16[2,1,128,512]{3,2,1,0:T(8,128)(2,1)S(1)}, bf16[2,1,128,512]{3,2,1,0:T(8,128)(2,1)S(1)}, u32[]{:S(2)}, u32[]{:S(2)}) collective-permute-start(bf16[2,1,128,512]{3,2,1,0:T(8,128)(2,1)S(1)} %get-tuple-element.31), channel_id=1, source_target_pairs={{0,2},{2,0},{1,3},{3,1},{4,6},{6,4},{5,7},{7,5},{8,10},{10,8},{9,1... | collective-permute-start | bytes 786440 | tf_op jit(solution)/shard_map/ppermute | solution.py:27
  8.9 0.3 collective-permute-start.6
  9.2 1.6 %collective-permute-start.2 = (bf16[1,1024,128]{2,1,0:T(8,128)(2,1)S(1)}, bf16[1,1024,128]{2,1,0:T(8,128)(2,1)S(1)}, u32[]{:S(2)}, u32[]{:S(2)}) collective-permute-start(bf16[1,1024,128]{2,1,0:T(8,128)(2,1)S(1)} %get-tuple-element.27.refs_0_), channel_id=1, source_target_pairs={{0,4},{4,0},{1,5},{5,1},{2,6},{6,2},{3,7},{7,3},{8,12},{12,8},{9,1... | collective-permute-start | bytes 786440 | tf_op jit(solution)/shard_map/ppermute | solution.py:27
  10.8 1.8 %slice_bitcast_fusion = (f32[128,2048]{1,0:T(8,128)S(1)}, f32[128,2048]{1,0:T(8,128)S(1)}) fusion(f32[1,1,256,2048]{3,2,1,0:T(8,128)} %param.7), kind=kLoop, calls=%fused_computation | loop fusion | bytes 4194304 | tf_op jit(solution)/shard_map/slice | solution.py:238
  12.6 6.8 %collective-permute-done.3.refs_2_ = bf16[1,1024,128]{2,1,0:T(8,128)(2,1)S(1)} collective-permute-done((bf16[1,1024,128]{2,1,0:T(8,128)(2,1)S(1)}, bf16[1,1024,128]{2,1,0:T(8,128)(2,1)S(1)}, u32[]{:S(2)}, u32[]{:S(2)}) %collective-permute-start.3) | collective-permute-done | bytes 262176 | tf_op jit(solution)/shard_map/ppermute | solution.py:27
  19.4 1.5 %collective-permute-start = (f32[128,2048]{1,0:T(8,128)S(1)}, f32[128,2048]{1,0:T(8,128)S(1)}, u32[]{:S(2)}, u32[]{:S(2)}) collective-permute-start(f32[128,2048]{1,0:T(8,128)S(1)} %get-tuple-element.50), channel_id=1, source_target_pairs={{0,16},{16,0},{1,17},{17,1},{2,18},{18,2},{3,19},{19,3},{4,20},{20... | collective-permute-start | bytes 3145736 | tf_op jit(solution)/shard_map/ppermute | solution.py:33
  20.9 0.4 collective-permute-done.6.refs_6_.refs_5_
  21.3 0.9 collective-permute-done.2.refs_1_
  22.2 0.1 shard_map.47
  22.3 1.6 %collective-permute-start.8 = (bf16[3,1024,128]{2,1,0:T(8,128)(2,1)S(1)}, bf16[3,1024,128]{2,1,0:T(8,128)(2,1)S(1)}, u32[]{:S(2)}, u32[]{:S(2)}) collective-permute-start(bf16[3,1024,128]{2,1,0:T(8,128)(2,1)S(1)} %get-tuple-element.33.refs_0_), channel_id=1, source_target_pairs={{0,2},{2,0},{1,3},{3,1},{4,6},{6,4},{5,7},{7,5},{8,10},{10,8},{9,1... | collective-permute-start | bytes 2359304 | tf_op jit(solution)/shard_map/ppermute | solution.py:27
  24.0 0.7 collective-permute-start.7
  24.6 2.3 %collective-permute-start.10 = (bf16[4,128,256]{2,1,0:T(8,128)(2,1)S(1)}, bf16[4,128,256]{2,1,0:T(8,128)(2,1)S(1)}, u32[]{:S(2)}, u32[]{:S(2)}) collective-permute-start(bf16[4,128,256]{2,1,0:T(8,128)(2,1)S(1)} %get-tuple-element.37.refs_2_), channel_id=1, source_target_pairs={{0,8},{8,0},{1,9},{9,1},{2,10},{10,2},{3,11},{11,3},{4,12},{12,4},... | collective-permute-start | bytes 786440 | tf_op jit(solution)/shard_map/ppermute | solution.py:27
  26.9 1.5 %collective-permute-start.12 = (bf16[4,128,256]{2,1,0:T(8,128)(2,1)S(1)}, bf16[4,128,256]{2,1,0:T(8,128)(2,1)S(1)}, u32[]{:S(2)}, u32[]{:S(2)}) collective-permute-start(bf16[4,128,256]{2,1,0:T(8,128)(2,1)S(1)} %get-tuple-element.38), channel_id=1, source_target_pairs={{0,12},{4,8},{8,4},{12,0},{1,13},{5,9},{9,5},{13,1},{2,14},{6,10},... | collective-permute-start | bytes 786440 | tf_op jit(solution)/shard_map/ppermute | solution.py:28
  28.3 7.5 %collective-permute-done.7.refs_1_ = bf16[1,1024,128]{2,1,0:T(8,128)(2,1)S(1)} collective-permute-done((bf16[1,1024,128]{2,1,0:T(8,128)(2,1)S(1)}, bf16[1,1024,128]{2,1,0:T(8,128)(2,1)S(1)}, u32[]{:S(2)}, u32[]{:S(2)}) %collective-permute-start.7) | collective-permute-done | bytes 262176 | tf_op jit(solution)/shard_map/ppermute | solution.py:27
  35.8 0.1 shard_map.48
  35.9 10.1 %collective-permute-done.10.refs_3_.refs_4_ = bf16[4,128,256]{2,1,0:T(8,128)(2,1)S(1)} collective-permute-done((bf16[4,128,256]{2,1,0:T(8,128)(2,1)S(1)}, bf16[4,128,256]{2,1,0:T(8,128)(2,1)S(1)}, u32[]{:S(2)}, u32[]{:S(2)}) %collective-permute-start.10) | collective-permute-done | bytes 262176 | tf_op jit(solution)/shard_map/ppermute | solution.py:27
  46.0 0.5 collective-permute-start.9
  46.5 2.5 %collective-permute-done.11.refs_4_.refs_3_ = bf16[4,128,256]{2,1,0:T(8,128)(2,1)S(1)} collective-permute-done((bf16[4,128,256]{2,1,0:T(8,128)(2,1)S(1)}, bf16[4,128,256]{2,1,0:T(8,128)(2,1)S(1)}, u32[]{:S(2)}, u32[]{:S(2)}) %collective-permute-start.11) | collective-permute-done | bytes 262176 | tf_op jit(solution)/shard_map/ppermute | solution.py:27
  49.1 3.3 %collective-permute-done.9.refs_2_ = bf16[1,1024,128]{2,1,0:T(8,128)(2,1)S(1)} collective-permute-done((bf16[1,1024,128]{2,1,0:T(8,128)(2,1)S(1)}, bf16[1,1024,128]{2,1,0:T(8,128)(2,1)S(1)}, u32[]{:S(2)}, u32[]{:S(2)}) %collective-permute-start.9) | collective-permute-done | bytes 262176 | tf_op jit(solution)/shard_map/ppermute | solution.py:27
  52.4 0.1 shard_map.49.refs_0_
  52.6 1.6 %collective-permute-start.1 = (f32[128,2048]{1,0:T(8,128)S(1)}, f32[128,2048]{1,0:T(8,128)S(1)}, u32[]{:S(2)}, u32[]{:S(2)}) collective-permute-start(f32[128,2048]{1,0:T(8,128)S(1)} %get-tuple-element.49), channel_id=1, source_target_pairs={{0,16},{16,0},{1,17},{17,1},{2,18},{18,2},{3,19},{19,3},{4,20},{20... | collective-permute-start | bytes 3145736 | tf_op jit(solution)/shard_map/ppermute | solution.py:33
  54.2 1.7 %collective-permute-start.16 = (bf16[4,128,256]{2,1,0:T(8,128)(2,1)S(1)}, bf16[4,128,256]{2,1,0:T(8,128)(2,1)S(1)}, u32[]{:S(2)}, u32[]{:S(2)}) collective-permute-start(bf16[4,128,256]{2,1,0:T(8,128)(2,1)S(1)} %get-tuple-element.40), channel_id=1, source_target_pairs={{0,12},{4,8},{8,4},{12,0},{1,13},{5,9},{9,5},{13,1},{2,14},{6,10},... | collective-permute-start | bytes 786440 | tf_op jit(solution)/shard_map/ppermute | solution.py:28
  55.9 1.8 %collective-permute-start.14 = (bf16[4,128,256]{2,1,0:T(8,128)(2,1)S(1)}, bf16[4,128,256]{2,1,0:T(8,128)(2,1)S(1)}, u32[]{:S(2)}, u32[]{:S(2)}) collective-permute-start(bf16[4,128,256]{2,1,0:T(8,128)(2,1)S(1)} %get-tuple-element.40), channel_id=1, source_target_pairs={{0,4},{4,0},{1,5},{5,1},{2,6},{6,2},{3,7},{7,3},{8,12},{12,8},{9,1... | collective-permute-start | bytes 786440 | tf_op jit(solution)/shard_map/ppermute | solution.py:27
  57.7 2.6 %shard_map.52.refs_0_ = s16[4,256,256]{2,1,0:T(8,128)(2,1)S(1)} custom-call(bf16[8,1024,128]{2,1,0:T(8,128)(2,1)S(1)} %shard_map.49.refs_0_, bf16[8,1024,128]{2,1,0:T(8,128)(2,1)S(1)} %collective-permute-done.13.refs_1_, bf16[4,128,256]{2,1,0:T(8,128)(2,1)S(1)} %get-tuple-element.37.refs_2_, ...), custom_call_target="tpu_custom_call" | custom-call | flops 1073741824 | bytes 5242880 | tf_op jit(solution)/shard_map/pallas_call | solution.py:41
  60.3 0.7 collective-permute-start.21
  60.9 12.9 %collective-permute-done.15.refs_4_ = bf16[4,128,256]{2,1,0:T(8,128)(2,1)S(1)} collective-permute-done((bf16[4,128,256]{2,1,0:T(8,128)(2,1)S(1)}, bf16[4,128,256]{2,1,0:T(8,128)(2,1)S(1)}, u32[]{:S(2)}, u32[]{:S(2)}) %collective-permute-start.15) | collective-permute-done | bytes 262176 | tf_op jit(solution)/shard_map/ppermute | solution.py:27
  73.9 1.3 %collective-permute-done.14.refs_3_ = bf16[4,128,256]{2,1,0:T(8,128)(2,1)S(1)} collective-permute-done((bf16[4,128,256]{2,1,0:T(8,128)(2,1)S(1)}, bf16[4,128,256]{2,1,0:T(8,128)(2,1)S(1)}, u32[]{:S(2)}, u32[]{:S(2)}) %collective-permute-start.14) | collective-permute-done | bytes 262176 | tf_op jit(solution)/shard_map/ppermute | solution.py:27
  75.2 2.6 %shard_map.50 = (s16[256,256]{1,0:T(8,128)(2,1)S(1)}, s16[256,256]{1,0:T(8,128)(2,1)S(1)}, s16[256,256]{1,0:T(8,128)(2,1)S(1)}, s16[256,256]{1,0:T(8,128)(2,1)S(1)}) custom-call(bf16[8,1024,128]{2,1,0:T(8,128)(2,1)S(1)} %shard_map.49.refs_0_, bf16[8,1024,128]{2,1,0:T(8,128)(2,1)S(1)} %collective-permute-done.13.refs_1_, ...), custom_call_target="tpu_custom_call" | custom-call | flops 1073741824 | bytes 5242880 | tf_op jit(solution)/shard_map/pallas_call | solution.py:41
  77.8 0.6 collective-permute-start.17
  78.4 4.8 %collective-permute-start.18 = (s16[256,256]{1,0:T(8,128)(2,1)S(1)}, s16[256,256]{1,0:T(8,128)(2,1)S(1)}, u32[]{:S(2)}, u32[]{:S(2)}) collective-permute-start(s16[256,256]{1,0:T(8,128)(2,1)S(1)} %get-tuple-element.43), channel_id=1, source_target_pairs={{0,4},{4,0},{1,5},{5,1},{2,6},{6,2},{3,7},{7,3},{8,12},{12,8},{9,1... | collective-permute-start | bytes 393224 | tf_op jit(solution)/shard_map/ppermute | solution.py:27
  83.2 0.9 collective-permute-start.19
  84.1 3.0 %collective-permute-done.18.refs_2_ = s16[256,256]{1,0:T(8,128)(2,1)S(1)} collective-permute-done((s16[256,256]{1,0:T(8,128)(2,1)S(1)}, s16[256,256]{1,0:T(8,128)(2,1)S(1)}, u32[]{:S(2)}, u32[]{:S(2)}) %collective-permute-start.18) | collective-permute-done | bytes 131104 | tf_op jit(solution)/shard_map/ppermute | solution.py:27
  87.1 3.3 %collective-permute-done.19.refs_3_ = s16[256,256]{1,0:T(8,128)(2,1)S(1)} collective-permute-done((s16[256,256]{1,0:T(8,128)(2,1)S(1)}, s16[256,256]{1,0:T(8,128)(2,1)S(1)}, u32[]{:S(2)}, u32[]{:S(2)}) %collective-permute-start.19) | collective-permute-done | bytes 131104 | tf_op jit(solution)/shard_map/ppermute | solution.py:28
  90.4 0.6 collective-permute-start.20
  91.1 0.6 collective-permute-start.22
  91.7 1.7 %collective-permute-start.23 = (s16[2,256,256]{2,1,0:T(8,128)(2,1)S(1)}, s16[2,256,256]{2,1,0:T(8,128)(2,1)S(1)}, u32[]{:S(2)}, u32[]{:S(2)}) collective-permute-start(s16[2,256,256]{2,1,0:T(8,128)(2,1)S(1)} %get-tuple-element.47), channel_id=1, source_target_pairs={{0,4},{4,0},{1,5},{5,1},{2,6},{6,2},{3,7},{7,3},{8,12},{12,8},{9,1... | collective-permute-start | bytes 786440 | tf_op jit(solution)/shard_map/ppermute | solution.py:27
  93.4 1.2 %collective-permute-start.24 = (s16[2,256,256]{2,1,0:T(8,128)(2,1)S(1)}, s16[2,256,256]{2,1,0:T(8,128)(2,1)S(1)}, u32[]{:S(2)}, u32[]{:S(2)}) collective-permute-start(s16[2,256,256]{2,1,0:T(8,128)(2,1)S(1)} %get-tuple-element.48), channel_id=1, source_target_pairs={{0,6},{2,4},{4,2},{6,0},{1,7},{3,5},{5,3},{7,1},{8,14},{10,12},{12... | collective-permute-start | bytes 786440 | tf_op jit(solution)/shard_map/ppermute | solution.py:28
  94.6 4.8 %collective-permute-done.22.refs_4_ = s16[2,256,256]{2,1,0:T(8,128)(2,1)S(1)} collective-permute-done((s16[2,256,256]{2,1,0:T(8,128)(2,1)S(1)}, s16[2,256,256]{2,1,0:T(8,128)(2,1)S(1)}, u32[]{:S(2)}, u32[]{:S(2)}) %collective-permute-start.22) | collective-permute-done | bytes 262176 | tf_op jit(solution)/shard_map/ppermute | solution.py:27
  99.5 0.3 shard_map.54.refs_5_.refs_1_
  99.8 3.7 %collective-permute-done.20.refs_4_ = s16[4,256,256]{2,1,0:T(8,128)(2,1)S(1)} collective-permute-done((s16[4,256,256]{2,1,0:T(8,128)(2,1)S(1)}, s16[4,256,256]{2,1,0:T(8,128)(2,1)S(1)}, u32[]{:S(2)}, u32[]{:S(2)}) %collective-permute-start.20) | collective-permute-done | bytes 524320 | tf_op jit(solution)/shard_map/ppermute | solution.py:33
  103.5 0.6 shard_map.55.refs_0_
  104.1 1.0 collective-permute-done.24.refs_6_
  105.1 1.4 %shard_map.56 = f32[256,2048]{1,0:T(8,128)} custom-call(f32[4,256,256]{2,1,0:T(8,128)S(1)} %shard_map.55.refs_0_, f32[2,256,256]{2,1,0:T(8,128)S(1)} %shard_map.54.refs_5_.refs_1_, f32[256,2048]{1,0:T(8,128)S(1)} %bitcast.11, f32[128,2048]{1,0:T(8,128)S(1)} %collective-permute-done.refs_6_.refs_1_.refs_3_, ...), custom_call_target="tpu_custom_call" | custom-call | tf_op jit(solution)/shard_map/pallas_call | solution.py:343
  (22 shorter events, 0.2 us)
Async XLA Ops:
  0.0 1.2 %copy-start.1 = (bf16[1,1,128,4096]{3,2,1,0:T(8,128)(2,1)S(1)}, bf16[1,1,128,4096]{3,2,1,0:T(8,128)(2,1)}, u32[]{:S(2)}) copy-start(bf16[1,1,128,4096]{3,2,1,0:T(8,128)(2,1)} %param.5) | copy-start | bytes 3145732
  1.2 1.0 copy-start.2
  2.3 0.7 copy-start.3
  3.3 16.1 %collective-permute-start.3 = (bf16[1,1024,128]{2,1,0:T(8,128)(2,1)S(1)}, bf16[1,1024,128]{2,1,0:T(8,128)(2,1)S(1)}, u32[]{:S(2)}, u32[]{:S(2)}) collective-permute-start(bf16[1,1024,128]{2,1,0:T(8,128)(2,1)S(1)} %get-tuple-element.28), channel_id=1, source_target_pairs={{0,8},{8,0},{1,9},{9,1},{2,10},{10,2},{3,11},{11,3},{4,12},{12,4},... | collective-permute-start | bytes 786440 | tf_op jit(solution)/shard_map/ppermute | solution.py:27
  7.4 13.6 %collective-permute-start.4 = (bf16[2,1,128,512]{3,2,1,0:T(8,128)(2,1)S(1)}, bf16[2,1,128,512]{3,2,1,0:T(8,128)(2,1)S(1)}, u32[]{:S(2)}, u32[]{:S(2)}) collective-permute-start(bf16[2,1,128,512]{3,2,1,0:T(8,128)(2,1)S(1)} %get-tuple-element.30), channel_id=1, source_target_pairs={{0,1},{1,0},{2,3},{3,2},{4,5},{5,4},{6,7},{7,6},{8,9},{9,8},{10,11... | collective-permute-start | bytes 786440 | tf_op jit(solution)/shard_map/ppermute | solution.py:33
  7.4 13.6 %collective-permute-start.5 = (bf16[2,1,128,512]{3,2,1,0:T(8,128)(2,1)S(1)}, bf16[2,1,128,512]{3,2,1,0:T(8,128)(2,1)S(1)}, u32[]{:S(2)}, u32[]{:S(2)}) collective-permute-start(bf16[2,1,128,512]{3,2,1,0:T(8,128)(2,1)S(1)} %get-tuple-element.31), channel_id=1, source_target_pairs={{0,2},{2,0},{1,3},{3,1},{4,6},{6,4},{5,7},{7,5},{8,10},{10,8},{9,1... | collective-permute-start | bytes 786440 | tf_op jit(solution)/shard_map/ppermute | solution.py:27
  8.9 12.4 %collective-permute-start.6 = (bf16[2,1,128,512]{3,2,1,0:T(8,128)(2,1)S(1)}, bf16[2,1,128,512]{3,2,1,0:T(8,128)(2,1)S(1)}, u32[]{:S(2)}, u32[]{:S(2)}) collective-permute-start(bf16[2,1,128,512]{3,2,1,0:T(8,128)(2,1)S(1)} %get-tuple-element.32), channel_id=1, source_target_pairs={{0,3},{1,2},{2,1},{3,0},{4,7},{5,6},{6,5},{7,4},{8,11},{9,10},{10,... | collective-permute-start | bytes 786440 | tf_op jit(solution)/shard_map/ppermute | solution.py:255
  9.2 12.9 %collective-permute-start.2 = (bf16[1,1024,128]{2,1,0:T(8,128)(2,1)S(1)}, bf16[1,1024,128]{2,1,0:T(8,128)(2,1)S(1)}, u32[]{:S(2)}, u32[]{:S(2)}) collective-permute-start(bf16[1,1024,128]{2,1,0:T(8,128)(2,1)S(1)} %get-tuple-element.27.refs_0_), channel_id=1, source_target_pairs={{0,4},{4,0},{1,5},{5,1},{2,6},{6,2},{3,7},{7,3},{8,12},{12,8},{9,1... | collective-permute-start | bytes 786440 | tf_op jit(solution)/shard_map/ppermute | solution.py:27
  19.4 33.0 %collective-permute-start = (f32[128,2048]{1,0:T(8,128)S(1)}, f32[128,2048]{1,0:T(8,128)S(1)}, u32[]{:S(2)}, u32[]{:S(2)}) collective-permute-start(f32[128,2048]{1,0:T(8,128)S(1)} %get-tuple-element.50), channel_id=1, source_target_pairs={{0,16},{16,0},{1,17},{17,1},{2,18},{18,2},{3,19},{19,3},{4,20},{20... | collective-permute-start | bytes 3145736 | tf_op jit(solution)/shard_map/ppermute | solution.py:33
  22.3 30.1 %collective-permute-start.8 = (bf16[3,1024,128]{2,1,0:T(8,128)(2,1)S(1)}, bf16[3,1024,128]{2,1,0:T(8,128)(2,1)S(1)}, u32[]{:S(2)}, u32[]{:S(2)}) collective-permute-start(bf16[3,1024,128]{2,1,0:T(8,128)(2,1)S(1)} %get-tuple-element.33.refs_0_), channel_id=1, source_target_pairs={{0,2},{2,0},{1,3},{3,1},{4,6},{6,4},{5,7},{7,5},{8,10},{10,8},{9,1... | collective-permute-start | bytes 2359304 | tf_op jit(solution)/shard_map/ppermute | solution.py:27
  24.0 11.8 %collective-permute-start.7 = (bf16[1,1024,128]{2,1,0:T(8,128)(2,1)S(1)}, bf16[1,1024,128]{2,1,0:T(8,128)(2,1)S(1)}, u32[]{:S(2)}, u32[]{:S(2)}) collective-permute-start(bf16[1,1024,128]{2,1,0:T(8,128)(2,1)S(1)} %get-tuple-element.34), channel_id=1, source_target_pairs={{0,4},{4,0},{1,5},{5,1},{2,6},{6,2},{3,7},{7,3},{8,12},{12,8},{9,1... | collective-permute-start | bytes 786440 | tf_op jit(solution)/shard_map/ppermute | solution.py:27
  24.6 21.4 %collective-permute-start.10 = (bf16[4,128,256]{2,1,0:T(8,128)(2,1)S(1)}, bf16[4,128,256]{2,1,0:T(8,128)(2,1)S(1)}, u32[]{:S(2)}, u32[]{:S(2)}) collective-permute-start(bf16[4,128,256]{2,1,0:T(8,128)(2,1)S(1)} %get-tuple-element.37.refs_2_), channel_id=1, source_target_pairs={{0,8},{8,0},{1,9},{9,1},{2,10},{10,2},{3,11},{11,3},{4,12},{12,4},... | collective-permute-start | bytes 786440 | tf_op jit(solution)/shard_map/ppermute | solution.py:27
  26.9 19.7 %collective-permute-start.12 = (bf16[4,128,256]{2,1,0:T(8,128)(2,1)S(1)}, bf16[4,128,256]{2,1,0:T(8,128)(2,1)S(1)}, u32[]{:S(2)}, u32[]{:S(2)}) collective-permute-start(bf16[4,128,256]{2,1,0:T(8,128)(2,1)S(1)} %get-tuple-element.38), channel_id=1, source_target_pairs={{0,12},{4,8},{8,4},{12,0},{1,13},{5,9},{9,5},{13,1},{2,14},{6,10},... | collective-permute-start | bytes 786440 | tf_op jit(solution)/shard_map/ppermute | solution.py:28
  35.8 13.3 %collective-permute-start.11 = (bf16[4,128,256]{2,1,0:T(8,128)(2,1)S(1)}, bf16[4,128,256]{2,1,0:T(8,128)(2,1)S(1)}, u32[]{:S(2)}, u32[]{:S(2)}) collective-permute-start(bf16[4,128,256]{2,1,0:T(8,128)(2,1)S(1)} %get-tuple-element.38), channel_id=1, source_target_pairs={{0,4},{4,0},{1,5},{5,1},{2,6},{6,2},{3,7},{7,3},{8,12},{12,8},{9,1... | collective-permute-start | bytes 786440 | tf_op jit(solution)/shard_map/ppermute | solution.py:27
  46.0 6.4 %collective-permute-start.9 = (bf16[1,1024,128]{2,1,0:T(8,128)(2,1)S(1)}, bf16[1,1024,128]{2,1,0:T(8,128)(2,1)S(1)}, u32[]{:S(2)}, u32[]{:S(2)}) collective-permute-start(bf16[1,1024,128]{2,1,0:T(8,128)(2,1)S(1)} %get-tuple-element.36), channel_id=1, source_target_pairs={{0,2},{2,0},{1,3},{3,1},{4,6},{6,4},{5,7},{7,5},{8,10},{10,8},{9,1... | collective-permute-start | bytes 786440 | tf_op jit(solution)/shard_map/ppermute | solution.py:27
  52.5 5.1 %collective-permute-start.13 = (bf16[8,1024,128]{2,1,0:T(8,128)(2,1)S(1)}, bf16[8,1024,128]{2,1,0:T(8,128)(2,1)S(1)}, u32[]{:S(2)}, u32[]{:S(2)}) collective-permute-start(bf16[8,1024,128]{2,1,0:T(8,128)(2,1)S(1)} %shard_map.49.refs_0_), channel_id=1, source_target_pairs={{0,1},{1,0},{2,3},{3,2},{4,5},{5,4},{6,7},{7,6},{8,9},{9,8},{10,11... | collective-permute-start | bytes 6291464 | tf_op jit(solution)/shard_map/ppermute | solution.py:33
  52.6 38.4 %collective-permute-start.1 = (f32[128,2048]{1,0:T(8,128)S(1)}, f32[128,2048]{1,0:T(8,128)S(1)}, u32[]{:S(2)}, u32[]{:S(2)}) collective-permute-start(f32[128,2048]{1,0:T(8,128)S(1)} %get-tuple-element.49), channel_id=1, source_target_pairs={{0,16},{16,0},{1,17},{17,1},{2,18},{18,2},{3,19},{19,3},{4,20},{20... | collective-permute-start | bytes 3145736 | tf_op jit(solution)/shard_map/ppermute | solution.py:33
  54.2 19.7 %collective-permute-start.15 = (bf16[4,128,256]{2,1,0:T(8,128)(2,1)S(1)}, bf16[4,128,256]{2,1,0:T(8,128)(2,1)S(1)}, u32[]{:S(2)}, u32[]{:S(2)}) collective-permute-start(bf16[4,128,256]{2,1,0:T(8,128)(2,1)S(1)} %get-tuple-element.39.refs_2_), channel_id=1, source_target_pairs={{0,8},{8,0},{1,9},{9,1},{2,10},{10,2},{3,11},{11,3},{4,12},{12,4},... | collective-permute-start | bytes 786440 | tf_op jit(solution)/shard_map/ppermute | solution.py:27
  54.2 19.7 %collective-permute-start.16 = (bf16[4,128,256]{2,1,0:T(8,128)(2,1)S(1)}, bf16[4,128,256]{2,1,0:T(8,128)(2,1)S(1)}, u32[]{:S(2)}, u32[]{:S(2)}) collective-permute-start(bf16[4,128,256]{2,1,0:T(8,128)(2,1)S(1)} %get-tuple-element.40), channel_id=1, source_target_pairs={{0,12},{4,8},{8,4},{12,0},{1,13},{5,9},{9,5},{13,1},{2,14},{6,10},... | collective-permute-start | bytes 786440 | tf_op jit(solution)/shard_map/ppermute | solution.py:28
  55.9 19.3 %collective-permute-start.14 = (bf16[4,128,256]{2,1,0:T(8,128)(2,1)S(1)}, bf16[4,128,256]{2,1,0:T(8,128)(2,1)S(1)}, u32[]{:S(2)}, u32[]{:S(2)}) collective-permute-start(bf16[4,128,256]{2,1,0:T(8,128)(2,1)S(1)} %get-tuple-element.40), channel_id=1, source_target_pairs={{0,4},{4,0},{1,5},{5,1},{2,6},{6,2},{3,7},{7,3},{8,12},{12,8},{9,1... | collective-permute-start | bytes 786440 | tf_op jit(solution)/shard_map/ppermute | solution.py:27
  60.3 30.7 %collective-permute-start.21 = (s16[4,256,256]{2,1,0:T(8,128)(2,1)S(1)}, s16[4,256,256]{2,1,0:T(8,128)(2,1)S(1)}, u32[]{:S(2)}, u32[]{:S(2)}) collective-permute-start(s16[4,256,256]{2,1,0:T(8,128)(2,1)S(1)} %shard_map.52.refs_0_), channel_id=1, source_target_pairs={{0,16},{16,0},{1,17},{17,1},{2,18},{18,2},{3,19},{19,3},{4,20},{20... | collective-permute-start | bytes 1572872 | tf_op jit(solution)/shard_map/ppermute | solution.py:33
  77.8 21.7 %copy-start = (f32[1,1,256,2048]{3,2,1,0:T(8,128)S(1)}, f32[1,1,256,2048]{3,2,1,0:T(8,128)}, u32[]{:S(2)}) copy-start(f32[1,1,256,2048]{3,2,1,0:T(8,128)} %param.7) | copy-start | bytes 6291460
  77.8 6.3 %collective-permute-start.17 = (s16[256,256]{1,0:T(8,128)(2,1)S(1)}, s16[256,256]{1,0:T(8,128)(2,1)S(1)}, u32[]{:S(2)}, u32[]{:S(2)}) collective-permute-start(s16[256,256]{1,0:T(8,128)(2,1)S(1)} %get-tuple-element.42), channel_id=1, source_target_pairs={{0,2},{2,0},{1,3},{3,1},{4,6},{6,4},{5,7},{7,5},{8,10},{10,8},{9,1... | collective-permute-start | bytes 393224 | tf_op jit(solution)/shard_map/ppermute | solution.py:27
  78.4 8.7 %collective-permute-start.18 = (s16[256,256]{1,0:T(8,128)(2,1)S(1)}, s16[256,256]{1,0:T(8,128)(2,1)S(1)}, u32[]{:S(2)}, u32[]{:S(2)}) collective-permute-start(s16[256,256]{1,0:T(8,128)(2,1)S(1)} %get-tuple-element.43), channel_id=1, source_target_pairs={{0,4},{4,0},{1,5},{5,1},{2,6},{6,2},{3,7},{7,3},{8,12},{12,8},{9,1... | collective-permute-start | bytes 393224 | tf_op jit(solution)/shard_map/ppermute | solution.py:27
  83.2 7.2 %collective-permute-start.19 = (s16[256,256]{1,0:T(8,128)(2,1)S(1)}, s16[256,256]{1,0:T(8,128)(2,1)S(1)}, u32[]{:S(2)}, u32[]{:S(2)}) collective-permute-start(s16[256,256]{1,0:T(8,128)(2,1)S(1)} %get-tuple-element.44), channel_id=1, source_target_pairs={{0,6},{2,4},{4,2},{6,0},{1,7},{3,5},{5,3},{7,1},{8,14},{10,12},{12... | collective-permute-start | bytes 393224 | tf_op jit(solution)/shard_map/ppermute | solution.py:28
  90.4 13.1 %collective-permute-start.20 = (s16[4,256,256]{2,1,0:T(8,128)(2,1)S(1)}, s16[4,256,256]{2,1,0:T(8,128)(2,1)S(1)}, u32[]{:S(2)}, u32[]{:S(2)}) collective-permute-start(s16[4,256,256]{2,1,0:T(8,128)(2,1)S(1)} %shard_map.51.refs_3_), channel_id=1, source_target_pairs={{0,16},{16,0},{1,17},{17,1},{2,18},{18,2},{3,19},{19,3},{4,20},{20... | collective-permute-start | bytes 1572872 | tf_op jit(solution)/shard_map/ppermute | solution.py:33
  91.1 8.4 %collective-permute-start.22 = (s16[2,256,256]{2,1,0:T(8,128)(2,1)S(1)}, s16[2,256,256]{2,1,0:T(8,128)(2,1)S(1)}, u32[]{:S(2)}, u32[]{:S(2)}) collective-permute-start(s16[2,256,256]{2,1,0:T(8,128)(2,1)S(1)} %get-tuple-element.46), channel_id=1, source_target_pairs={{0,2},{2,0},{1,3},{3,1},{4,6},{6,4},{5,7},{7,5},{8,10},{10,8},{9,1... | collective-permute-start | bytes 786440 | tf_op jit(solution)/shard_map/ppermute | solution.py:27
  91.7 12.4 %collective-permute-start.23 = (s16[2,256,256]{2,1,0:T(8,128)(2,1)S(1)}, s16[2,256,256]{2,1,0:T(8,128)(2,1)S(1)}, u32[]{:S(2)}, u32[]{:S(2)}) collective-permute-start(s16[2,256,256]{2,1,0:T(8,128)(2,1)S(1)} %get-tuple-element.47), channel_id=1, source_target_pairs={{0,4},{4,0},{1,5},{5,1},{2,6},{6,2},{3,7},{7,3},{8,12},{12,8},{9,1... | collective-permute-start | bytes 786440 | tf_op jit(solution)/shard_map/ppermute | solution.py:27
  93.4 11.7 %collective-permute-start.24 = (s16[2,256,256]{2,1,0:T(8,128)(2,1)S(1)}, s16[2,256,256]{2,1,0:T(8,128)(2,1)S(1)}, u32[]{:S(2)}, u32[]{:S(2)}) collective-permute-start(s16[2,256,256]{2,1,0:T(8,128)(2,1)S(1)} %get-tuple-element.48), channel_id=1, source_target_pairs={{0,6},{2,4},{4,2},{6,0},{1,7},{3,5},{5,3},{7,1},{8,14},{10,12},{12... | collective-permute-start | bytes 786440 | tf_op jit(solution)/shard_map/ppermute | solution.py:28

commit v5 on v4

--- a/solution.py
+++ b/solution.py
@@ -58,19 +58,24 @@
         for s in range(inputs_ref.shape[0]):
             start = pl.multiple_of(part * half, half)
             ref[s] = inputs_ref[s, :, pl.ds(start, half)].T
-    seqs, length, width = ids_ref.shape[0], cot_ref.shape[1], outs[0].shape[3]
-    core_count = len(outs) // 2
+    core_count, _, seqs, length, width = outs[0].shape
     own_y, own_c = lax.axis_index("y"), lax.axis_index("c")
     for s in range(seqs):
         kept = jnp.broadcast_to((ids_ref[s : s + 1, :] >= FIRST_TEXT).astype(jnp.float32), (128, length)).T
         kept = kept[:, :1] > 0.5
-        for at, ref in enumerate(outs):
-            to_y = own_y ^ (at // core_count)
-            to_c = lax.rem(own_c + at % core_count, core_count)
-            for zl in range(2):
-                start = pl.multiple_of(((to_c * 2 + zl) * 2 + to_y) * width, width)
-                piece = cot_ref[s, :, pl.ds(start, width)]
-                ref[zl, s] = jnp.where(kept, piece, jnp.zeros_like(piece))
+        for dy, ref in enumerate(outs):
+            for dc in range(core_count):
+                to_c = lax.rem(own_c + dc, core_count)
+                for zl in range(2):
+                    start = pl.multiple_of(((to_c * 2 + zl) * 2 + (own_y ^ dy)) * width, width)
+                    piece = cot_ref[s, :, pl.ds(start, width)]
+                    ref[dc, zl, s] = jnp.where(kept, piece, jnp.zeros_like(piece))
+
+
+def core_kernel(here, there, *outs):
+    for at, out in enumerate(outs):
+        out[0] = here[at]
+        out[1] = there[at]
 
 
 def fill(out, *refs):
@@ -81,11 +86,13 @@
 
 
 def pack(start, own_ref, other_ref, sources):
-    own, width = lax.axis_index("zl"), other_ref.shape[2]
+    own, width, seqs = lax.axis_index("zl"), other_ref.shape[2], sources[0].shape[2]
     for which, ref in enumerate((own_ref, other_ref)):
-        for i, source in enumerate(sources):
-            seqs = source.shape[1]
-            ref[i * seqs : (i + 1) * seqs] = source[own ^ which, :, :, start : start + width]
+        at = 0
+        for dy in range(2):
+            for source in sources:
+                ref[at : at + seqs] = source[dy, own ^ which, :, :, start : start + width]
+                at += seqs
 
 
 def gather_kernel(keep, z1, z2, *refs):
@@ -137,58 +144,64 @@
             outs[at][...] = code
 
 
-def models_kernel(models, *refs):
+def pick(values, j):
+    own, models = lax.axis_index("mp"), len(values)
+    chosen = values[0]
+    for offset in range(1, models):
+        chosen = jnp.where(lax.rem(own + models - offset, models) == j, values[offset], chosen)
+    return chosen
+
+
+def code_steps(codes, j):
+    whole = [code.astype(jnp.int32) for code in codes]
+    return (pick(whole, j) - pick(whole, 0)).astype(jnp.float32)
+
+
+def steps_kernel(models, *refs):
     for at, out in enumerate(refs[models:]):
-        for m in range(models):
-            out[m] = refs[m][at]
-
-
-def merge_chunk(senders, models, tile_width, first, width, code_scale, weights, codes, store):
-    own_zl, own_y, own_m = lax.axis_index("zl"), lax.axis_index("y"), lax.axis_index("mp")
-
-    def pick(values, j):
-        chosen = values[0]
-        for offset in range(1, models):
-            chosen = jnp.where(lax.rem(own_m + models - offset, models) == j, values[offset], chosen)
-        return chosen
-
+        for j in range(1, models):
+            steps = jnp.round(code_steps([ref[at] for ref in refs[:models]], j) * 0.5)
+            out[j - 1] = jnp.clip(steps, -32768.0, 32767.0).astype(jnp.int32).astype(jnp.int16)
+
+
+def merge_chunk(senders, models, tile_width, first, width, code_scale, weights, steps, store):
+    own_zl, own_y = lax.axis_index("zl"), lax.axis_index("y")
     for at in senders:
         sub = (own_zl ^ (at // 2)) * 2 + (own_y ^ (at % 2))
         start = pl.multiple_of(sub * tile_width + first, 128)
-        codes_here = [codes(m, at).astype(jnp.int32) for m in range(models)]
-        weights_here = [weights[0][:, pl.ds(start, width)]]
-        for m in range(1, models):
-            halves = [half[:, pl.ds(start, width)] for half in weights[2 * m - 1 : 2 * m + 1]]
-            weights_here.append(jnp.concatenate(halves, axis=0))
-        base = pick(codes_here, 0)
+        weights_here = [weight[:, pl.ds(start, width)] for weight in weights]
         num, den = pick(weights_here, 0), None
         for j in range(1, models):
-            ratio = jnp.exp((pick(codes_here, j) - base).astype(jnp.float32) * (1.0 / code_scale))
+            ratio = jnp.exp(steps(at, j) * (1.0 / code_scale))
             num = num + ratio * pick(weights_here, j)
             den = 1.0 + ratio if den is None else den + ratio
         store(at, start, num if den is None else num / den)
 
 
+def two_steps(value):
+    return value.astype(jnp.int32).astype(jnp.float32) * 2.0
+
+
 def early_merge_kernel(models, tile_width, first, width, code_scale, *refs):
     def store(at, start, value):
         refs[-1][at] = value
 
-    weights, codes = refs[: 2 * models - 1], refs[2 * models - 1 : -1]
-    merge_chunk(range(4), models, tile_width, first, width, code_scale, weights, lambda m, at: codes[m][at], store)
+    weights, codes = refs[:models], refs[models:-1]
+    merge_chunk(range(4), models, tile_width, first, width, code_scale, weights, lambda at, j: code_steps([code[at] for code in codes], j), store)
 
 
 def near_merge_kernel(models, tile_width, first, width, code_scale, *refs):
     def store(at, start, value):
         refs[-1][at] = value
 
-    weights, codes = refs[: 2 * models - 1], refs[2 * models - 1 : -1]
-    merge_chunk(range(2), models, tile_width, first, width, code_scale, weights, lambda m, at: codes[at][m], store)
+    weights, codes = refs[:models], refs[models:-1]
+    merge_chunk(range(2), models, tile_width, first, width, code_scale, weights, lambda at, j: two_steps(codes[at][j - 1]), store)
 
 
 def last_merge_kernel(models, tile_width, firsts, widths, code_scale, *refs):
     count = len(widths) - 1
     last, nears, refs = refs[0], refs[1 : 1 + count], refs[1 + count :]
-    weights, codes, (out, parts, done) = refs[: 2 * models - 1], refs[2 * models - 1 : -3], refs[-3:]
+    weights, codes, (out, parts, done) = refs[:models], refs[models:-3], refs[-3:]
     own_zl, own_y = lax.axis_index("zl"), lax.axis_index("y")
     copies = []
 
@@ -209,7 +222,7 @@
 
         here = codes[2 * k : 2 * k + 2]
         merge_chunk(
-            range(2, 4), models, tile_width, first, width, code_scale, weights, lambda m, at: here[at - 2][m], store
+            range(2, 4), models, tile_width, first, width, code_scale, weights, lambda at, j: two_steps(here[at - 2][j - 1]), store
         )
     for copy in copies:
         copy.wait()
@@ -232,33 +245,13 @@
     peak = LARGEST**4 * length + damping
     code_scale = 65535.0 / (math.log(peak) - math.log(damping))
 
-    early_rows = weights.shape[0] // 2
-    other_weights = []
-    for offset in range(1, models):
-        other_weights += [rotate(weights[:early_rows], "mp", offset), rotate(weights[early_rows:], "mp", offset)]
-
-    col_shape = jax.ShapeDtypeStruct((2, seqs, length, tile_width), bf)
+    other_weights = [rotate(weights, "mp", offset) for offset in range(1, models)]
+    col_shape = jax.ShapeDtypeStruct((core_count, 2, seqs, length, tile_width), bf)
     row_shape = jax.ShapeDtypeStruct((seqs, half, length), bf)
-    keep, send, *col_parts = call(front_kernel, (row_shape,) * 2 + (col_shape,) * (2 * core_count))(
+    keep, send, here, there = call(front_kernel, (row_shape, row_shape, col_shape, col_shape))(
         inputs, token_ids, cotangent
     )
 
-    got = []
-    for at, part in enumerate(col_parts):
-        dy, dc = at // core_count, at % core_count
-        if dy and dc:
-            size = 2 * core_count
-            perm = []
-            for i in range(size):
-                y, c = i // core_count, i % core_count
-                perm.append((i, (y ^ 1) * core_count + (c + dc) % core_count))
-            part = lax.ppermute(part, ("y", "c"), perm)
-        elif dy:
-            part = swap(part, "y")
-        elif dc:
-            part = rotate(part, "c", dc)
-        got.append(part)
-
     starts = [sum(widths[:k]) for k in range(len(widths))]
 
     def several(count, width):
@@ -269,6 +262,9 @@
 
     z2 = swap(send, "zh")
     z1 = swap(keep, "zl")
+    pair_shape = jax.ShapeDtypeStruct((2, 2, seqs, length, tile_width), bf)
+    got = call(core_kernel, (pair_shape,) * core_count)(here, swap(there, "y"), after=[z1, z2])
+    got = [rotate(part, "c", dc) if dc else part for dc, part in enumerate(got)]
     packs = [None] * len(widths)
     near, pass_on, own, other = call(
         gather_kernel, (many_rows(3), many_rows(1)) + (several(2 * core_count, widths[0]),) * 2
@@ -285,7 +281,7 @@
     from_both = swap(packs[0][1], ("zh", "zl"))
     first_cols = [packs[0][0], from_zl, from_zh, from_both]
     all_rows = call(third_kernel, many_rows(8))(
-        own_rows, swap(near, "y"), swap(far, "y"), after=[from_zh, from_zl, from_both] + other_weights[::2]
+        own_rows, swap(near, "y"), swap(far, "y"), after=[from_zh, from_zl, from_both] + other_weights
     )
     rows = [rotate(all_rows, "c", dc) if dc else all_rows for dc in range(core_count)]
     places = []
@@ -312,9 +308,9 @@
         if not last:
             from_models = [rotate(outs[0], "mp", offset) for offset in range(1, models)]
             parts = call(
-                functools.partial(models_kernel, models),
-                (jax.ShapeDtypeStruct((models, span, width), jnp.int16),) * 4,
-            )(outs[0], *from_models, after=other_weights[1::2])
+                functools.partial(steps_kernel, models),
+                (jax.ShapeDtypeStruct((models - 1, span, width), jnp.int16),) * 4,
+            )(outs[0], *from_models, after=other_weights)
             parts = [parts[0], swap(parts[1], "y"), swap(parts[2], "zl"), swap(parts[3], ("zl", "y"))]
             nears.append(
                 call(
@@ -332,7 +328,7 @@
                 over_y,
                 over_z,
                 far,
-                after=() if k else other_weights[1::2],
+                after=() if k else other_weights,
             )
             all_codes = [codes] + [rotate(codes, "mp", offset) for offset in range(1, models)]
     early = call(

time: 107 us -> 105 us (0.981)
  local copies, waits for them, and re-layouts: 4.68 us -> 2.92 us
    ppermute x4, waiting for transfers between devices: 4.26 us -> 1.54 us  [swap(): return lax.ppermute(value, axes, [(i, i ^ 3) for i in range(4)])]
    ppermute x6 -> x5, waiting for transfers between devices: 3.71 us -> 6.36 us  [rotate(): lax.ppermute(value, axis, [(i, (i + offset) % size) for i in range(size)])]
    ppermute x14, starting transfers between devices: 21.8 us -> 24.1 us  [swap(): return lax.ppermute(value, axes, [(0, 1), (1, 0)])]
    slice x1 -> x0, local copies, waits for them, and re-layouts: 1.75 us -> none  [shards(): weights[early_rows:]]
    ppermute x4, starting transfers between devices: 5.33 us -> 3.92 us  [swap(): return lax.ppermute(value, axes, [(i, i ^ 3) for i in range(4)])]
    pallas_call x10 -> x11, Pallas kernels: 6.89 us -> 7.22 us  [run(): pl.pallas_call(kernel, out_shape=out_shape, in_specs=[VMEM] * len(args) +...]
    ppermute x6 -> x5, starting transfers between devices: 4.44 us -> 4.28 us  [rotate(): lax.ppermute(value, axis, [(i, (i + offset) % size) for i in range(size)])]
  transfers between devices with their start and end apart: 25 -> 23, of which waited for: 14 -> 11; matrix products, arithmetic and copies ran while one was open for 2% -> 0% of each run, Pallas kernels for 6% -> 7%
where the time goes in v5:
time: 105 us
  waiting for transfers between devices  61.2 us (58%)
  starting transfers between devices  32.3 us (31%)
  Pallas kernels  8.61 us (8%)
  local copies, waits for them, and re-layouts  2.92 us (3%)
    ppermute x14, waiting for transfers between devices, swap(): return lax.ppermute(value, axes, [(0, 1), (1, 0)])  53.3 us
    ppermute x14, starting transfers between devices, swap(): return lax.ppermute(value, axes, [(0, 1), (1, 0)])  24.1 us
    pallas_call x11, Pallas kernels, run(): pl.pallas_call(kernel, out_shape=out_shape, in_specs=[VMEM] * len(args) +...  7.22 us
    ppermute x5, waiting for transfers between devices, rotate(): lax.ppermute(value, axis, [(i, (i + offset) % size) for i in range(size)])  6.36 us
    ppermute x5, starting transfers between devices, rotate(): lax.ppermute(value, axis, [(i, (i + offset) % size) for i in range(size)])  4.28 us
    ppermute x4, starting transfers between devices, swap(): return lax.ppermute(value, axes, [(i, i ^ 3) for i in range(4)])  3.92 us
    unnamed x8, local copies, waits for them, and re-layouts  2.92 us
  transfers between devices with their start and end apart: 23, of which 11 were waited for; matrix products, arithmetic and copies ran while one was open for 0% of the time, Pallas kernels for 7%

profile of v5, /device:TPU:0, one launch (start us, length us, event | category | flops | bytes accessed | tf_op | source)
XLA Modules:
  0.0 105.1 jit_solution(12584367843273088677)
XLA Ops:
  0.0 2.9 %collective-permute-start = (f32[256,2048]{1,0:T(8,128)}, f32[256,2048]{1,0:T(8,128)S(1)}, u32[]{:S(2)}, u32[]{:S(2)}) collective-permute-start(f32[256,2048]{1,0:T(8,128)} %bitcast.5), channel_id=1, source_target_pairs={{0,16},{16,0},{1,17},{17,1},{2,18},{18,2},{3,19},{19,3},{4,20},{20... | collective-permute-start | bytes 6291464 | tf_op jit(solution)/shard_map/ppermute | solution.py:33
  2.9 1.2 %copy-done.1 = bf16[1,1,128,4096]{3,2,1,0:T(8,128)(2,1)S(1)} copy-done((bf16[1,1,128,4096]{3,2,1,0:T(8,128)(2,1)S(1)}, bf16[1,1,128,4096]{3,2,1,0:T(8,128)(2,1)}, u32[]{:S(2)}) %copy-start.1) | copy-done | bytes 1048600
  4.2 1.0 copy-done.2
  5.2 0.7 copy-done.3
  5.9 0.3 shard_map.46
  6.2 1.6 %collective-permute-start.3 = (bf16[2,2,1,128,512]{4,3,2,1,0:T(8,128)(2,1)S(1)}, bf16[2,2,1,128,512]{4,3,2,1,0:T(8,128)(2,1)S(1)}, u32[]{:S(2)}, u32[]{:S(2)}) collective-permute-start(bf16[2,2,1,128,512]{4,3,2,1,0:T(8,128)(2,1)S(1)} %get-tuple-element.30), channel_id=1, source_target_pairs={{0,2},{2,0},{1,3},{3,1},{4,6},{6,4},{5,7},{7,5},{8,10},{10,8},{9,1... | collective-permute-start | bytes 1572872 | tf_op jit(solution)/shard_map/ppermute | solution.py:27
  7.8 1.6 %collective-permute-start.1 = (bf16[1,1024,128]{2,1,0:T(8,128)(2,1)S(1)}, bf16[1,1024,128]{2,1,0:T(8,128)(2,1)S(1)}, u32[]{:S(2)}, u32[]{:S(2)}) collective-permute-start(bf16[1,1024,128]{2,1,0:T(8,128)(2,1)S(1)} %get-tuple-element.27.refs_0_), channel_id=1, source_target_pairs={{0,4},{4,0},{1,5},{5,1},{2,6},{6,2},{3,7},{7,3},{8,12},{12,8},{9,1... | collective-permute-start | bytes 786440 | tf_op jit(solution)/shard_map/ppermute | solution.py:27
  9.4 2.6 %collective-permute-start.2 = (bf16[1,1024,128]{2,1,0:T(8,128)(2,1)S(1)}, bf16[1,1024,128]{2,1,0:T(8,128)(2,1)S(1)}, u32[]{:S(2)}, u32[]{:S(2)}) collective-permute-start(bf16[1,1024,128]{2,1,0:T(8,128)(2,1)S(1)} %get-tuple-element.28), channel_id=1, source_target_pairs={{0,8},{8,0},{1,9},{9,1},{2,10},{10,2},{3,11},{11,3},{4,12},{12,4},... | collective-permute-start | bytes 786440 | tf_op jit(solution)/shard_map/ppermute | solution.py:27
  12.0 8.8 %collective-permute-done.1.refs_2_.refs_1_ = bf16[1,1024,128]{2,1,0:T(8,128)(2,1)S(1)} collective-permute-done((bf16[1,1024,128]{2,1,0:T(8,128)(2,1)S(1)}, bf16[1,1024,128]{2,1,0:T(8,128)(2,1)S(1)}, u32[]{:S(2)}, u32[]{:S(2)}) %collective-permute-start.1) | collective-permute-done | bytes 262176 | tf_op jit(solution)/shard_map/ppermute | solution.py:27
  20.8 2.4 %collective-permute-done.2.refs_3_.refs_2_ = bf16[1,1024,128]{2,1,0:T(8,128)(2,1)S(1)} collective-permute-done((bf16[1,1024,128]{2,1,0:T(8,128)(2,1)S(1)}, bf16[1,1024,128]{2,1,0:T(8,128)(2,1)S(1)}, u32[]{:S(2)}, u32[]{:S(2)}) %collective-permute-start.2) | collective-permute-done | bytes 262176 | tf_op jit(solution)/shard_map/ppermute | solution.py:27
  23.1 0.1 shard_map.47
  23.2 0.1 collective-permute-start.4
  23.3 1.9 %collective-permute-done.4.refs_4_.refs_3_ = bf16[2,2,1,128,512]{4,3,2,1,0:T(8,128)(2,1)S(1)} collective-permute-done((bf16[2,2,1,128,512]{4,3,2,1,0:T(8,128)(2,1)S(1)}, bf16[2,2,1,128,512]{4,3,2,1,0:T(8,128)(2,1)S(1)}, u32[]{:S(2)}, u32[]{:S(2)}) %collective-permute-start.4) | collective-permute-done | bytes 524320 | tf_op jit(solution)/shard_map/ppermute | solution.py:33
  25.2 0.1 shard_map.48
  25.3 0.6 collective-permute-start.6
  25.9 0.4 collective-permute-start.5
  26.3 2.0 %collective-permute-start.10 = (bf16[4,128,256]{2,1,0:T(8,128)(2,1)S(1)}, bf16[4,128,256]{2,1,0:T(8,128)(2,1)S(1)}, u32[]{:S(2)}, u32[]{:S(2)}) collective-permute-start(bf16[4,128,256]{2,1,0:T(8,128)(2,1)S(1)} %get-tuple-element.38), channel_id=1, source_target_pairs={{0,12},{4,8},{8,4},{12,0},{1,13},{5,9},{9,5},{13,1},{2,14},{6,10},... | collective-permute-start | bytes 786440 | tf_op jit(solution)/shard_map/ppermute | solution.py:28
  28.4 1.1 %collective-permute-start.9 = (bf16[4,128,256]{2,1,0:T(8,128)(2,1)S(1)}, bf16[4,128,256]{2,1,0:T(8,128)(2,1)S(1)}, u32[]{:S(2)}, u32[]{:S(2)}) collective-permute-start(bf16[4,128,256]{2,1,0:T(8,128)(2,1)S(1)} %get-tuple-element.38), channel_id=1, source_target_pairs={{0,4},{4,0},{1,5},{5,1},{2,6},{6,2},{3,7},{7,3},{8,12},{12,8},{9,1... | collective-permute-start | bytes 786440 | tf_op jit(solution)/shard_map/ppermute | solution.py:27
  29.5 11.2 %collective-permute-done.5.refs_1_ = bf16[1,1024,128]{2,1,0:T(8,128)(2,1)S(1)} collective-permute-done((bf16[1,1024,128]{2,1,0:T(8,128)(2,1)S(1)}, bf16[1,1024,128]{2,1,0:T(8,128)(2,1)S(1)}, u32[]{:S(2)}, u32[]{:S(2)}) %collective-permute-start.5) | collective-permute-done | bytes 262176 | tf_op jit(solution)/shard_map/ppermute | solution.py:27
  40.7 1.3 %collective-permute-start.8 = (bf16[4,128,256]{2,1,0:T(8,128)(2,1)S(1)}, bf16[4,128,256]{2,1,0:T(8,128)(2,1)S(1)}, u32[]{:S(2)}, u32[]{:S(2)}) collective-permute-start(bf16[4,128,256]{2,1,0:T(8,128)(2,1)S(1)} %get-tuple-element.37.refs_2_), channel_id=1, source_target_pairs={{0,8},{8,0},{1,9},{9,1},{2,10},{10,2},{3,11},{11,3},{4,12},{12,4},... | collective-permute-start | bytes 786440 | tf_op jit(solution)/shard_map/ppermute | solution.py:27
  41.9 0.1 shard_map.49
  42.1 1.6 %collective-permute-start.7 = (bf16[1,1024,128]{2,1,0:T(8,128)(2,1)S(1)}, bf16[1,1024,128]{2,1,0:T(8,128)(2,1)S(1)}, u32[]{:S(2)}, u32[]{:S(2)}) collective-permute-start(bf16[1,1024,128]{2,1,0:T(8,128)(2,1)S(1)} %get-tuple-element.36), channel_id=1, source_target_pairs={{0,2},{2,0},{1,3},{3,1},{4,6},{6,4},{5,7},{7,5},{8,10},{10,8},{9,1... | collective-permute-start | bytes 786440 | tf_op jit(solution)/shard_map/ppermute | solution.py:27
  43.7 9.9 %collective-permute-done.8.refs_3_.refs_4_ = bf16[4,128,256]{2,1,0:T(8,128)(2,1)S(1)} collective-permute-done((bf16[4,128,256]{2,1,0:T(8,128)(2,1)S(1)}, bf16[4,128,256]{2,1,0:T(8,128)(2,1)S(1)}, u32[]{:S(2)}, u32[]{:S(2)}) %collective-permute-start.8) | collective-permute-done | bytes 262176 | tf_op jit(solution)/shard_map/ppermute | solution.py:27
  53.6 0.0 collective-permute-done.7.refs_2_
  53.6 0.1 shard_map.50.refs_0_
  53.8 0.1 collective-permute-start.11
  53.8 0.1 collective-permute-start.12
  53.9 2.9 %collective-permute-start.13 = (bf16[4,128,256]{2,1,0:T(8,128)(2,1)S(1)}, bf16[4,128,256]{2,1,0:T(8,128)(2,1)S(1)}, u32[]{:S(2)}, u32[]{:S(2)}) collective-permute-start(bf16[4,128,256]{2,1,0:T(8,128)(2,1)S(1)} %get-tuple-element.39.refs_2_), channel_id=1, source_target_pairs={{0,8},{8,0},{1,9},{9,1},{2,10},{10,2},{3,11},{11,3},{4,12},{12,4},... | collective-permute-start | bytes 786440 | tf_op jit(solution)/shard_map/ppermute | solution.py:27
  56.8 1.5 %collective-permute-start.14 = (bf16[4,128,256]{2,1,0:T(8,128)(2,1)S(1)}, bf16[4,128,256]{2,1,0:T(8,128)(2,1)S(1)}, u32[]{:S(2)}, u32[]{:S(2)}) collective-permute-start(bf16[4,128,256]{2,1,0:T(8,128)(2,1)S(1)} %get-tuple-element.40), channel_id=1, source_target_pairs={{0,12},{4,8},{8,4},{12,0},{1,13},{5,9},{9,5},{13,1},{2,14},{6,10},... | collective-permute-start | bytes 786440 | tf_op jit(solution)/shard_map/ppermute | solution.py:28
  58.3 2.6 %shard_map.53.refs_0_ = s16[4,256,256]{2,1,0:T(8,128)(2,1)S(1)} custom-call(bf16[8,1024,128]{2,1,0:T(8,128)(2,1)S(1)} %shard_map.50.refs_0_, bf16[8,1024,128]{2,1,0:T(8,128)(2,1)S(1)} %collective-permute-done.11.refs_1_, bf16[4,128,256]{2,1,0:T(8,128)(2,1)S(1)} %get-tuple-element.37.refs_2_, bf16[4,128,256]{2,1,0:T(8,128)(2,1)S(1)} %collective-permute-done.9.refs_4_.refs_3_, ...), custom_call_target="tpu_custom_call" | custom-call | flops 1073741824 | bytes 5242880 | tf_op jit(solution)/shard_map/pallas_call | solution.py:41
  60.9 0.6 collective-permute-start.19
  61.5 6.3 %collective-permute-done.12.refs_3_ = bf16[4,128,256]{2,1,0:T(8,128)(2,1)S(1)} collective-permute-done((bf16[4,128,256]{2,1,0:T(8,128)(2,1)S(1)}, bf16[4,128,256]{2,1,0:T(8,128)(2,1)S(1)}, u32[]{:S(2)}, u32[]{:S(2)}) %collective-permute-start.12) | collective-permute-done | bytes 262176 | tf_op jit(solution)/shard_map/ppermute | solution.py:27
  67.8 7.5 %collective-permute-done.13.refs_4_ = bf16[4,128,256]{2,1,0:T(8,128)(2,1)S(1)} collective-permute-done((bf16[4,128,256]{2,1,0:T(8,128)(2,1)S(1)}, bf16[4,128,256]{2,1,0:T(8,128)(2,1)S(1)}, u32[]{:S(2)}, u32[]{:S(2)}) %collective-permute-start.13) | collective-permute-done | bytes 262176 | tf_op jit(solution)/shard_map/ppermute | solution.py:27
  75.3 2.6 %shard_map.51 = (s16[256,256]{1,0:T(8,128)(2,1)S(1)}, s16[256,256]{1,0:T(8,128)(2,1)S(1)}, s16[256,256]{1,0:T(8,128)(2,1)S(1)}, s16[256,256]{1,0:T(8,128)(2,1)S(1)}) custom-call(bf16[8,1024,128]{2,1,0:T(8,128)(2,1)S(1)} %shard_map.50.refs_0_, bf16[8,1024,128]{2,1,0:T(8,128)(2,1)S(1)} %collective-permute-done.11.refs_1_, ...), custom_call_target="tpu_custom_call" | custom-call | flops 1073741824 | bytes 5242880 | tf_op jit(solution)/shard_map/pallas_call | solution.py:41
  77.9 1.6 %collective-permute-start.15 = (s16[256,256]{1,0:T(8,128)(2,1)S(1)}, s16[256,256]{1,0:T(8,128)(2,1)S(1)}, u32[]{:S(2)}, u32[]{:S(2)}) collective-permute-start(s16[256,256]{1,0:T(8,128)(2,1)S(1)} %get-tuple-element.42), channel_id=1, source_target_pairs={{0,2},{2,0},{1,3},{3,1},{4,6},{6,4},{5,7},{7,5},{8,10},{10,8},{9,1... | collective-permute-start | bytes 393224 | tf_op jit(solution)/shard_map/ppermute | solution.py:27
  79.5 5.6 %collective-permute-start.16 = (s16[256,256]{1,0:T(8,128)(2,1)S(1)}, s16[256,256]{1,0:T(8,128)(2,1)S(1)}, u32[]{:S(2)}, u32[]{:S(2)}) collective-permute-start(s16[256,256]{1,0:T(8,128)(2,1)S(1)} %get-tuple-element.43), channel_id=1, source_target_pairs={{0,4},{4,0},{1,5},{5,1},{2,6},{6,2},{3,7},{7,3},{8,12},{12,8},{9,1... | collective-permute-start | bytes 393224 | tf_op jit(solution)/shard_map/ppermute | solution.py:27
  85.1 4.3 %collective-permute-done.16.refs_2_ = s16[256,256]{1,0:T(8,128)(2,1)S(1)} collective-permute-done((s16[256,256]{1,0:T(8,128)(2,1)S(1)}, s16[256,256]{1,0:T(8,128)(2,1)S(1)}, u32[]{:S(2)}, u32[]{:S(2)}) %collective-permute-start.16) | collective-permute-done | bytes 131104 | tf_op jit(solution)/shard_map/ppermute | solution.py:27
  89.4 1.5 %collective-permute-done.17.refs_3_ = s16[256,256]{1,0:T(8,128)(2,1)S(1)} collective-permute-done((s16[256,256]{1,0:T(8,128)(2,1)S(1)}, s16[256,256]{1,0:T(8,128)(2,1)S(1)}, u32[]{:S(2)}, u32[]{:S(2)}) %collective-permute-start.17) | collective-permute-done | bytes 131104 | tf_op jit(solution)/shard_map/ppermute | solution.py:28
  91.0 0.6 collective-permute-start.18
  91.6 0.4 shard_map.54
  92.0 1.4 %collective-permute-start.20 = (s16[1,256,256]{2,1,0:T(8,128)(2,1)S(1)}, s16[1,256,256]{2,1,0:T(8,128)(2,1)S(1)}, u32[]{:S(2)}, u32[]{:S(2)}) collective-permute-start(s16[1,256,256]{2,1,0:T(8,128)(2,1)S(1)} %get-tuple-element.46), channel_id=1, source_target_pairs={{0,2},{2,0},{1,3},{3,1},{4,6},{6,4},{5,7},{7,5},{8,10},{10,8},{9,1... | collective-permute-start | bytes 393224 | tf_op jit(solution)/shard_map/ppermute | solution.py:27
  93.4 1.7 %collective-permute-start.21 = (s16[1,256,256]{2,1,0:T(8,128)(2,1)S(1)}, s16[1,256,256]{2,1,0:T(8,128)(2,1)S(1)}, u32[]{:S(2)}, u32[]{:S(2)}) collective-permute-start(s16[1,256,256]{2,1,0:T(8,128)(2,1)S(1)} %get-tuple-element.47), channel_id=1, source_target_pairs={{0,4},{4,0},{1,5},{5,1},{2,6},{6,2},{3,7},{7,3},{8,12},{12,8},{9,1... | collective-permute-start | bytes 393224 | tf_op jit(solution)/shard_map/ppermute | solution.py:27
  95.2 0.4 collective-permute-start.22
  95.6 2.9 %collective-permute-done.20.refs_3_ = s16[1,256,256]{2,1,0:T(8,128)(2,1)S(1)} collective-permute-done((s16[1,256,256]{2,1,0:T(8,128)(2,1)S(1)}, s16[1,256,256]{2,1,0:T(8,128)(2,1)S(1)}, u32[]{:S(2)}, u32[]{:S(2)}) %collective-permute-start.20) | collective-permute-done | bytes 131104 | tf_op jit(solution)/shard_map/ppermute | solution.py:27
  98.5 0.2 shard_map.55.refs_4_.refs_1_
  98.7 4.5 %collective-permute-done.18.refs_3_ = s16[4,256,256]{2,1,0:T(8,128)(2,1)S(1)} collective-permute-done((s16[4,256,256]{2,1,0:T(8,128)(2,1)S(1)}, s16[4,256,256]{2,1,0:T(8,128)(2,1)S(1)}, u32[]{:S(2)}, u32[]{:S(2)}) %collective-permute-start.18) | collective-permute-done | bytes 524320 | tf_op jit(solution)/shard_map/ppermute | solution.py:33
  103.1 0.6 shard_map.56.refs_0_
  103.7 1.4 %shard_map.57 = f32[256,2048]{1,0:T(8,128)} custom-call(f32[4,256,256]{2,1,0:T(8,128)S(1)} %shard_map.56.refs_0_, f32[2,256,256]{2,1,0:T(8,128)S(1)} %shard_map.55.refs_4_.refs_1_, f32[256,2048]{1,0:T(8,128)S(1)} %bitcast.8, f32[256,2048]{1,0:T(8,128)S(1)} %collective-permute-done.refs_6_.refs_2_.refs_1_.refs_3_, ...), custom_call_target="tpu_custom_call" | custom-call | tf_op jit(solution)/shard_map/pallas_call | solution.py:339
  (18 shorter events, 0.1 us)
Async XLA Ops:
  0.0 53.6 %collective-permute-start = (f32[256,2048]{1,0:T(8,128)}, f32[256,2048]{1,0:T(8,128)S(1)}, u32[]{:S(2)}, u32[]{:S(2)}) collective-permute-start(f32[256,2048]{1,0:T(8,128)} %bitcast.5), channel_id=1, source_target_pairs={{0,16},{16,0},{1,17},{17,1},{2,18},{18,2},{3,19},{19,3},{4,20},{20... | collective-permute-start | bytes 6291464 | tf_op jit(solution)/shard_map/ppermute | solution.py:33
  2.9 1.2 %copy-start.1 = (bf16[1,1,128,4096]{3,2,1,0:T(8,128)(2,1)S(1)}, bf16[1,1,128,4096]{3,2,1,0:T(8,128)(2,1)}, u32[]{:S(2)}) copy-start(bf16[1,1,128,4096]{3,2,1,0:T(8,128)(2,1)} %param.5) | copy-start | bytes 3145732
  4.2 1.0 copy-start.2
  5.2 0.7 copy-start.3
  6.2 16.9 %collective-permute-start.3 = (bf16[2,2,1,128,512]{4,3,2,1,0:T(8,128)(2,1)S(1)}, bf16[2,2,1,128,512]{4,3,2,1,0:T(8,128)(2,1)S(1)}, u32[]{:S(2)}, u32[]{:S(2)}) collective-permute-start(bf16[2,2,1,128,512]{4,3,2,1,0:T(8,128)(2,1)S(1)} %get-tuple-element.30), channel_id=1, source_target_pairs={{0,2},{2,0},{1,3},{3,1},{4,6},{6,4},{5,7},{7,5},{8,10},{10,8},{9,1... | collective-permute-start | bytes 1572872 | tf_op jit(solution)/shard_map/ppermute | solution.py:27
  7.8 13.0 %collective-permute-start.1 = (bf16[1,1024,128]{2,1,0:T(8,128)(2,1)S(1)}, bf16[1,1024,128]{2,1,0:T(8,128)(2,1)S(1)}, u32[]{:S(2)}, u32[]{:S(2)}) collective-permute-start(bf16[1,1024,128]{2,1,0:T(8,128)(2,1)S(1)} %get-tuple-element.27.refs_0_), channel_id=1, source_target_pairs={{0,4},{4,0},{1,5},{5,1},{2,6},{6,2},{3,7},{7,3},{8,12},{12,8},{9,1... | collective-permute-start | bytes 786440 | tf_op jit(solution)/shard_map/ppermute | solution.py:27
  9.4 13.8 %collective-permute-start.2 = (bf16[1,1024,128]{2,1,0:T(8,128)(2,1)S(1)}, bf16[1,1024,128]{2,1,0:T(8,128)(2,1)S(1)}, u32[]{:S(2)}, u32[]{:S(2)}) collective-permute-start(bf16[1,1024,128]{2,1,0:T(8,128)(2,1)S(1)} %get-tuple-element.28), channel_id=1, source_target_pairs={{0,8},{8,0},{1,9},{9,1},{2,10},{10,2},{3,11},{11,3},{4,12},{12,4},... | collective-permute-start | bytes 786440 | tf_op jit(solution)/shard_map/ppermute | solution.py:27
  23.2 2.0 %collective-permute-start.4 = (bf16[2,2,1,128,512]{4,3,2,1,0:T(8,128)(2,1)S(1)}, bf16[2,2,1,128,512]{4,3,2,1,0:T(8,128)(2,1)S(1)}, u32[]{:S(2)}, u32[]{:S(2)}) collective-permute-start(bf16[2,2,1,128,512]{4,3,2,1,0:T(8,128)(2,1)S(1)} %get-tuple-element.32), channel_id=1, source_target_pairs={{0,1},{1,0},{2,3},{3,2},{4,5},{5,4},{6,7},{7,6},{8,9},{9,8},{10,11... | collective-permute-start | bytes 1572872 | tf_op jit(solution)/shard_map/ppermute | solution.py:33
  25.3 28.3 %collective-permute-start.6 = (bf16[3,1024,128]{2,1,0:T(8,128)(2,1)S(1)}, bf16[3,1024,128]{2,1,0:T(8,128)(2,1)S(1)}, u32[]{:S(2)}, u32[]{:S(2)}) collective-permute-start(bf16[3,1024,128]{2,1,0:T(8,128)(2,1)S(1)} %get-tuple-element.33.refs_0_), channel_id=1, source_target_pairs={{0,2},{2,0},{1,3},{3,1},{4,6},{6,4},{5,7},{7,5},{8,10},{10,8},{9,1... | collective-permute-start | bytes 2359304 | tf_op jit(solution)/shard_map/ppermute | solution.py:27
  25.9 14.8 %collective-permute-start.5 = (bf16[1,1024,128]{2,1,0:T(8,128)(2,1)S(1)}, bf16[1,1024,128]{2,1,0:T(8,128)(2,1)S(1)}, u32[]{:S(2)}, u32[]{:S(2)}) collective-permute-start(bf16[1,1024,128]{2,1,0:T(8,128)(2,1)S(1)} %get-tuple-element.34), channel_id=1, source_target_pairs={{0,4},{4,0},{1,5},{5,1},{2,6},{6,2},{3,7},{7,3},{8,12},{12,8},{9,1... | collective-permute-start | bytes 786440 | tf_op jit(solution)/shard_map/ppermute | solution.py:27
  26.3 15.7 %collective-permute-start.10 = (bf16[4,128,256]{2,1,0:T(8,128)(2,1)S(1)}, bf16[4,128,256]{2,1,0:T(8,128)(2,1)S(1)}, u32[]{:S(2)}, u32[]{:S(2)}) collective-permute-start(bf16[4,128,256]{2,1,0:T(8,128)(2,1)S(1)} %get-tuple-element.38), channel_id=1, source_target_pairs={{0,12},{4,8},{8,4},{12,0},{1,13},{5,9},{9,5},{13,1},{2,14},{6,10},... | collective-permute-start | bytes 786440 | tf_op jit(solution)/shard_map/ppermute | solution.py:28
  28.4 25.2 %collective-permute-start.9 = (bf16[4,128,256]{2,1,0:T(8,128)(2,1)S(1)}, bf16[4,128,256]{2,1,0:T(8,128)(2,1)S(1)}, u32[]{:S(2)}, u32[]{:S(2)}) collective-permute-start(bf16[4,128,256]{2,1,0:T(8,128)(2,1)S(1)} %get-tuple-element.38), channel_id=1, source_target_pairs={{0,4},{4,0},{1,5},{5,1},{2,6},{6,2},{3,7},{7,3},{8,12},{12,8},{9,1... | collective-permute-start | bytes 786440 | tf_op jit(solution)/shard_map/ppermute | solution.py:27
  40.7 12.9 %collective-permute-start.8 = (bf16[4,128,256]{2,1,0:T(8,128)(2,1)S(1)}, bf16[4,128,256]{2,1,0:T(8,128)(2,1)S(1)}, u32[]{:S(2)}, u32[]{:S(2)}) collective-permute-start(bf16[4,128,256]{2,1,0:T(8,128)(2,1)S(1)} %get-tuple-element.37.refs_2_), channel_id=1, source_target_pairs={{0,8},{8,0},{1,9},{9,1},{2,10},{10,2},{3,11},{11,3},{4,12},{12,4},... | collective-permute-start | bytes 786440 | tf_op jit(solution)/shard_map/ppermute | solution.py:27
  42.1 11.5 %collective-permute-start.7 = (bf16[1,1024,128]{2,1,0:T(8,128)(2,1)S(1)}, bf16[1,1024,128]{2,1,0:T(8,128)(2,1)S(1)}, u32[]{:S(2)}, u32[]{:S(2)}) collective-permute-start(bf16[1,1024,128]{2,1,0:T(8,128)(2,1)S(1)} %get-tuple-element.36), channel_id=1, source_target_pairs={{0,2},{2,0},{1,3},{3,1},{4,6},{6,4},{5,7},{7,5},{8,10},{10,8},{9,1... | collective-permute-start | bytes 786440 | tf_op jit(solution)/shard_map/ppermute | solution.py:27
  53.8 4.5 %collective-permute-start.11 = (bf16[8,1024,128]{2,1,0:T(8,128)(2,1)S(1)}, bf16[8,1024,128]{2,1,0:T(8,128)(2,1)S(1)}, u32[]{:S(2)}, u32[]{:S(2)}) collective-permute-start(bf16[8,1024,128]{2,1,0:T(8,128)(2,1)S(1)} %shard_map.50.refs_0_), channel_id=1, source_target_pairs={{0,1},{1,0},{2,3},{3,2},{4,5},{5,4},{6,7},{7,6},{8,9},{9,8},{10,11... | collective-permute-start | bytes 6291464 | tf_op jit(solution)/shard_map/ppermute | solution.py:33
  53.8 13.9 %collective-permute-start.12 = (bf16[4,128,256]{2,1,0:T(8,128)(2,1)S(1)}, bf16[4,128,256]{2,1,0:T(8,128)(2,1)S(1)}, u32[]{:S(2)}, u32[]{:S(2)}) collective-permute-start(bf16[4,128,256]{2,1,0:T(8,128)(2,1)S(1)} %get-tuple-element.40), channel_id=1, source_target_pairs={{0,4},{4,0},{1,5},{5,1},{2,6},{6,2},{3,7},{7,3},{8,12},{12,8},{9,1... | collective-permute-start | bytes 786440 | tf_op jit(solution)/shard_map/ppermute | solution.py:27
  53.9 21.4 %collective-permute-start.13 = (bf16[4,128,256]{2,1,0:T(8,128)(2,1)S(1)}, bf16[4,128,256]{2,1,0:T(8,128)(2,1)S(1)}, u32[]{:S(2)}, u32[]{:S(2)}) collective-permute-start(bf16[4,128,256]{2,1,0:T(8,128)(2,1)S(1)} %get-tuple-element.39.refs_2_), channel_id=1, source_target_pairs={{0,8},{8,0},{1,9},{9,1},{2,10},{10,2},{3,11},{11,3},{4,12},{12,4},... | collective-permute-start | bytes 786440 | tf_op jit(solution)/shard_map/ppermute | solution.py:27
  56.8 18.5 %collective-permute-start.14 = (bf16[4,128,256]{2,1,0:T(8,128)(2,1)S(1)}, bf16[4,128,256]{2,1,0:T(8,128)(2,1)S(1)}, u32[]{:S(2)}, u32[]{:S(2)}) collective-permute-start(bf16[4,128,256]{2,1,0:T(8,128)(2,1)S(1)} %get-tuple-element.40), channel_id=1, source_target_pairs={{0,12},{4,8},{8,4},{12,0},{1,13},{5,9},{9,5},{13,1},{2,14},{6,10},... | collective-permute-start | bytes 786440 | tf_op jit(solution)/shard_map/ppermute | solution.py:28
  60.9 30.7 %collective-permute-start.19 = (s16[4,256,256]{2,1,0:T(8,128)(2,1)S(1)}, s16[4,256,256]{2,1,0:T(8,128)(2,1)S(1)}, u32[]{:S(2)}, u32[]{:S(2)}) collective-permute-start(s16[4,256,256]{2,1,0:T(8,128)(2,1)S(1)} %shard_map.53.refs_0_), channel_id=1, source_target_pairs={{0,16},{16,0},{1,17},{17,1},{2,18},{18,2},{3,19},{19,3},{4,20},{20... | collective-permute-start | bytes 1572872 | tf_op jit(solution)/shard_map/ppermute | solution.py:33
  77.9 7.2 %collective-permute-start.15 = (s16[256,256]{1,0:T(8,128)(2,1)S(1)}, s16[256,256]{1,0:T(8,128)(2,1)S(1)}, u32[]{:S(2)}, u32[]{:S(2)}) collective-permute-start(s16[256,256]{1,0:T(8,128)(2,1)S(1)} %get-tuple-element.42), channel_id=1, source_target_pairs={{0,2},{2,0},{1,3},{3,1},{4,6},{6,4},{5,7},{7,5},{8,10},{10,8},{9,1... | collective-permute-start | bytes 393224 | tf_op jit(solution)/shard_map/ppermute | solution.py:27
  79.5 10.0 %collective-permute-start.16 = (s16[256,256]{1,0:T(8,128)(2,1)S(1)}, s16[256,256]{1,0:T(8,128)(2,1)S(1)}, u32[]{:S(2)}, u32[]{:S(2)}) collective-permute-start(s16[256,256]{1,0:T(8,128)(2,1)S(1)} %get-tuple-element.43), channel_id=1, source_target_pairs={{0,4},{4,0},{1,5},{5,1},{2,6},{6,2},{3,7},{7,3},{8,12},{12,8},{9,1... | collective-permute-start | bytes 393224 | tf_op jit(solution)/shard_map/ppermute | solution.py:27
  85.1 5.9 %collective-permute-start.17 = (s16[256,256]{1,0:T(8,128)(2,1)S(1)}, s16[256,256]{1,0:T(8,128)(2,1)S(1)}, u32[]{:S(2)}, u32[]{:S(2)}) collective-permute-start(s16[256,256]{1,0:T(8,128)(2,1)S(1)} %get-tuple-element.44), channel_id=1, source_target_pairs={{0,6},{2,4},{4,2},{6,0},{1,7},{3,5},{5,3},{7,1},{8,14},{10,12},{12... | collective-permute-start | bytes 393224 | tf_op jit(solution)/shard_map/ppermute | solution.py:28
  91.0 7.5 %copy-start = (f32[1,1,256,2048]{3,2,1,0:T(8,128)S(1)}, f32[1,1,256,2048]{3,2,1,0:T(8,128)}, u32[]{:S(2)}) copy-start(f32[1,1,256,2048]{3,2,1,0:T(8,128)} %param.7) | copy-start | bytes 6291460
  91.0 12.1 %collective-permute-start.18 = (s16[4,256,256]{2,1,0:T(8,128)(2,1)S(1)}, s16[4,256,256]{2,1,0:T(8,128)(2,1)S(1)}, u32[]{:S(2)}, u32[]{:S(2)}) collective-permute-start(s16[4,256,256]{2,1,0:T(8,128)(2,1)S(1)} %shard_map.52.refs_2_), channel_id=1, source_target_pairs={{0,16},{16,0},{1,17},{17,1},{2,18},{18,2},{3,19},{19,3},{4,20},{20... | collective-permute-start | bytes 1572872 | tf_op jit(solution)/shard_map/ppermute | solution.py:33
  92.0 6.4 %collective-permute-start.20 = (s16[1,256,256]{2,1,0:T(8,128)(2,1)S(1)}, s16[1,256,256]{2,1,0:T(8,128)(2,1)S(1)}, u32[]{:S(2)}, u32[]{:S(2)}) collective-permute-start(s16[1,256,256]{2,1,0:T(8,128)(2,1)S(1)} %get-tuple-element.46), channel_id=1, source_target_pairs={{0,2},{2,0},{1,3},{3,1},{4,6},{6,4},{5,7},{7,5},{8,10},{10,8},{9,1... | collective-permute-start | bytes 393224 | tf_op jit(solution)/shard_map/ppermute | solution.py:27
  93.4 10.3 %collective-permute-start.21 = (s16[1,256,256]{2,1,0:T(8,128)(2,1)S(1)}, s16[1,256,256]{2,1,0:T(8,128)(2,1)S(1)}, u32[]{:S(2)}, u32[]{:S(2)}) collective-permute-start(s16[1,256,256]{2,1,0:T(8,128)(2,1)S(1)} %get-tuple-element.47), channel_id=1, source_target_pairs={{0,4},{4,0},{1,5},{5,1},{2,6},{6,2},{3,7},{7,3},{8,12},{12,8},{9,1... | collective-permute-start | bytes 393224 | tf_op jit(solution)/shard_map/ppermute | solution.py:27
  95.2 8.6 %collective-permute-start.22 = (s16[1,256,256]{2,1,0:T(8,128)(2,1)S(1)}, s16[1,256,256]{2,1,0:T(8,128)(2,1)S(1)}, u32[]{:S(2)}, u32[]{:S(2)}) collective-permute-start(s16[1,256,256]{2,1,0:T(8,128)(2,1)S(1)} %get-tuple-element.48), channel_id=1, source_target_pairs={{0,6},{2,4},{4,2},{6,0},{1,7},{3,5},{5,3},{7,1},{8,14},{10,12},{12... | collective-permute-start | bytes 393224 | tf_op jit(solution)/shard_map/ppermute | solution.py:28

commit v6 on v5

--- a/solution.py
+++ b/solution.py
@@ -187,7 +187,11 @@
         refs[-1][at] = value
 
     weights, codes = refs[:models], refs[models:-1]
-    merge_chunk(range(4), models, tile_width, first, width, code_scale, weights, lambda at, j: code_steps([code[at] for code in codes], j), store)
+
+    def steps(at, j):
+        return code_steps([codes[2 * m + 1][at - 1] if at else codes[2 * m][...] for m in range(models)], j)
+
+    merge_chunk(range(4), models, tile_width, first, width, code_scale, weights, steps, store)
 
 
 def near_merge_kernel(models, tile_width, first, width, code_scale, *refs):
@@ -323,14 +327,13 @@
             far = swap(outs[3], ("zl", "y"))
             over_z = swap(outs[2], "zl")
             over_y = swap(outs[1], "y")
-            codes = call(code_kernel, four_shape)(
-                outs[0],
-                over_y,
-                over_z,
-                far,
-                after=() if k else other_weights,
+            x_near = [rotate(outs[0], "mp", offset) for offset in range(1, models)]
+            codes = call(code_kernel, jax.ShapeDtypeStruct((3, span, width), jnp.int16))(
+                over_y, over_z, far, after=x_near + ([] if k else other_weights)
             )
-            all_codes = [codes] + [rotate(codes, "mp", offset) for offset in range(1, models)]
+            all_codes = [outs[0], codes]
+            for offset in range(1, models):
+                all_codes += [x_near[offset - 1], rotate(codes, "mp", offset)]
     early = call(
         functools.partial(early_merge_kernel, models, tile_width, starts[-1], widths[-1], code_scale),
         jax.ShapeDtypeStruct((4, span, widths[-1]), jnp.float32),

time: 105 us -> 103 us (0.981)
  waiting for transfers between devices: 61.2 us -> 58 us
    ppermute x5 -> x6, waiting for transfers between devices: 6.36 us -> 3.56 us  [rotate(): lax.ppermute(value, axis, [(i, (i + offset) % size) for i in range(size)])]
    ppermute x5 -> x6, starting transfers between devices: 4.28 us -> 4.82 us  [rotate(): lax.ppermute(value, axis, [(i, (i + offset) % size) for i in range(size)])]
  transfers between devices with their start and end apart: 23 -> 24, of which waited for: 11 -> 12; matrix products, arithmetic and copies ran while one was open for 0% -> 0% of each run, Pallas kernels for 7% -> 7%
where the time goes in v6:
time: 103 us; the launch traced here: 102 us
  waiting for transfers between devices  58 us (56%)
  starting transfers between devices  32.8 us (32%)
  Pallas kernels  8.6 us (8%)
  local copies, waits for them, and re-layouts  2.93 us (3%)
    ppermute x14, waiting for transfers between devices, swap(): return lax.ppermute(value, axes, [(0, 1), (1, 0)])  52.8 us
    ppermute x14, starting transfers between devices, swap(): return lax.ppermute(value, axes, [(0, 1), (1, 0)])  24.1 us
    pallas_call x11, Pallas kernels, run(): pl.pallas_call(kernel, out_shape=out_shape, in_specs=[VMEM] * len(args) +...  7.21 us
    ppermute x6, starting transfers between devices, rotate(): lax.ppermute(value, axis, [(i, (i + offset) % size) for i in range(size)])  4.82 us
    ppermute x4, starting transfers between devices, swap(): return lax.ppermute(value, axes, [(i, i ^ 3) for i in range(4)])  3.92 us
    ppermute x6, waiting for transfers between devices, rotate(): lax.ppermute(value, axis, [(i, (i + offset) % size) for i in range(size)])  3.56 us
    unnamed x8, local copies, waits for them, and re-layouts  2.93 us
  transfers between devices with their start and end apart: 24, of which 12 were waited for; matrix products, arithmetic and copies ran while one was open for 0% of the time, Pallas kernels for 7%

profile of v6, /device:TPU:0, one launch (start us, length us, event | category | flops | bytes accessed | tf_op | source)
XLA Modules:
  0.0 102.4 jit_solution(14168521356070029592)
XLA Ops:
  0.0 2.9 %collective-permute-start = (f32[256,2048]{1,0:T(8,128)}, f32[256,2048]{1,0:T(8,128)S(1)}, u32[]{:S(2)}, u32[]{:S(2)}) collective-permute-start(f32[256,2048]{1,0:T(8,128)} %bitcast.5), channel_id=1, source_target_pairs={{0,16},{16,0},{1,17},{17,1},{2,18},{18,2},{3,19},{19,3},{4,20},{20... | collective-permute-start | bytes 6291464 | tf_op jit(solution)/shard_map/ppermute | solution.py:33
  2.9 1.2 %copy-done.1 = bf16[1,1,128,4096]{3,2,1,0:T(8,128)(2,1)S(1)} copy-done((bf16[1,1,128,4096]{3,2,1,0:T(8,128)(2,1)S(1)}, bf16[1,1,128,4096]{3,2,1,0:T(8,128)(2,1)}, u32[]{:S(2)}) %copy-start.1) | copy-done | bytes 1048600
  4.2 1.0 %copy-done.2 = bf16[1,1,128,2048]{3,2,1,0:T(8,128)(2,1)S(1)} copy-done((bf16[1,1,128,2048]{3,2,1,0:T(8,128)(2,1)S(1)}, bf16[1,1,128,2048]{3,2,1,0:T(8,128)(2,1)}, u32[]{:S(2)}) %copy-start.2) | copy-done | bytes 524312
  5.2 0.7 copy-done.3
  5.9 0.3 shard_map.46
  6.2 1.6 %collective-permute-start.3 = (bf16[2,2,1,128,512]{4,3,2,1,0:T(8,128)(2,1)S(1)}, bf16[2,2,1,128,512]{4,3,2,1,0:T(8,128)(2,1)S(1)}, u32[]{:S(2)}, u32[]{:S(2)}) collective-permute-start(bf16[2,2,1,128,512]{4,3,2,1,0:T(8,128)(2,1)S(1)} %get-tuple-element.30), channel_id=1, source_target_pairs={{0,2},{2,0},{1,3},{3,1},{4,6},{6,4},{5,7},{7,5},{8,10},{10,8},{9,1... | collective-permute-start | bytes 1572872 | tf_op jit(solution)/shard_map/ppermute | solution.py:27
  7.8 1.6 %collective-permute-start.1 = (bf16[1,1024,128]{2,1,0:T(8,128)(2,1)S(1)}, bf16[1,1024,128]{2,1,0:T(8,128)(2,1)S(1)}, u32[]{:S(2)}, u32[]{:S(2)}) collective-permute-start(bf16[1,1024,128]{2,1,0:T(8,128)(2,1)S(1)} %get-tuple-element.27.refs_0_), channel_id=1, source_target_pairs={{0,4},{4,0},{1,5},{5,1},{2,6},{6,2},{3,7},{7,3},{8,12},{12,8},{9,1... | collective-permute-start | bytes 786440 | tf_op jit(solution)/shard_map/ppermute | solution.py:27
  9.4 2.6 %collective-permute-start.2 = (bf16[1,1024,128]{2,1,0:T(8,128)(2,1)S(1)}, bf16[1,1024,128]{2,1,0:T(8,128)(2,1)S(1)}, u32[]{:S(2)}, u32[]{:S(2)}) collective-permute-start(bf16[1,1024,128]{2,1,0:T(8,128)(2,1)S(1)} %get-tuple-element.28), channel_id=1, source_target_pairs={{0,8},{8,0},{1,9},{9,1},{2,10},{10,2},{3,11},{11,3},{4,12},{12,4},... | collective-permute-start | bytes 786440 | tf_op jit(solution)/shard_map/ppermute | solution.py:27
  12.0 8.8 %collective-permute-done.1.refs_2_.refs_1_ = bf16[1,1024,128]{2,1,0:T(8,128)(2,1)S(1)} collective-permute-done((bf16[1,1024,128]{2,1,0:T(8,128)(2,1)S(1)}, bf16[1,1024,128]{2,1,0:T(8,128)(2,1)S(1)}, u32[]{:S(2)}, u32[]{:S(2)}) %collective-permute-start.1) | collective-permute-done | bytes 262176 | tf_op jit(solution)/shard_map/ppermute | solution.py:27
  20.8 2.4 %collective-permute-done.2.refs_3_.refs_2_ = bf16[1,1024,128]{2,1,0:T(8,128)(2,1)S(1)} collective-permute-done((bf16[1,1024,128]{2,1,0:T(8,128)(2,1)S(1)}, bf16[1,1024,128]{2,1,0:T(8,128)(2,1)S(1)}, u32[]{:S(2)}, u32[]{:S(2)}) %collective-permute-start.2) | collective-permute-done | bytes 262176 | tf_op jit(solution)/shard_map/ppermute | solution.py:27
  23.2 0.1 collective-permute-start.4
  23.3 1.9 %collective-permute-done.4.refs_4_.refs_3_ = bf16[2,2,1,128,512]{4,3,2,1,0:T(8,128)(2,1)S(1)} collective-permute-done((bf16[2,2,1,128,512]{4,3,2,1,0:T(8,128)(2,1)S(1)}, bf16[2,2,1,128,512]{4,3,2,1,0:T(8,128)(2,1)S(1)}, u32[]{:S(2)}, u32[]{:S(2)}) %collective-permute-start.4) | collective-permute-done | bytes 524320 | tf_op jit(solution)/shard_map/ppermute | solution.py:33
  25.2 0.1 shard_map.48
  25.3 0.6 collective-permute-start.6
  25.9 0.4 collective-permute-start.5
  26.3 2.0 %collective-permute-start.10 = (bf16[4,128,256]{2,1,0:T(8,128)(2,1)S(1)}, bf16[4,128,256]{2,1,0:T(8,128)(2,1)S(1)}, u32[]{:S(2)}, u32[]{:S(2)}) collective-permute-start(bf16[4,128,256]{2,1,0:T(8,128)(2,1)S(1)} %get-tuple-element.38), channel_id=1, source_target_pairs={{0,12},{4,8},{8,4},{12,0},{1,13},{5,9},{9,5},{13,1},{2,14},{6,10},... | collective-permute-start | bytes 786440 | tf_op jit(solution)/shard_map/ppermute | solution.py:28
  28.4 1.1 %collective-permute-start.9 = (bf16[4,128,256]{2,1,0:T(8,128)(2,1)S(1)}, bf16[4,128,256]{2,1,0:T(8,128)(2,1)S(1)}, u32[]{:S(2)}, u32[]{:S(2)}) collective-permute-start(bf16[4,128,256]{2,1,0:T(8,128)(2,1)S(1)} %get-tuple-element.38), channel_id=1, source_target_pairs={{0,4},{4,0},{1,5},{5,1},{2,6},{6,2},{3,7},{7,3},{8,12},{12,8},{9,1... | collective-permute-start | bytes 786440 | tf_op jit(solution)/shard_map/ppermute | solution.py:27
  29.5 11.2 %collective-permute-done.5.refs_1_ = bf16[1,1024,128]{2,1,0:T(8,128)(2,1)S(1)} collective-permute-done((bf16[1,1024,128]{2,1,0:T(8,128)(2,1)S(1)}, bf16[1,1024,128]{2,1,0:T(8,128)(2,1)S(1)}, u32[]{:S(2)}, u32[]{:S(2)}) %collective-permute-start.5) | collective-permute-done | bytes 262176 | tf_op jit(solution)/shard_map/ppermute | solution.py:27
  40.7 1.3 %collective-permute-start.8 = (bf16[4,128,256]{2,1,0:T(8,128)(2,1)S(1)}, bf16[4,128,256]{2,1,0:T(8,128)(2,1)S(1)}, u32[]{:S(2)}, u32[]{:S(2)}) collective-permute-start(bf16[4,128,256]{2,1,0:T(8,128)(2,1)S(1)} %get-tuple-element.37.refs_2_), channel_id=1, source_target_pairs={{0,8},{8,0},{1,9},{9,1},{2,10},{10,2},{3,11},{11,3},{4,12},{12,4},... | collective-permute-start | bytes 786440 | tf_op jit(solution)/shard_map/ppermute | solution.py:27
  41.9 0.1 shard_map.49
  42.1 1.6 %collective-permute-start.7 = (bf16[1,1024,128]{2,1,0:T(8,128)(2,1)S(1)}, bf16[1,1024,128]{2,1,0:T(8,128)(2,1)S(1)}, u32[]{:S(2)}, u32[]{:S(2)}) collective-permute-start(bf16[1,1024,128]{2,1,0:T(8,128)(2,1)S(1)} %get-tuple-element.36), channel_id=1, source_target_pairs={{0,2},{2,0},{1,3},{3,1},{4,6},{6,4},{5,7},{7,5},{8,10},{10,8},{9,1... | collective-permute-start | bytes 786440 | tf_op jit(solution)/shard_map/ppermute | solution.py:27
  43.7 9.9 %collective-permute-done.8.refs_3_.refs_4_ = bf16[4,128,256]{2,1,0:T(8,128)(2,1)S(1)} collective-permute-done((bf16[4,128,256]{2,1,0:T(8,128)(2,1)S(1)}, bf16[4,128,256]{2,1,0:T(8,128)(2,1)S(1)}, u32[]{:S(2)}, u32[]{:S(2)}) %collective-permute-start.8) | collective-permute-done | bytes 262176 | tf_op jit(solution)/shard_map/ppermute | solution.py:27
  53.6 0.1 shard_map.50.refs_0_
  53.8 0.1 collective-permute-start.11
  53.8 0.1 collective-permute-start.12
  53.9 2.9 %collective-permute-start.13 = (bf16[4,128,256]{2,1,0:T(8,128)(2,1)S(1)}, bf16[4,128,256]{2,1,0:T(8,128)(2,1)S(1)}, u32[]{:S(2)}, u32[]{:S(2)}) collective-permute-start(bf16[4,128,256]{2,1,0:T(8,128)(2,1)S(1)} %get-tuple-element.39.refs_2_), channel_id=1, source_target_pairs={{0,8},{8,0},{1,9},{9,1},{2,10},{10,2},{3,11},{11,3},{4,12},{12,4},... | collective-permute-start | bytes 786440 | tf_op jit(solution)/shard_map/ppermute | solution.py:27
  56.8 1.5 %collective-permute-start.14 = (bf16[4,128,256]{2,1,0:T(8,128)(2,1)S(1)}, bf16[4,128,256]{2,1,0:T(8,128)(2,1)S(1)}, u32[]{:S(2)}, u32[]{:S(2)}) collective-permute-start(bf16[4,128,256]{2,1,0:T(8,128)(2,1)S(1)} %get-tuple-element.40), channel_id=1, source_target_pairs={{0,12},{4,8},{8,4},{12,0},{1,13},{5,9},{9,5},{13,1},{2,14},{6,10},... | collective-permute-start | bytes 786440 | tf_op jit(solution)/shard_map/ppermute | solution.py:28
  58.3 2.6 %shard_map.53.refs_0_ = s16[4,256,256]{2,1,0:T(8,128)(2,1)S(1)} custom-call(bf16[8,1024,128]{2,1,0:T(8,128)(2,1)S(1)} %shard_map.50.refs_0_, bf16[8,1024,128]{2,1,0:T(8,128)(2,1)S(1)} %collective-permute-done.11.refs_1_, bf16[4,128,256]{2,1,0:T(8,128)(2,1)S(1)} %get-tuple-element.37.refs_2_, bf16[4,128,256]{2,1,0:T(8,128)(2,1)S(1)} %collective-permute-done.9.refs_4_.refs_3_, ...), custom_call_target="tpu_custom_call" | custom-call | flops 1073741824 | bytes 5242880 | tf_op jit(solution)/shard_map/pallas_call | solution.py:41
  60.9 0.6 collective-permute-start.20
  61.5 6.3 %collective-permute-done.12.refs_3_ = bf16[4,128,256]{2,1,0:T(8,128)(2,1)S(1)} collective-permute-done((bf16[4,128,256]{2,1,0:T(8,128)(2,1)S(1)}, bf16[4,128,256]{2,1,0:T(8,128)(2,1)S(1)}, u32[]{:S(2)}, u32[]{:S(2)}) %collective-permute-start.12) | collective-permute-done | bytes 262176 | tf_op jit(solution)/shard_map/ppermute | solution.py:27
  67.8 7.5 %collective-permute-done.13.refs_4_ = bf16[4,128,256]{2,1,0:T(8,128)(2,1)S(1)} collective-permute-done((bf16[4,128,256]{2,1,0:T(8,128)(2,1)S(1)}, bf16[4,128,256]{2,1,0:T(8,128)(2,1)S(1)}, u32[]{:S(2)}, u32[]{:S(2)}) %collective-permute-start.13) | collective-permute-done | bytes 262176 | tf_op jit(solution)/shard_map/ppermute | solution.py:27
  75.3 2.6 %shard_map.51 = (s16[256,256]{1,0:T(8,128)(2,1)S(1)}, s16[256,256]{1,0:T(8,128)(2,1)S(1)}, s16[256,256]{1,0:T(8,128)(2,1)S(1)}, s16[256,256]{1,0:T(8,128)(2,1)S(1)}) custom-call(bf16[8,1024,128]{2,1,0:T(8,128)(2,1)S(1)} %shard_map.50.refs_0_, bf16[8,1024,128]{2,1,0:T(8,128)(2,1)S(1)} %collective-permute-done.11.refs_1_, ...), custom_call_target="tpu_custom_call" | custom-call | flops 1073741824 | bytes 5242880 | tf_op jit(solution)/shard_map/pallas_call | solution.py:41
  77.9 1.6 %collective-permute-start.15 = (s16[256,256]{1,0:T(8,128)(2,1)S(1)}, s16[256,256]{1,0:T(8,128)(2,1)S(1)}, u32[]{:S(2)}, u32[]{:S(2)}) collective-permute-start(s16[256,256]{1,0:T(8,128)(2,1)S(1)} %get-tuple-element.42), channel_id=1, source_target_pairs={{0,2},{2,0},{1,3},{3,1},{4,6},{6,4},{5,7},{7,5},{8,10},{10,8},{9,1... | collective-permute-start | bytes 393224 | tf_op jit(solution)/shard_map/ppermute | solution.py:27
  79.5 5.6 %collective-permute-start.16 = (s16[256,256]{1,0:T(8,128)(2,1)S(1)}, s16[256,256]{1,0:T(8,128)(2,1)S(1)}, u32[]{:S(2)}, u32[]{:S(2)}) collective-permute-start(s16[256,256]{1,0:T(8,128)(2,1)S(1)} %get-tuple-element.43), channel_id=1, source_target_pairs={{0,4},{4,0},{1,5},{5,1},{2,6},{6,2},{3,7},{7,3},{8,12},{12,8},{9,1... | collective-permute-start | bytes 393224 | tf_op jit(solution)/shard_map/ppermute | solution.py:27
  85.1 0.5 collective-permute-start.18
  85.7 3.8 %collective-permute-done.16.refs_1_ = s16[256,256]{1,0:T(8,128)(2,1)S(1)} collective-permute-done((s16[256,256]{1,0:T(8,128)(2,1)S(1)}, s16[256,256]{1,0:T(8,128)(2,1)S(1)}, u32[]{:S(2)}, u32[]{:S(2)}) %collective-permute-start.16) | collective-permute-done | bytes 131104 | tf_op jit(solution)/shard_map/ppermute | solution.py:27
  89.5 1.5 %collective-permute-done.17.refs_2_ = s16[256,256]{1,0:T(8,128)(2,1)S(1)} collective-permute-done((s16[256,256]{1,0:T(8,128)(2,1)S(1)}, s16[256,256]{1,0:T(8,128)(2,1)S(1)}, u32[]{:S(2)}, u32[]{:S(2)}) %collective-permute-start.17) | collective-permute-done | bytes 131104 | tf_op jit(solution)/shard_map/ppermute | solution.py:28
  91.0 0.6 collective-permute-start.19
  91.6 0.4 shard_map.54
  92.0 1.4 %collective-permute-start.21 = (s16[1,256,256]{2,1,0:T(8,128)(2,1)S(1)}, s16[1,256,256]{2,1,0:T(8,128)(2,1)S(1)}, u32[]{:S(2)}, u32[]{:S(2)}) collective-permute-start(s16[1,256,256]{2,1,0:T(8,128)(2,1)S(1)} %get-tuple-element.46), channel_id=1, source_target_pairs={{0,2},{2,0},{1,3},{3,1},{4,6},{6,4},{5,7},{7,5},{8,10},{10,8},{9,1... | collective-permute-start | bytes 393224 | tf_op jit(solution)/shard_map/ppermute | solution.py:27
  93.4 1.7 %collective-permute-start.22 = (s16[1,256,256]{2,1,0:T(8,128)(2,1)S(1)}, s16[1,256,256]{2,1,0:T(8,128)(2,1)S(1)}, u32[]{:S(2)}, u32[]{:S(2)}) collective-permute-start(s16[1,256,256]{2,1,0:T(8,128)(2,1)S(1)} %get-tuple-element.47), channel_id=1, source_target_pairs={{0,4},{4,0},{1,5},{5,1},{2,6},{6,2},{3,7},{7,3},{8,12},{12,8},{9,1... | collective-permute-start | bytes 393224 | tf_op jit(solution)/shard_map/ppermute | solution.py:27
  95.2 0.4 collective-permute-start.23
  95.6 2.9 %collective-permute-done.21.refs_3_ = s16[1,256,256]{2,1,0:T(8,128)(2,1)S(1)} collective-permute-done((s16[1,256,256]{2,1,0:T(8,128)(2,1)S(1)}, s16[1,256,256]{2,1,0:T(8,128)(2,1)S(1)}, u32[]{:S(2)}, u32[]{:S(2)}) %collective-permute-start.21) | collective-permute-done | bytes 131104 | tf_op jit(solution)/shard_map/ppermute | solution.py:27
  98.5 0.2 shard_map.55.refs_6_.refs_1_
  98.7 1.6 %collective-permute-done.19.refs_5_ = s16[3,256,256]{2,1,0:T(8,128)(2,1)S(1)} collective-permute-done((s16[3,256,256]{2,1,0:T(8,128)(2,1)S(1)}, s16[3,256,256]{2,1,0:T(8,128)(2,1)S(1)}, u32[]{:S(2)}, u32[]{:S(2)}) %collective-permute-start.19) | collective-permute-done | bytes 393248 | tf_op jit(solution)/shard_map/ppermute | solution.py:33
  100.3 0.6 shard_map.56.refs_0_
  100.9 0.1 collective-permute-done.23.refs_5_
  101.0 1.4 %shard_map.57 = f32[256,2048]{1,0:T(8,128)} custom-call(f32[4,256,256]{2,1,0:T(8,128)S(1)} %shard_map.56.refs_0_, f32[2,256,256]{2,1,0:T(8,128)S(1)} %shard_map.55.refs_6_.refs_1_, f32[256,2048]{1,0:T(8,128)S(1)} %bitcast.8, f32[256,2048]{1,0:T(8,128)S(1)} %collective-permute-done.refs_6_.refs_2_.refs_1_.refs_3_, ...), custom_call_target="tpu_custom_call" | custom-call | tf_op jit(solution)/shard_map/pallas_call | solution.py:342
  (20 shorter events, 0.1 us)
Async XLA Ops:
  0.0 53.6 %collective-permute-start = (f32[256,2048]{1,0:T(8,128)}, f32[256,2048]{1,0:T(8,128)S(1)}, u32[]{:S(2)}, u32[]{:S(2)}) collective-permute-start(f32[256,2048]{1,0:T(8,128)} %bitcast.5), channel_id=1, source_target_pairs={{0,16},{16,0},{1,17},{17,1},{2,18},{18,2},{3,19},{19,3},{4,20},{20... | collective-permute-start | bytes 6291464 | tf_op jit(solution)/shard_map/ppermute | solution.py:33
  2.9 1.2 %copy-start.1 = (bf16[1,1,128,4096]{3,2,1,0:T(8,128)(2,1)S(1)}, bf16[1,1,128,4096]{3,2,1,0:T(8,128)(2,1)}, u32[]{:S(2)}) copy-start(bf16[1,1,128,4096]{3,2,1,0:T(8,128)(2,1)} %param.5) | copy-start | bytes 3145732
  4.2 1.0 %copy-start.2 = (bf16[1,1,128,2048]{3,2,1,0:T(8,128)(2,1)S(1)}, bf16[1,1,128,2048]{3,2,1,0:T(8,128)(2,1)}, u32[]{:S(2)}) copy-start(bf16[1,1,128,2048]{3,2,1,0:T(8,128)(2,1)} %param.4) | copy-start | bytes 1572868
  5.2 0.7 copy-start.3
  6.2 16.9 %collective-permute-start.3 = (bf16[2,2,1,128,512]{4,3,2,1,0:T(8,128)(2,1)S(1)}, bf16[2,2,1,128,512]{4,3,2,1,0:T(8,128)(2,1)S(1)}, u32[]{:S(2)}, u32[]{:S(2)}) collective-permute-start(bf16[2,2,1,128,512]{4,3,2,1,0:T(8,128)(2,1)S(1)} %get-tuple-element.30), channel_id=1, source_target_pairs={{0,2},{2,0},{1,3},{3,1},{4,6},{6,4},{5,7},{7,5},{8,10},{10,8},{9,1... | collective-permute-start | bytes 1572872 | tf_op jit(solution)/shard_map/ppermute | solution.py:27
  7.8 13.0 %collective-permute-start.1 = (bf16[1,1024,128]{2,1,0:T(8,128)(2,1)S(1)}, bf16[1,1024,128]{2,1,0:T(8,128)(2,1)S(1)}, u32[]{:S(2)}, u32[]{:S(2)}) collective-permute-start(bf16[1,1024,128]{2,1,0:T(8,128)(2,1)S(1)} %get-tuple-element.27.refs_0_), channel_id=1, source_target_pairs={{0,4},{4,0},{1,5},{5,1},{2,6},{6,2},{3,7},{7,3},{8,12},{12,8},{9,1... | collective-permute-start | bytes 786440 | tf_op jit(solution)/shard_map/ppermute | solution.py:27
  9.4 13.8 %collective-permute-start.2 = (bf16[1,1024,128]{2,1,0:T(8,128)(2,1)S(1)}, bf16[1,1024,128]{2,1,0:T(8,128)(2,1)S(1)}, u32[]{:S(2)}, u32[]{:S(2)}) collective-permute-start(bf16[1,1024,128]{2,1,0:T(8,128)(2,1)S(1)} %get-tuple-element.28), channel_id=1, source_target_pairs={{0,8},{8,0},{1,9},{9,1},{2,10},{10,2},{3,11},{11,3},{4,12},{12,4},... | collective-permute-start | bytes 786440 | tf_op jit(solution)/shard_map/ppermute | solution.py:27
  23.2 2.0 %collective-permute-start.4 = (bf16[2,2,1,128,512]{4,3,2,1,0:T(8,128)(2,1)S(1)}, bf16[2,2,1,128,512]{4,3,2,1,0:T(8,128)(2,1)S(1)}, u32[]{:S(2)}, u32[]{:S(2)}) collective-permute-start(bf16[2,2,1,128,512]{4,3,2,1,0:T(8,128)(2,1)S(1)} %get-tuple-element.32), channel_id=1, source_target_pairs={{0,1},{1,0},{2,3},{3,2},{4,5},{5,4},{6,7},{7,6},{8,9},{9,8},{10,11... | collective-permute-start | bytes 1572872 | tf_op jit(solution)/shard_map/ppermute | solution.py:33
  25.3 28.3 %collective-permute-start.6 = (bf16[3,1024,128]{2,1,0:T(8,128)(2,1)S(1)}, bf16[3,1024,128]{2,1,0:T(8,128)(2,1)S(1)}, u32[]{:S(2)}, u32[]{:S(2)}) collective-permute-start(bf16[3,1024,128]{2,1,0:T(8,128)(2,1)S(1)} %get-tuple-element.33.refs_0_), channel_id=1, source_target_pairs={{0,2},{2,0},{1,3},{3,1},{4,6},{6,4},{5,7},{7,5},{8,10},{10,8},{9,1... | collective-permute-start | bytes 2359304 | tf_op jit(solution)/shard_map/ppermute | solution.py:27
  25.9 14.8 %collective-permute-start.5 = (bf16[1,1024,128]{2,1,0:T(8,128)(2,1)S(1)}, bf16[1,1024,128]{2,1,0:T(8,128)(2,1)S(1)}, u32[]{:S(2)}, u32[]{:S(2)}) collective-permute-start(bf16[1,1024,128]{2,1,0:T(8,128)(2,1)S(1)} %get-tuple-element.34), channel_id=1, source_target_pairs={{0,4},{4,0},{1,5},{5,1},{2,6},{6,2},{3,7},{7,3},{8,12},{12,8},{9,1... | collective-permute-start | bytes 786440 | tf_op jit(solution)/shard_map/ppermute | solution.py:27
  26.3 15.7 %collective-permute-start.10 = (bf16[4,128,256]{2,1,0:T(8,128)(2,1)S(1)}, bf16[4,128,256]{2,1,0:T(8,128)(2,1)S(1)}, u32[]{:S(2)}, u32[]{:S(2)}) collective-permute-start(bf16[4,128,256]{2,1,0:T(8,128)(2,1)S(1)} %get-tuple-element.38), channel_id=1, source_target_pairs={{0,12},{4,8},{8,4},{12,0},{1,13},{5,9},{9,5},{13,1},{2,14},{6,10},... | collective-permute-start | bytes 786440 | tf_op jit(solution)/shard_map/ppermute | solution.py:28
  28.4 25.2 %collective-permute-start.9 = (bf16[4,128,256]{2,1,0:T(8,128)(2,1)S(1)}, bf16[4,128,256]{2,1,0:T(8,128)(2,1)S(1)}, u32[]{:S(2)}, u32[]{:S(2)}) collective-permute-start(bf16[4,128,256]{2,1,0:T(8,128)(2,1)S(1)} %get-tuple-element.38), channel_id=1, source_target_pairs={{0,4},{4,0},{1,5},{5,1},{2,6},{6,2},{3,7},{7,3},{8,12},{12,8},{9,1... | collective-permute-start | bytes 786440 | tf_op jit(solution)/shard_map/ppermute | solution.py:27
  40.7 12.9 %collective-permute-start.8 = (bf16[4,128,256]{2,1,0:T(8,128)(2,1)S(1)}, bf16[4,128,256]{2,1,0:T(8,128)(2,1)S(1)}, u32[]{:S(2)}, u32[]{:S(2)}) collective-permute-start(bf16[4,128,256]{2,1,0:T(8,128)(2,1)S(1)} %get-tuple-element.37.refs_2_), channel_id=1, source_target_pairs={{0,8},{8,0},{1,9},{9,1},{2,10},{10,2},{3,11},{11,3},{4,12},{12,4},... | collective-permute-start | bytes 786440 | tf_op jit(solution)/shard_map/ppermute | solution.py:27
  42.1 11.5 %collective-permute-start.7 = (bf16[1,1024,128]{2,1,0:T(8,128)(2,1)S(1)}, bf16[1,1024,128]{2,1,0:T(8,128)(2,1)S(1)}, u32[]{:S(2)}, u32[]{:S(2)}) collective-permute-start(bf16[1,1024,128]{2,1,0:T(8,128)(2,1)S(1)} %get-tuple-element.36), channel_id=1, source_target_pairs={{0,2},{2,0},{1,3},{3,1},{4,6},{6,4},{5,7},{7,5},{8,10},{10,8},{9,1... | collective-permute-start | bytes 786440 | tf_op jit(solution)/shard_map/ppermute | solution.py:27
  53.8 4.5 %collective-permute-start.11 = (bf16[8,1024,128]{2,1,0:T(8,128)(2,1)S(1)}, bf16[8,1024,128]{2,1,0:T(8,128)(2,1)S(1)}, u32[]{:S(2)}, u32[]{:S(2)}) collective-permute-start(bf16[8,1024,128]{2,1,0:T(8,128)(2,1)S(1)} %shard_map.50.refs_0_), channel_id=1, source_target_pairs={{0,1},{1,0},{2,3},{3,2},{4,5},{5,4},{6,7},{7,6},{8,9},{9,8},{10,11... | collective-permute-start | bytes 6291464 | tf_op jit(solution)/shard_map/ppermute | solution.py:33
  53.8 13.9 %collective-permute-start.12 = (bf16[4,128,256]{2,1,0:T(8,128)(2,1)S(1)}, bf16[4,128,256]{2,1,0:T(8,128)(2,1)S(1)}, u32[]{:S(2)}, u32[]{:S(2)}) collective-permute-start(bf16[4,128,256]{2,1,0:T(8,128)(2,1)S(1)} %get-tuple-element.40), channel_id=1, source_target_pairs={{0,4},{4,0},{1,5},{5,1},{2,6},{6,2},{3,7},{7,3},{8,12},{12,8},{9,1... | collective-permute-start | bytes 786440 | tf_op jit(solution)/shard_map/ppermute | solution.py:27
  53.9 21.4 %collective-permute-start.13 = (bf16[4,128,256]{2,1,0:T(8,128)(2,1)S(1)}, bf16[4,128,256]{2,1,0:T(8,128)(2,1)S(1)}, u32[]{:S(2)}, u32[]{:S(2)}) collective-permute-start(bf16[4,128,256]{2,1,0:T(8,128)(2,1)S(1)} %get-tuple-element.39.refs_2_), channel_id=1, source_target_pairs={{0,8},{8,0},{1,9},{9,1},{2,10},{10,2},{3,11},{11,3},{4,12},{12,4},... | collective-permute-start | bytes 786440 | tf_op jit(solution)/shard_map/ppermute | solution.py:27
  56.8 18.5 %collective-permute-start.14 = (bf16[4,128,256]{2,1,0:T(8,128)(2,1)S(1)}, bf16[4,128,256]{2,1,0:T(8,128)(2,1)S(1)}, u32[]{:S(2)}, u32[]{:S(2)}) collective-permute-start(bf16[4,128,256]{2,1,0:T(8,128)(2,1)S(1)} %get-tuple-element.40), channel_id=1, source_target_pairs={{0,12},{4,8},{8,4},{12,0},{1,13},{5,9},{9,5},{13,1},{2,14},{6,10},... | collective-permute-start | bytes 786440 | tf_op jit(solution)/shard_map/ppermute | solution.py:28
  60.9 30.7 %collective-permute-start.20 = (s16[4,256,256]{2,1,0:T(8,128)(2,1)S(1)}, s16[4,256,256]{2,1,0:T(8,128)(2,1)S(1)}, u32[]{:S(2)}, u32[]{:S(2)}) collective-permute-start(s16[4,256,256]{2,1,0:T(8,128)(2,1)S(1)} %shard_map.53.refs_0_), channel_id=1, source_target_pairs={{0,16},{16,0},{1,17},{17,1},{2,18},{18,2},{3,19},{19,3},{4,20},{20... | collective-permute-start | bytes 1572872 | tf_op jit(solution)/shard_map/ppermute | solution.py:33
  77.9 20.6 %copy-start = (f32[1,1,256,2048]{3,2,1,0:T(8,128)S(1)}, f32[1,1,256,2048]{3,2,1,0:T(8,128)}, u32[]{:S(2)}) copy-start(f32[1,1,256,2048]{3,2,1,0:T(8,128)} %param.7) | copy-start | bytes 6291460
  77.9 7.8 %collective-permute-start.15 = (s16[256,256]{1,0:T(8,128)(2,1)S(1)}, s16[256,256]{1,0:T(8,128)(2,1)S(1)}, u32[]{:S(2)}, u32[]{:S(2)}) collective-permute-start(s16[256,256]{1,0:T(8,128)(2,1)S(1)} %get-tuple-element.42), channel_id=1, source_target_pairs={{0,2},{2,0},{1,3},{3,1},{4,6},{6,4},{5,7},{7,5},{8,10},{10,8},{9,1... | collective-permute-start | bytes 393224 | tf_op jit(solution)/shard_map/ppermute | solution.py:27
  79.5 10.0 %collective-permute-start.16 = (s16[256,256]{1,0:T(8,128)(2,1)S(1)}, s16[256,256]{1,0:T(8,128)(2,1)S(1)}, u32[]{:S(2)}, u32[]{:S(2)}) collective-permute-start(s16[256,256]{1,0:T(8,128)(2,1)S(1)} %get-tuple-element.43), channel_id=1, source_target_pairs={{0,4},{4,0},{1,5},{5,1},{2,6},{6,2},{3,7},{7,3},{8,12},{12,8},{9,1... | collective-permute-start | bytes 393224 | tf_op jit(solution)/shard_map/ppermute | solution.py:27
  85.1 5.9 %collective-permute-start.17 = (s16[256,256]{1,0:T(8,128)(2,1)S(1)}, s16[256,256]{1,0:T(8,128)(2,1)S(1)}, u32[]{:S(2)}, u32[]{:S(2)}) collective-permute-start(s16[256,256]{1,0:T(8,128)(2,1)S(1)} %get-tuple-element.44), channel_id=1, source_target_pairs={{0,6},{2,4},{4,2},{6,0},{1,7},{3,5},{5,3},{7,1},{8,14},{10,12},{12... | collective-permute-start | bytes 393224 | tf_op jit(solution)/shard_map/ppermute | solution.py:28
  85.1 5.9 %collective-permute-start.18 = (s16[256,256]{1,0:T(8,128)(2,1)S(1)}, s16[256,256]{1,0:T(8,128)(2,1)S(1)}, u32[]{:S(2)}, u32[]{:S(2)}) collective-permute-start(s16[256,256]{1,0:T(8,128)(2,1)S(1)} %get-tuple-element.41.refs_2_), channel_id=1, source_target_pairs={{0,16},{16,0},{1,17},{17,1},{2,18},{18,2},{3,19},{19,3},{4,20},{20... | collective-permute-start | bytes 393224 | tf_op jit(solution)/shard_map/ppermute | solution.py:33
  91.0 9.3 %collective-permute-start.19 = (s16[3,256,256]{2,1,0:T(8,128)(2,1)S(1)}, s16[3,256,256]{2,1,0:T(8,128)(2,1)S(1)}, u32[]{:S(2)}, u32[]{:S(2)}) collective-permute-start(s16[3,256,256]{2,1,0:T(8,128)(2,1)S(1)} %shard_map.52.refs_3_), channel_id=1, source_target_pairs={{0,16},{16,0},{1,17},{17,1},{2,18},{18,2},{3,19},{19,3},{4,20},{20... | collective-permute-start | bytes 1179656 | tf_op jit(solution)/shard_map/ppermute | solution.py:33
  92.0 6.4 %collective-permute-start.21 = (s16[1,256,256]{2,1,0:T(8,128)(2,1)S(1)}, s16[1,256,256]{2,1,0:T(8,128)(2,1)S(1)}, u32[]{:S(2)}, u32[]{:S(2)}) collective-permute-start(s16[1,256,256]{2,1,0:T(8,128)(2,1)S(1)} %get-tuple-element.46), channel_id=1, source_target_pairs={{0,2},{2,0},{1,3},{3,1},{4,6},{6,4},{5,7},{7,5},{8,10},{10,8},{9,1... | collective-permute-start | bytes 393224 | tf_op jit(solution)/shard_map/ppermute | solution.py:27
  93.4 7.5 %collective-permute-start.22 = (s16[1,256,256]{2,1,0:T(8,128)(2,1)S(1)}, s16[1,256,256]{2,1,0:T(8,128)(2,1)S(1)}, u32[]{:S(2)}, u32[]{:S(2)}) collective-permute-start(s16[1,256,256]{2,1,0:T(8,128)(2,1)S(1)} %get-tuple-element.47), channel_id=1, source_target_pairs={{0,4},{4,0},{1,5},{5,1},{2,6},{6,2},{3,7},{7,3},{8,12},{12,8},{9,1... | collective-permute-start | bytes 393224 | tf_op jit(solution)/shard_map/ppermute | solution.py:27
  95.2 5.9 %collective-permute-start.23 = (s16[1,256,256]{2,1,0:T(8,128)(2,1)S(1)}, s16[1,256,256]{2,1,0:T(8,128)(2,1)S(1)}, u32[]{:S(2)}, u32[]{:S(2)}) collective-permute-start(s16[1,256,256]{2,1,0:T(8,128)(2,1)S(1)} %get-tuple-element.48), channel_id=1, source_target_pairs={{0,6},{2,4},{4,2},{6,0},{1,7},{3,5},{5,3},{7,1},{8,14},{10,12},{12... | collective-permute-start | bytes 393224 | tf_op jit(solution)/shard_map/ppermute | solution.py:28
